TPU v7x, 512 devices: a whole 4x4x16 slice. The times are simulated.
512 devices in a mesh: band: 64 (over z, y_hi, core), tslice: 8 (over x, y_lo).
Axes of the slice: x: 4, y: 4 (y_hi: 2, y_lo: 2; y = y_hi * 2 + y_lo), z: 16, core: 2. Of those that a mesh axis runs over, the one named last changes fastest.
Arguments:
- voltages: bfloat16 [2048, 131072], P('band', 'tslice'), may hold values from -6 to 6
- taper: float32 [4, 2048], replicated, may hold values from -0.0625 to 0.0625
- input_of: int32 [2048], replicated, may hold values from 0 to 2047, each once
- band_start: int32 [64], replicated, may hold values from 0 to 4
Outputs:
- visibility: bfloat16 [64, 2, 2048, 2048], P('band', None, 'tslice')
Inputs may be any that keep to these rules, and one draw needn't show every extreme that they name: `input_of`: every signal has its own input. `band_start`: a band's 12 correlated channels lie within its own 16 channels.
All inputs are finite; a program needn't handle non-finite values.
Results may differ from a plain program's by a relative error of at most 0.0069.
Values may be sent and summed in bfloat16 or wider, within the bound.
No kernel may reach another device: no remote copies, remote signals or barrier semaphores. Data moves between devices by JAX's collectives and lax.ppermute only.
A program may use at most 128 MiB of HBM per device.

v0:
```python
import jax
import jax.numpy as jnp
from jax import lax
from jax.sharding import PartitionSpec as P

CHANNELS = 1024
TAPS = 4
CORR = 12


def passed_along(value, axis, steps):
    count = lax.axis_size(axis)
    leading, last = (max(0, -steps), min(count, count - steps))
    return lax.ppermute(value, axis, [(source, source + steps) for source in range(leading, last)])


def make_basis(channel_ids, length):
    index = jnp.arange(length, dtype=jnp.int32)
    m = channel_ids[:, None] * index[None, :] % length
    phases = 2.0 * jnp.pi / length * m.astype(jnp.float32)
    stacked = jnp.stack([jnp.cos(phases), -jnp.sin(phases)], axis=1)
    return stacked.reshape(2 * channel_ids.shape[0], length).astype(jnp.bfloat16)


def on_device(voltages, taper, input_of, band_start):
    length = 2 * CHANNELS
    band_count = lax.axis_size("band")
    slices = lax.axis_size("tslice")
    sig_dev = voltages.shape[0]
    frame_count = voltages.shape[1] // length
    signals = input_of.shape[0]
    row_count = signals // slices
    ch_band = CHANNELS // band_count
    position = lax.axis_index("tslice")
    tail_part = voltages[:, (frame_count - TAPS + 1) * length :]
    before = passed_along(tail_part, "tslice", 1)
    extended = jnp.concatenate([before, voltages], axis=1).astype(jnp.float32)
    extended = extended.reshape(sig_dev, frame_count + TAPS - 1, length)
    filtered = taper[0][None, None, :] * extended[:, 0:frame_count, :]
    for tap_index in range(1, TAPS):
        filtered = (
            filtered
            + taper[tap_index][None, None, :] * extended[:, tap_index : tap_index + frame_count, :]
        )
    filtered = (
        jnp.transpose(filtered, (1, 0, 2))
        .astype(jnp.bfloat16)
        .reshape(frame_count * sig_dev, length)
    )
    picked = (jnp.arange(band_count, dtype=jnp.int32) * ch_band + band_start)[:, None] + jnp.arange(
        CORR, dtype=jnp.int32
    )[None, :]
    picked = picked.reshape(band_count * CORR)
    contract = (((1,), (1,)), ((), ()))
    dft_basis = make_basis(jnp.arange(CHANNELS, dtype=jnp.int32), length)
    spectra_all = lax.dot_general(
        dft_basis, filtered, contract, preferred_element_type=jnp.float32
    ).astype(jnp.bfloat16)
    spectra = jnp.take(spectra_all.reshape(CHANNELS, 2 * frame_count * sig_dev), picked, axis=0)
    spectra = spectra.reshape(band_count, CORR, 2, frame_count, sig_dev)
    turned = lax.all_to_all(spectra, "band", split_axis=0, concat_axis=4, tiled=True)[0]
    ordered = jnp.take(turned, input_of, axis=3)
    block_data = lax.all_gather(ordered, "tslice", axis=2, tiled=True)
    left_rows = lax.dynamic_slice_in_dim(block_data, position * row_count, row_count, 3)
    swapped = jnp.concatenate([left_rows[:, 1:2], -left_rows[:, 0:1]], axis=1)
    left_both = jnp.stack([left_rows, swapped], axis=0)
    summed = jnp.einsum(
        "ocjfs,cjft->ost", left_both, block_data, preferred_element_type=jnp.float32
    )
    norm_scale = 1.0 / (CORR * frame_count * slices)
    visible = (summed * norm_scale).astype(jnp.bfloat16)
    return visible[None]


def solution(mesh):
    return jax.shard_map(
        on_device,
        mesh=mesh,
        in_specs=(P("band", "tslice"), P(), P(), P()),
        out_specs=P("band", None, "tslice", None),
        check_vma=False,
    )
```

profile of v0, /device:TPU:26, one launch (start us, length us, event | category | flops | bytes accessed | tf_op | source)
XLA Modules:
  0.0 366.9 jit_solution(14094511861070047739)
XLA Ops:
  6.5 1.0 slice.34
  7.6 3.6 collective-permute-start
  11.2 34.4 %negate_convert_fusion = (bf16[1024,1,2048]{2,0,1:T(8,128)(2,1)S(1)}, bf16[1024,1,2048]{2,0,1:T(8,128)(2,1)}) fusion(), kind=kLoop, calls=%fused_computation.9 | loop fusion | flops 35651584 | bytes 8388608 | tf_op jit(solution)/shard_map/convert.2
  45.6 0.1 iota_add_fusion
  45.6 0.1 compare_and_fusion
  45.7 6.2 %pad_maximum_fusion = bf16[1024,2,2048]{2,0,1:T(8,128)(2,1)} fusion(bf16[1024,1,2048]{2,0,1:T(8,128)(2,1)S(1)} %get-tuple-element.11, bf16[1024,1,2048]{2,0,1:T(8,128)(2,1)} %get-tuple-element.12), kind=kLoop, calls=%fused_computation.8 | loop fusion | flops 4194304 | bytes 16777216 | tf_op jit(solution)/shard_map/stack | solution.py:21
  51.9 16.4 %copy.14 = bf16[1024,2,2048]{2,1,0:T(2,128)(2,1)} copy(bf16[1024,2,2048]{2,0,1:T(8,128)(2,1)} %pad_maximum_fusion) | data formatting | bytes 16777216 | tf_op jit(solution)/shard_map/stack | solution.py:21
  68.3 13.1 %convert_element_type.46 = bf16[2048,2048]{1,0:T(8,128)(2,1)} reshape(bf16[1024,2,2048]{2,1,0:T(2,128)(2,1)} %copy.14) | data formatting | bytes 16777216 | tf_op jit(solution)/shard_map/convert_element_type | solution.py:22
  81.4 0.1 add.103
  81.6 1.4 maximum_convert_fusion
  83.0 2.4 reshape.144
  85.4 7.0 %fusion.21 = bf16[8,32,2048]{2,0,1:T(8,128)(2,1)S(1)} fusion(f32[32,11,2048]{2,1,0:T(8,128)} %reshape.144, f32[2048]{0:T(1024)S(1)} %bitcast.47, f32[2048]{0:T(1024)S(1)} %bitcast.48, f32[2048]{0:T(1024)S(1)} %bitcast.46, f32[2048]{0:T(1024)S(1)} %bitcast.45), kind=kLoop, calls=%fused_computation.33 | loop fusion | flops 4194304 | bytes 9469952 | tf_op jit(solution)/shard_map/convert_element_type | solution.py:47
  92.4 0.6 copy.15
  93.0 5.8 %convolution_convert_fusion = bf16[2048,256]{1,0:T(8,128)(2,1)S(1)} fusion(bf16[2048,2048]{1,0:T(8,128)(2,1)} %convert_element_type.46, bf16[256,2048]{1,0:T(8,128)(2,1)S(1)} %bitcast.44), kind=kOutput, calls=%fused_computation.20 | convolution fusion | flops 2148007936 | bytes 10485760 | tf_op jit(solution)/shard_map/dot_general | solution.py:56
  98.8 0.4 reshape.143
  99.2 3.3 gather_fusion
  102.5 3.4 gather.11
  106.0 2.6 broadcast_select_fusion
  108.6 5.8 %reshape.165 = bf16[64,2,3072]{2,1,0:T(2,128)(2,1)} reshape(bf16[64,12,2,8,32]{4,3,2,1,0:T(8,128)(2,1)} %broadcast_select_fusion) | data formatting | bytes 1572864
  114.5 18.8 %all-to-all-start = ((bf16[64,2,3072]{2,1,0:T(2,128)(2,1)}), bf16[64,2,3072]{2,1,0:T(2,128)(2,1)}, u32[]{:S(2)}, u32[]{:S(2)}) async-start(bf16[64,2,3072]{2,1,0:T(2,128)(2,1)} %reshape.165), calls=%async_computation | async-start | bytes 1572864 | tf_op jit(solution)/shard_map/all_to_all | solution.py:61
  133.2 0.0 all-gather.2.cloned.1.call-start
  133.3 44.7 %all-to-all-done = bf16[64,2,3072]{2,1,0:T(2,128)(2,1)} async-done(((bf16[64,2,3072]{2,1,0:T(2,128)(2,1)}), bf16[64,2,3072]{2,1,0:T(2,128)(2,1)}, u32[]{:S(2)}, u32[]{:S(2)}) %all-to-all-start) | async-done | bytes 786464 | tf_op jit(solution)/shard_map/all_to_all | solution.py:61
  178.0 4.0 %reshape.166 = bf16[64,12,2,8,32]{4,3,2,1,0:T(8,128)(2,1)S(1)} reshape(bf16[64,2,3072]{2,1,0:T(2,128)(2,1)} %all-to-all-done) | data formatting | bytes 1572864
  182.1 8.7 %copy.22 = bf16[1,12,2,8,64,32]{1,3,5,4,2,0:T(8,128)(2,1)} copy(bf16[1,12,2,8,64,32]{5,3,2,1,4,0:T(8,128)(2,1)S(1)} %bitcast.42) | data formatting | bytes 1572864 | tf_op jit(solution)/shard_map/squeeze | solution.py:61
  190.7 19.9 %gather_fusion.1 = bf16[2048,12,2,8]{1,3,2,0:T(8,128)(2,1)} fusion(bf16[12,2,8,2048]{0,2,3,1:T(8,128)(2,1)} %bitcast.43, s32[2048]{0:T(1024)S(1)} %fusion.22), kind=kCustom, calls=%fused_computation.1 | custom fusion | bytes 1581056 | tf_op jit(solution)/shard_map/jit(_take)/gather | solution.py:62
  210.6 9.0 %copy.18 = bf16[2048,12,2,8]{0,3,2,1:T(8,128)(2,1)S(1)} copy(bf16[2048,12,2,8]{1,3,2,0:T(8,128)(2,1)} %gather_fusion.1) | data formatting | bytes 1572864 | tf_op jit(solution)/shard_map/jit(_take)/gather | solution.py:62
  219.7 1.0 select_bitcast_fusion
  220.7 129.4 %all-gather.2.cloned.1.call-done = bf16[12,2,64,2048]{3,2,1,0:T(8,128)(2,1)} async-done(((bf16[12,2,8,2048]{3,2,1,0:T(8,128)(2,1)}), bf16[12,2,64,2048]{3,2,1,0:T(8,128)(2,1)}) %all-gather.2.cloned.1.call-update) | async-done | bytes 6291472 | tf_op jit(solution)/shard_map/all_gather | solution.py:63
  350.0 1.2 constant_dynamic-slice_fusion
  351.3 0.1 maximum_bitcast_fusion
  351.4 1.2 dynamic-slice_bitcast_fusion
  352.6 7.4 %fusion.11 = bf16[1,2,256,2048]{3,2,1,0:T(8,128)(2,1)} fusion(bf16[12,2,64,2048]{3,2,1,0:T(8,128)(2,1)} %all-gather.2.cloned.1.call-done, bf16[1,12,2,64,256]{4,3,2,1,0:T(8,128)(2,1)S(1)} %maximum_bitcast_fusion, bf16[1,12,2,64,256]{4,3,2,1,0:T(8,128)(2,1)S(1)} %dynamic-slice_bitcast_fusion), kind=kOutput, calls=%fused_computation.19 | convolution fusion | flops 3224109056 | bytes 9961472 | tf_op jit(solution)/shard_map/ocjfs,cjft->ost/dot_general | solution.py:67
  (14 shorter events, 0.1 us)
Async XLA Ops:
  7.6 38.0 %copy-start.2 = (s32[64]{0:T(128)S(1)}, s32[64]{0:T(128)}, u32[]{:S(2)}) copy-start(s32[64]{0:T(128)} %param.7) | copy-start | bytes 772
  7.6 74.0 %collective-permute-start = (bf16[32,6144]{1,0:T(8,128)(2,1)S(1)}, bf16[32,6144]{1,0:T(8,128)(2,1)S(1)}, u32[]{:S(2)}, u32[]{:S(2)}) collective-permute-start(bf16[32,6144]{1,0:T(8,128)(2,1)S(1)} %slice.34), channel_id=1, source_target_pairs={{0,1},{1,2},{2,3},{3,4},{4,5},{5,6},{6,7},{8,9},{9,10},{10,11},{11... | collective-permute-start | bytes 1179656 | tf_op jit(solution)/shard_map/ppermute | solution.py:14
  68.3 13.3 %copy-start.1 = (f32[4,2048]{1,0:T(4,128)S(1)}, f32[4,2048]{1,0:T(4,128)}, u32[]{:S(2)}) copy-start(f32[4,2048]{1,0:T(4,128)} %param.5) | copy-start | bytes 98308
  108.6 24.7 %copy-start = (s32[2048]{0:T(1024)S(1)}, s32[2048]{0:T(1024)}, u32[]{:S(2)}) copy-start(s32[2048]{0:T(1024)} %param.6) | copy-start | bytes 24580
  114.5 63.6 %all-to-all-start = ((bf16[64,2,3072]{2,1,0:T(2,128)(2,1)}), bf16[64,2,3072]{2,1,0:T(2,128)(2,1)}, u32[]{:S(2)}, u32[]{:S(2)}) async-start(bf16[64,2,3072]{2,1,0:T(2,128)(2,1)} %reshape.165), calls=%async_computation | async-start | bytes 1572864 | tf_op jit(solution)/shard_map/all_to_all | solution.py:61
  133.2 216.8 %all-gather.2.cloned.1.call-start = ((), (), s32[]{:S(2)}) async-start(), calls=%async_computation.1 | async-start | bytes 7077888 | tf_op jit(solution)/shard_map/all_gather | solution.py:63
Sparse Core Ops, SparseCore 0:
  220.8 129.2 all-gather.1
where the time goes:
time: 368 us; the launch traced here: 367 us
  waiting for transfers between devices  174 us (47%)
  local copies, waits for them, and re-layouts  89.5 us (24%)
  other arithmetic  54.1 us (15%)
  starting transfers between devices  22.4 us (6%)
  between operations  13.6 us (4%)
  matrix products  13.2 us (4%)
    all_gather x1, waiting for transfers between devices, on_device(): block_data = lax.all_gather(ordered, 'tslice', axis=2, tiled=True)  129 us
    all_to_all x1, waiting for transfers between devices, on_device(): lax.all_to_all(spectra, 'band', split_axis=0, concat_axis=4, tiled=True)[0]  44.7 us
    another operation x1, other arithmetic  34.4 us
    gather x2, local copies, waits for them, and re-layouts, on_device(): ordered = jnp.take(turned, input_of, axis=3)  28.9 us
    all_to_all x1, starting transfers between devices, on_device(): lax.all_to_all(spectra, 'band', split_axis=0, concat_axis=4, tiled=True)[0]  18.8 us
    another operation x1, local copies, waits for them, and re-layouts, make_basis(): stacked = jnp.stack([jnp.cos(phases), -jnp.sin(phases)], axis=1)  16.4 us
    convert_element_type x1, local copies, waits for them, and re-layouts, make_basis(): stacked.reshape(2 * channel_ids.shape[0], length).astype(jnp.bfloat16)  13.1 us
    unnamed x8, local copies, waits for them, and re-layouts  9.89 us
  transfers between devices with their start and end apart: 3, of which 2 were waited for; matrix products, arithmetic and copies ran while one was open for 19% of the time, Pallas kernels for 0%

commit v1 on v0

v1 whole, which is shorter than its diff:
```python
import functools

import jax
import jax.numpy as jnp
import numpy as np
from jax import lax
from jax.experimental import pallas as pl
from jax.experimental.pallas import tpu as pltpu
from jax.sharding import PartitionSpec as P

CHANNELS = 1024
TAPS = 4
CORR = 12
MIB = 1 << 20
NT = (((1,), (1,)), ((), ()))


def make_basis(bands, length):
    index = np.arange(length, dtype=np.int64)
    m = (np.arange(CHANNELS, dtype=np.int64)[:, None] * index[None, :]) % length
    phases = np.float32(2.0 * np.pi / length) * m.astype(np.float32)
    stacked = np.stack([np.cos(phases), -np.sin(phases)], axis=0)
    stacked = stacked.reshape(2, bands, CHANNELS // bands, length).transpose(1, 0, 2, 3)
    return stacked.reshape(2 * CHANNELS, length).astype(jnp.bfloat16)


def spectra_kernel(group, start_ref, volt_ref, before_ref, taper_ref, basis_ref, out_ref, filt):
    sig_dev = volt_ref.shape[0]
    length = taper_ref.shape[1]
    frames = volt_ref.shape[1] // length
    ch_band = basis_ref.shape[0] // (2 * group)
    step = pl.program_id(0)

    @pl.when(step == 0)
    def _():
        def frame(at):
            if at < 0:
                return before_ref[:, (at + TAPS - 1) * length : (at + TAPS) * length]
            return volt_ref[:, at * length : (at + 1) * length]

        for at in range(frames):
            total = taper_ref[0:1, :] * frame(at - TAPS + 1).astype(jnp.float32)
            for tap in range(1, TAPS):
                total = total + taper_ref[tap : tap + 1, :] * frame(
                    at + tap - TAPS + 1
                ).astype(jnp.float32)
            filt[at * sig_dev : (at + 1) * sig_dev, :] = total.astype(jnp.bfloat16)

    products = lax.dot_general(
        basis_ref[...], filt[...], NT, preferred_element_type=jnp.float32
    ).astype(jnp.bfloat16)
    shape = (2 * CORR, products.shape[0])
    row = lax.broadcasted_iota(jnp.int32, shape, 0)
    at_first = lax.broadcasted_iota(jnp.int32, shape, 1) - row
    at_first = at_first - jnp.where(row < CORR, 0, ch_band - CORR)
    picks = [
        jnp.where(at_first == band * 2 * ch_band + start_ref[step * group + band], 1.0, 0.0)
        for band in range(group)
    ]
    picked = jnp.concatenate(picks, axis=0).astype(jnp.bfloat16)
    spectra = jnp.dot(picked, products, preferred_element_type=jnp.float32)
    for band in range(group):
        out_ref[band] = spectra[band * 2 * CORR : (band + 1) * 2 * CORR].astype(jnp.bfloat16)


def picked_spectra(voltages, before, taper, basis, band_start, bands):
    group = 8
    sig_dev, samples = voltages.shape
    length = taper.shape[1]
    columns = sig_dev * (samples // length)
    rows = 2 * CHANNELS // bands * group
    return pl.pallas_call(
        functools.partial(spectra_kernel, group),
        grid_spec=pltpu.PrefetchScalarGridSpec(
            num_scalar_prefetch=1,
            grid=(bands // group,),
            in_specs=[
                pl.BlockSpec(voltages.shape, lambda g, s: (0, 0)),
                pl.BlockSpec(before.shape, lambda g, s: (0, 0)),
                pl.BlockSpec(taper.shape, lambda g, s: (0, 0)),
                pl.BlockSpec((rows, length), lambda g, s: (g, 0)),
            ],
            out_specs=pl.BlockSpec((group, 2 * CORR, columns), lambda g, s: (g, 0, 0)),
            scratch_shapes=[
                pltpu.VMEM((columns, length), jnp.bfloat16),
            ],
        ),
        out_shape=jax.ShapeDtypeStruct((bands, 2 * CORR, columns), jnp.bfloat16),
        compiler_params=pltpu.CompilerParams(vmem_limit_bytes=40 * MIB),
        cost_estimate=pl.CostEstimate(
            flops=2 * 2 * CHANNELS * length * columns,
            bytes_accessed=2 * 2 * CHANNELS * length + 4 * sig_dev * samples,
            transcendentals=0,
        ),
    )(band_start, voltages, before, taper, basis)


def order_kernel(turned_ref, input_ref, out_ref, lined):
    bands, values, columns = turned_ref.shape
    signals = out_ref.shape[1]
    sig_dev = signals // bands
    frames = columns // sig_dev
    per_tile = 128 // sig_dev

    def tile(at, carry):
        lane = lax.broadcasted_iota(jnp.int32, (values, 128), 1) // sig_dev
        blocks = [turned_ref[at * per_tile + k].astype(jnp.float32) for k in range(per_tile)]
        for frame in range(frames):
            half, place = frame // per_tile, frame % per_tile
            merged = None
            for k in range(per_tile):
                piece = blocks[k][:, half * 128 : (half + 1) * 128]
                shift = (k - place) * sig_dev % 128
                if shift:
                    piece = pltpu.roll(piece, shift, 1)
                merged = piece if merged is None else jnp.where(lane == k, piece, merged)
            lined[at, frame * values : (frame + 1) * values, :] = merged
        return carry

    lax.fori_loop(0, bands // per_tile, tile, 0)
    wanted = input_ref[...]
    part = 256
    total = None
    for at in range(signals // part):
        held = jnp.concatenate([lined[2 * at], lined[2 * at + 1]], axis=1).astype(jnp.bfloat16)
        row = lax.broadcasted_iota(jnp.int32, (part, signals), 0) + at * part
        chosen = jnp.where(row == wanted, 1.0, 0.0).astype(jnp.bfloat16)
        product = jnp.dot(held, chosen, preferred_element_type=jnp.float32)
        total = product if total is None else total + product
    out_ref[...] = total.astype(jnp.bfloat16)


def order_signals(turned, input_of):
    bands, values, columns = turned.shape
    signals = input_of.shape[0]
    rows = values * columns * bands // signals
    return pl.pallas_call(
        order_kernel,
        in_specs=[pl.BlockSpec(memory_space=pltpu.VMEM)] * 2,
        out_specs=pl.BlockSpec(memory_space=pltpu.VMEM),
        out_shape=jax.ShapeDtypeStruct((rows, signals), jnp.bfloat16),
        scratch_shapes=[pltpu.VMEM((signals // 128, rows, 128), jnp.float32)],
        compiler_params=pltpu.CompilerParams(vmem_limit_bytes=40 * MIB),
        cost_estimate=pl.CostEstimate(
            flops=2 * rows * signals * signals,
            bytes_accessed=4 * rows * signals,
            transcendentals=0,
        ),
    )(turned, input_of.reshape(1, signals))


def correlate_kernel(scale, count, position_ref, *refs):
    own_refs, tile_refs = refs[:count], refs[count : 2 * count]
    out_ref, left = refs[2 * count], refs[2 * count + 1]
    row_count = out_ref.shape[2]
    values = 2 * CORR

    @pl.when(pl.program_id(0) == 0)
    def _():
        own = jnp.concatenate([r[...] for r in own_refs], axis=0)
        depth = own.shape[0]
        part = 384
        row = lax.broadcasted_iota(jnp.int32, (part, part), 0)
        column = lax.broadcasted_iota(jnp.int32, (part, part), 1)
        upper = row % values < CORR
        swap = jnp.where(upper & (column == row + CORR), 1.0, 0.0)
        swap = swap - jnp.where(jnp.logical_not(upper) & (column == row - CORR), 1.0, 0.0)
        swap = swap.astype(jnp.bfloat16)
        for at in range(depth // part):
            piece = own[at * part : (at + 1) * part]
            left[:row_count, at * part : (at + 1) * part] = jnp.transpose(
                piece.astype(jnp.float32)
            ).astype(jnp.bfloat16)
            turned = jnp.dot(swap, piece, preferred_element_type=jnp.float32)
            left[row_count:, at * part : (at + 1) * part] = jnp.transpose(turned).astype(
                jnp.bfloat16
            )

    right = jnp.concatenate([r[...] for r in tile_refs], axis=0)
    summed = jnp.dot(left[...], right, preferred_element_type=jnp.float32) * scale
    out_ref[0, 0] = summed[:row_count].astype(jnp.bfloat16)
    out_ref[0, 1] = summed[row_count:].astype(jnp.bfloat16)


def correlate(position, blocks, row_count, scale):
    signals = blocks[0].shape[1]
    depth = sum(b.shape[0] for b in blocks)
    tile = 512
    count = len(blocks)
    own_specs = [pl.BlockSpec((b.shape[0], row_count), lambda g, p: (0, p[0])) for b in blocks]
    tile_specs = [pl.BlockSpec((b.shape[0], tile), lambda g, p: (0, g)) for b in blocks]
    return pl.pallas_call(
        functools.partial(correlate_kernel, scale, count),
        grid_spec=pltpu.PrefetchScalarGridSpec(
            num_scalar_prefetch=1,
            grid=(signals // tile,),
            in_specs=own_specs + tile_specs,
            out_specs=pl.BlockSpec((1, 2, row_count, tile), lambda g, p: (0, 0, 0, g)),
            scratch_shapes=[pltpu.VMEM((2 * row_count, depth), jnp.bfloat16)],
        ),
        out_shape=jax.ShapeDtypeStruct((1, 2, row_count, signals), jnp.bfloat16),
        compiler_params=pltpu.CompilerParams(vmem_limit_bytes=40 * MIB),
        cost_estimate=pl.CostEstimate(
            flops=4 * row_count * signals * depth,
            bytes_accessed=2 * signals * depth + 4 * row_count * signals,
            transcendentals=0,
        ),
    )(position, *blocks, *blocks)


def from_slice(value, dx, dy, slices):
    along = slices // 2
    pairs = []
    for target in range(slices):
        source = ((target // 2 + dx) % along) * 2 + (target % 2 + dy) % 2
        pairs.append((source, target))
    return lax.ppermute(value, "tslice", pairs)


def gather_slices(own, slices):
    take = functools.partial(from_slice, slices=slices)
    right = take(own, 1, 0)
    other = take(own, 0, 1)
    left = take(own, -1, 0)
    right_other = take(right, 0, 1)
    left_other = take(other, -1, 0)
    far = take(right, 1, 0)
    third = own.shape[0] // 3
    far_other = [
        take(right_other[:third], 1, 0),
        take(left_other[third : 2 * third], -1, 0),
        take(far[2 * third :], 0, 1),
    ]
    return [own, right, other, left, right_other, left_other, far] + far_other


def on_device(voltages, taper, input_of, band_start):
    length = 2 * CHANNELS
    bands = lax.axis_size("band")
    slices = lax.axis_size("tslice")
    frames = voltages.shape[1] // length
    signals = input_of.shape[0]
    position = lax.axis_index("tslice")
    tail = voltages[:, (frames - TAPS + 1) * length :]
    before = lax.ppermute(tail, "tslice", [(s, s + 1) for s in range(slices - 1)])
    basis = jnp.asarray(make_basis(bands, length))
    spectra = picked_spectra(voltages, before, taper, basis, band_start, bands)
    turned = lax.all_to_all(spectra, "band", split_axis=0, concat_axis=0, tiled=True)
    own = order_signals(turned, input_of)
    blocks = gather_slices(own, slices)
    scale = 1.0 / (CORR * frames * slices)
    return correlate(
        position.astype(jnp.int32).reshape(1), blocks, signals // slices, scale
    )


def solution(mesh):
    return jax.shard_map(
        on_device,
        mesh=mesh,
        in_specs=(P("band", "tslice"), P(), P(), P()),
        out_specs=P("band", None, "tslice", None),
        check_vma=False,
    )
```

time: 368 us -> 169 us (0.46)
  the two profiles are of different devices: /device:TPU:26 before, /device:TPU:32 now
where the time goes in v1:
time: 169 us; the launch traced here: 168 us
  blocking collectives  61.7 us (37%)
  waiting for transfers between devices  40.6 us (24%)
  starting transfers between devices  35.8 us (21%)
  Pallas kernels  17.6 us (10%)
  local copies, waits for them, and re-layouts  12.5 us (7%)
    all_to_all x1, blocking collectives, on_device(): lax.all_to_all(spectra, 'band', split_axis=0, concat_axis=0, tiled=True)  61.7 us
    ppermute x9, waiting for transfers between devices, from_slice(): return lax.ppermute(value, 'tslice', pairs)  32.3 us
    ppermute x9, starting transfers between devices, from_slice(): return lax.ppermute(value, 'tslice', pairs)  32.3 us
    unnamed x18, local copies, waits for them, and re-layouts  9.23 us
    ppermute x1, waiting for transfers between devices, on_device(): lax.ppermute(tail, 'tslice', [(s, s + 1) for s in range(slices - 1)])  8.33 us
    pallas_call x1, Pallas kernels, correlate(): pl.pallas_call(functools.partial(correlate_kernel, scale, count), grid_sp...  7.12 us
    pallas_call x1, Pallas kernels, picked_spectra(): pl.pallas_call(functools.partial(spectra_kernel, group), grid_spec=pltpu....  6.95 us
    pallas_call x1, Pallas kernels, order_signals(): pl.pallas_call(order_kernel, in_specs=[pl.BlockSpec(memory_space=pltpu.VM...  3.56 us
  transfers between devices with their start and end apart: 10, of which 5 were waited for; matrix products, arithmetic and copies ran while one was open for 1% of the time, Pallas kernels for 0%

profile of v1, /device:TPU:32, one launch (start us, length us, event | category | flops | bytes accessed | tf_op | source)
XLA Modules:
  0.0 168.3 jit_solution(9591087213069543800)
XLA Ops:
  0.0 1.0 slice.12
  1.0 3.5 %collective-permute-start = (bf16[32,6144]{1,0:T(8,128)(2,1)S(1)}, bf16[32,6144]{1,0:T(8,128)(2,1)S(1)}, u32[]{:S(2)}, u32[]{:S(2)}) collective-permute-start(bf16[32,6144]{1,0:T(8,128)(2,1)S(1)} %slice.12), channel_id=1, source_target_pairs={{0,1},{1,2},{2,3},{3,4},{4,5},{5,6},{6,7},{8,9},{9,10},{10,11},{11... | collective-permute-start | bytes 1179656 | tf_op jit(solution)/shard_map/ppermute | solution.py:245
  4.6 8.3 %collective-permute-done.before_ref = bf16[32,6144]{1,0:T(8,128)(2,1)S(1)} collective-permute-done((bf16[32,6144]{1,0:T(8,128)(2,1)S(1)}, bf16[32,6144]{1,0:T(8,128)(2,1)S(1)}, u32[]{:S(2)}, u32[]{:S(2)}) %collective-permute-start) | collective-permute-done | bytes 393248 | tf_op jit(solution)/shard_map/ppermute | solution.py:245
  12.9 3.4 %copy-done = bf16[2048,2048]{1,0:T(8,128)(2,1)S(1)} copy-done((bf16[2048,2048]{1,0:T(8,128)(2,1)S(1)}, bf16[2048,2048]{1,0:T(8,128)(2,1)}, u32[]{:S(2)}) %copy-start) | copy-done | bytes 8388632
  16.3 1.2 copy-done.5
  17.6 0.8 copy-done.6
  18.3 0.7 copy-done.7
  19.0 6.9 %shard_map.55 = bf16[64,24,256]{2,1,0:T(8,128)(2,1)S(1)} custom-call(s32[64]{0:T(128)S(1)} %copy-done.7, bf16[32,16384]{1,0:T(8,128)(2,1)S(1)} %copy-done.5, bf16[32,6144]{1,0:T(8,128)(2,1)S(1)} %collective-permute-done.before_ref, f32[4,2048]{1,0:T(4,128)S(1)} %copy-done.6, bf16[2048,2048]{1,0:T(8,128)(2,1)S(1)} %copy-done), custom_call_target="tpu_custom_call" | custom-call | flops 2147483648 | bytes 10485760 | tf_op jit(solution)/shard_map/pallas_call | solution.py:72
  25.9 61.7 %all_to_all.5.turned_ref = bf16[64,24,256]{2,1,0:T(8,128)(2,1)S(1)} all-to-all(bf16[64,24,256]{2,1,0:T(8,128)(2,1)S(1)} %shard_map.55), channel_id=1, replica_groups=mesh['band'=64,'tslice'=8] {'band'}, dimensions={0} | all-to-all | bytes 1572864 | tf_op jit(solution)/shard_map/all_to_all | solution.py:248
  87.6 3.6 %shard_map.56.refs_0_.refs_10_ = bf16[192,2048]{1,0:T(8,128)(2,1)S(1)} custom-call(bf16[64,24,256]{2,1,0:T(8,128)(2,1)S(1)} %all_to_all.5.turned_ref, s32[1,2048]{1,0:T(1,128)S(1)} %bitcast.2), custom_call_target="tpu_custom_call" | custom-call | flops 1610612736 | bytes 1572864 | tf_op jit(solution)/shard_map/pallas_call | solution.py:137
  91.1 3.8 %collective-permute-start.2 = (bf16[192,2048]{1,0:T(8,128)(2,1)S(1)}, bf16[192,2048]{1,0:T(8,128)(2,1)S(1)}, u32[]{:S(2)}, u32[]{:S(2)}) collective-permute-start(bf16[192,2048]{1,0:T(8,128)(2,1)S(1)} %shard_map.56.refs_0_.refs_10_), channel_id=1, source_target_pairs={{1,0},{0,1},{3,2},{2,3},{5,4},{4,5},{7,6},{6,7},{9,8},{8,9},{11,10... | collective-permute-start | bytes 2359304 | tf_op jit(solution)/shard_map/ppermute | solution.py:217
  94.9 4.9 %collective-permute-start.1 = (bf16[192,2048]{1,0:T(8,128)(2,1)S(1)}, bf16[192,2048]{1,0:T(8,128)(2,1)S(1)}, u32[]{:S(2)}, u32[]{:S(2)}) collective-permute-start(bf16[192,2048]{1,0:T(8,128)(2,1)S(1)} %shard_map.56.refs_0_.refs_10_), channel_id=1, source_target_pairs={{2,0},{3,1},{4,2},{5,3},{6,4},{7,5},{0,6},{1,7},{10,8},{11,9},{12,... | collective-permute-start | bytes 2359304 | tf_op jit(solution)/shard_map/ppermute | solution.py:217
  99.8 12.9 %collective-permute-done.2.refs_2_.refs_12_ = bf16[192,2048]{1,0:T(8,128)(2,1)S(1)} collective-permute-done((bf16[192,2048]{1,0:T(8,128)(2,1)S(1)}, bf16[192,2048]{1,0:T(8,128)(2,1)S(1)}, u32[]{:S(2)}, u32[]{:S(2)}) %collective-permute-start.2) | collective-permute-done | bytes 786464 | tf_op jit(solution)/shard_map/ppermute | solution.py:217
  112.8 5.3 %collective-permute-start.5 = (bf16[192,2048]{1,0:T(8,128)(2,1)S(1)}, bf16[192,2048]{1,0:T(8,128)(2,1)S(1)}, u32[]{:S(2)}, u32[]{:S(2)}) collective-permute-start(bf16[192,2048]{1,0:T(8,128)(2,1)S(1)} %collective-permute-done.2.refs_2_.refs_12_), channel_id=1, source_target_pairs={{6,0},{7,1},{0,2},{1,3},{2,4},{3,5},{4,6},{5,7},{14,8},{15,9},{8,1... | collective-permute-start | bytes 2359304 | tf_op jit(solution)/shard_map/ppermute | solution.py:217
  118.1 0.9 copy-done.1
  119.0 0.0 collective-permute-done.1.refs_1_.refs_11_
  119.0 3.5 %collective-permute-start.6 = (bf16[192,2048]{1,0:T(8,128)(2,1)S(1)}, bf16[192,2048]{1,0:T(8,128)(2,1)S(1)}, u32[]{:S(2)}, u32[]{:S(2)}) collective-permute-start(bf16[192,2048]{1,0:T(8,128)(2,1)S(1)} %collective-permute-done.1.refs_1_.refs_11_), channel_id=1, source_target_pairs={{2,0},{3,1},{4,2},{5,3},{6,4},{7,5},{0,6},{1,7},{10,8},{11,9},{12,... | collective-permute-start | bytes 2359304 | tf_op jit(solution)/shard_map/ppermute | solution.py:217
  122.5 3.6 %collective-permute-start.4 = (bf16[192,2048]{1,0:T(8,128)(2,1)S(1)}, bf16[192,2048]{1,0:T(8,128)(2,1)S(1)}, u32[]{:S(2)}, u32[]{:S(2)}) collective-permute-start(bf16[192,2048]{1,0:T(8,128)(2,1)S(1)} %collective-permute-done.1.refs_1_.refs_11_), channel_id=1, source_target_pairs={{1,0},{0,1},{3,2},{2,3},{5,4},{4,5},{7,6},{6,7},{9,8},{8,9},{11,10... | collective-permute-start | bytes 2359304 | tf_op jit(solution)/shard_map/ppermute | solution.py:217
  126.2 1.9 %collective-permute-start.3 = (bf16[192,2048]{1,0:T(8,128)(2,1)S(1)}, bf16[192,2048]{1,0:T(8,128)(2,1)}, u32[]{:S(2)}, u32[]{:S(2)}) collective-permute-start(bf16[192,2048]{1,0:T(8,128)(2,1)S(1)} %shard_map.56.refs_0_.refs_10_), channel_id=1, source_target_pairs={{6,0},{7,1},{0,2},{1,3},{2,4},{3,5},{4,6},{5,7},{14,8},{15,9},{8,1... | collective-permute-start | bytes 2359304 | tf_op jit(solution)/shard_map/ppermute | solution.py:217
  128.1 9.7 %collective-permute-done.5.refs_5_.refs_15_ = bf16[192,2048]{1,0:T(8,128)(2,1)S(1)} collective-permute-done((bf16[192,2048]{1,0:T(8,128)(2,1)S(1)}, bf16[192,2048]{1,0:T(8,128)(2,1)S(1)}, u32[]{:S(2)}, u32[]{:S(2)}) %collective-permute-start.5) | collective-permute-done | bytes 786464 | tf_op jit(solution)/shard_map/ppermute | solution.py:217
  137.8 0.7 slice.17
  138.6 2.7 %collective-permute-start.8 = (bf16[64,2048]{1,0:T(8,128)(2,1)}, bf16[64,2048]{1,0:T(8,128)(2,1)S(1)}, u32[]{:S(2)}, u32[]{:S(2)}) collective-permute-start(bf16[64,2048]{1,0:T(8,128)(2,1)} %slice.17), channel_id=1, source_target_pairs={{6,0},{7,1},{0,2},{1,3},{2,4},{3,5},{4,6},{5,7},{14,8},{15,9},{8,1... | collective-permute-start | bytes 786440 | tf_op jit(solution)/shard_map/ppermute | solution.py:217
  141.2 0.7 slice.18
  142.0 2.2 %collective-permute-start.9 = (bf16[64,2048]{1,0:T(8,128)(2,1)}, bf16[64,2048]{1,0:T(8,128)(2,1)}, u32[]{:S(2)}, u32[]{:S(2)}) collective-permute-start(bf16[64,2048]{1,0:T(8,128)(2,1)} %slice.18), channel_id=1, source_target_pairs={{1,0},{0,1},{3,2},{2,3},{5,4},{4,5},{7,6},{6,7},{9,8},{8,9},{11,10... | collective-permute-start | bytes 786440 | tf_op jit(solution)/shard_map/ppermute | solution.py:217
  144.2 0.7 slice.16
  144.9 4.3 %collective-permute-start.7 = (bf16[64,2048]{1,0:T(8,128)(2,1)}, bf16[64,2048]{1,0:T(8,128)(2,1)}, u32[]{:S(2)}, u32[]{:S(2)}) collective-permute-start(bf16[64,2048]{1,0:T(8,128)(2,1)} %slice.16), channel_id=1, source_target_pairs={{2,0},{3,1},{4,2},{5,3},{6,4},{7,5},{0,6},{1,7},{10,8},{11,9},{12,... | collective-permute-start | bytes 786440 | tf_op jit(solution)/shard_map/ppermute | solution.py:217
  149.3 5.5 %collective-permute-done.3.refs_3_.refs_13_ = bf16[192,2048]{1,0:T(8,128)(2,1)} collective-permute-done((bf16[192,2048]{1,0:T(8,128)(2,1)S(1)}, bf16[192,2048]{1,0:T(8,128)(2,1)}, u32[]{:S(2)}, u32[]{:S(2)}) %collective-permute-start.3) | collective-permute-done | bytes 786464 | tf_op jit(solution)/shard_map/ppermute | solution.py:217
  154.8 4.1 %collective-permute-done.8.refs_8_.refs_18_ = bf16[64,2048]{1,0:T(8,128)(2,1)S(1)} collective-permute-done((bf16[64,2048]{1,0:T(8,128)(2,1)}, bf16[64,2048]{1,0:T(8,128)(2,1)S(1)}, u32[]{:S(2)}, u32[]{:S(2)}) %collective-permute-start.8) | collective-permute-done | bytes 262176 | tf_op jit(solution)/shard_map/ppermute | solution.py:217
  158.9 0.0 collective-permute-done.9.refs_9_.refs_19_
  158.9 1.1 copy-done.2
  160.0 1.1 copy-done.4
  161.2 7.1 %shard_map.57 = bf16[1,2,256,2048]{3,2,1,0:T(8,128)(2,1)} custom-call(s32[1]{0:T(128)} %bitcast.position_ref, bf16[192,2048]{1,0:T(8,128)(2,1)S(1)} %shard_map.56.refs_0_.refs_10_, bf16[192,2048]{1,0:T(8,128)(2,1)S(1)} %copy-done.4, bf16[192,2048]{1,0:T(8,128)(2,1)S(1)} %copy-done.2, bf16[192,2048]{1,0:T(8,128)(2,1)} %collective-permute-done.3.refs_3_.refs_13_, ...), custom_call_target="tpu_custom_call" | custom-call | flops 3221225472 | bytes 8388608 | tf_op jit(solution)/shard_map/pallas_call | solution.py:192
  (14 shorter events, 0.0 us)
Async XLA Ops:
  0.0 87.6 %copy-start.8 = (s32[2048]{0:T(1024)S(1)}, s32[2048]{0:T(1024)}, u32[]{:S(2)}) copy-start(s32[2048]{0:T(1024)} %param.7) | copy-start | bytes 24580
  1.0 11.8 %collective-permute-start = (bf16[32,6144]{1,0:T(8,128)(2,1)S(1)}, bf16[32,6144]{1,0:T(8,128)(2,1)S(1)}, u32[]{:S(2)}, u32[]{:S(2)}) collective-permute-start(bf16[32,6144]{1,0:T(8,128)(2,1)S(1)} %slice.12), channel_id=1, source_target_pairs={{0,1},{1,2},{2,3},{3,4},{4,5},{5,6},{6,7},{8,9},{9,10},{10,11},{11... | collective-permute-start | bytes 1179656 | tf_op jit(solution)/shard_map/ppermute | solution.py:245
  12.9 3.4 %copy-start = (bf16[2048,2048]{1,0:T(8,128)(2,1)S(1)}, bf16[2048,2048]{1,0:T(8,128)(2,1)}, u32[]{:S(2)}) copy-start(bf16[2048,2048]{1,0:T(8,128)(2,1)} %constant.6.clone.basis_ref) | copy-start | bytes 25165828
  16.3 1.2 copy-start.5
  17.6 0.8 copy-start.6
  18.3 0.7 copy-start.7
  91.1 21.6 %collective-permute-start.2 = (bf16[192,2048]{1,0:T(8,128)(2,1)S(1)}, bf16[192,2048]{1,0:T(8,128)(2,1)S(1)}, u32[]{:S(2)}, u32[]{:S(2)}) collective-permute-start(bf16[192,2048]{1,0:T(8,128)(2,1)S(1)} %shard_map.56.refs_0_.refs_10_), channel_id=1, source_target_pairs={{1,0},{0,1},{3,2},{2,3},{5,4},{4,5},{7,6},{6,7},{9,8},{8,9},{11,10... | collective-permute-start | bytes 2359304 | tf_op jit(solution)/shard_map/ppermute | solution.py:217
  94.9 24.1 %collective-permute-start.1 = (bf16[192,2048]{1,0:T(8,128)(2,1)S(1)}, bf16[192,2048]{1,0:T(8,128)(2,1)S(1)}, u32[]{:S(2)}, u32[]{:S(2)}) collective-permute-start(bf16[192,2048]{1,0:T(8,128)(2,1)S(1)} %shard_map.56.refs_0_.refs_10_), channel_id=1, source_target_pairs={{2,0},{3,1},{4,2},{5,3},{6,4},{7,5},{0,6},{1,7},{10,8},{11,9},{12,... | collective-permute-start | bytes 2359304 | tf_op jit(solution)/shard_map/ppermute | solution.py:217
  112.8 25.0 %collective-permute-start.5 = (bf16[192,2048]{1,0:T(8,128)(2,1)S(1)}, bf16[192,2048]{1,0:T(8,128)(2,1)S(1)}, u32[]{:S(2)}, u32[]{:S(2)}) collective-permute-start(bf16[192,2048]{1,0:T(8,128)(2,1)S(1)} %collective-permute-done.2.refs_2_.refs_12_), channel_id=1, source_target_pairs={{6,0},{7,1},{0,2},{1,3},{2,4},{3,5},{4,6},{5,7},{14,8},{15,9},{8,1... | collective-permute-start | bytes 2359304 | tf_op jit(solution)/shard_map/ppermute | solution.py:217
  118.1 0.9 copy-start.1
  119.0 25.1 %copy-start.3 = (bf16[192,2048]{1,0:T(8,128)(2,1)}, bf16[192,2048]{1,0:T(8,128)(2,1)S(1)}, u32[]{:S(2)}) copy-start(bf16[192,2048]{1,0:T(8,128)(2,1)S(1)} %collective-permute-done.1.refs_1_.refs_11_) | copy-start | bytes 2359300
  119.0 22.2 %collective-permute-start.6 = (bf16[192,2048]{1,0:T(8,128)(2,1)S(1)}, bf16[192,2048]{1,0:T(8,128)(2,1)S(1)}, u32[]{:S(2)}, u32[]{:S(2)}) collective-permute-start(bf16[192,2048]{1,0:T(8,128)(2,1)S(1)} %collective-permute-done.1.refs_1_.refs_11_), channel_id=1, source_target_pairs={{2,0},{3,1},{4,2},{5,3},{6,4},{7,5},{0,6},{1,7},{10,8},{11,9},{12,... | collective-permute-start | bytes 2359304 | tf_op jit(solution)/shard_map/ppermute | solution.py:217
  122.5 21.6 %collective-permute-start.4 = (bf16[192,2048]{1,0:T(8,128)(2,1)S(1)}, bf16[192,2048]{1,0:T(8,128)(2,1)S(1)}, u32[]{:S(2)}, u32[]{:S(2)}) collective-permute-start(bf16[192,2048]{1,0:T(8,128)(2,1)S(1)} %collective-permute-done.1.refs_1_.refs_11_), channel_id=1, source_target_pairs={{1,0},{0,1},{3,2},{2,3},{5,4},{4,5},{7,6},{6,7},{9,8},{8,9},{11,10... | collective-permute-start | bytes 2359304 | tf_op jit(solution)/shard_map/ppermute | solution.py:217
  126.2 28.6 %collective-permute-start.3 = (bf16[192,2048]{1,0:T(8,128)(2,1)S(1)}, bf16[192,2048]{1,0:T(8,128)(2,1)}, u32[]{:S(2)}, u32[]{:S(2)}) collective-permute-start(bf16[192,2048]{1,0:T(8,128)(2,1)S(1)} %shard_map.56.refs_0_.refs_10_), channel_id=1, source_target_pairs={{6,0},{7,1},{0,2},{1,3},{2,4},{3,5},{4,6},{5,7},{14,8},{15,9},{8,1... | collective-permute-start | bytes 2359304 | tf_op jit(solution)/shard_map/ppermute | solution.py:217
  138.6 20.3 %collective-permute-start.8 = (bf16[64,2048]{1,0:T(8,128)(2,1)}, bf16[64,2048]{1,0:T(8,128)(2,1)S(1)}, u32[]{:S(2)}, u32[]{:S(2)}) collective-permute-start(bf16[64,2048]{1,0:T(8,128)(2,1)} %slice.17), channel_id=1, source_target_pairs={{6,0},{7,1},{0,2},{1,3},{2,4},{3,5},{4,6},{5,7},{14,8},{15,9},{8,1... | collective-permute-start | bytes 786440 | tf_op jit(solution)/shard_map/ppermute | solution.py:217
  142.0 16.9 %collective-permute-start.9 = (bf16[64,2048]{1,0:T(8,128)(2,1)}, bf16[64,2048]{1,0:T(8,128)(2,1)}, u32[]{:S(2)}, u32[]{:S(2)}) collective-permute-start(bf16[64,2048]{1,0:T(8,128)(2,1)} %slice.18), channel_id=1, source_target_pairs={{1,0},{0,1},{3,2},{2,3},{5,4},{4,5},{7,6},{6,7},{9,8},{8,9},{11,10... | collective-permute-start | bytes 786440 | tf_op jit(solution)/shard_map/ppermute | solution.py:217
  144.9 14.0 %collective-permute-start.7 = (bf16[64,2048]{1,0:T(8,128)(2,1)}, bf16[64,2048]{1,0:T(8,128)(2,1)}, u32[]{:S(2)}, u32[]{:S(2)}) collective-permute-start(bf16[64,2048]{1,0:T(8,128)(2,1)} %slice.16), channel_id=1, source_target_pairs={{2,0},{3,1},{4,2},{5,3},{6,4},{7,5},{0,6},{1,7},{10,8},{11,9},{12,... | collective-permute-start | bytes 786440 | tf_op jit(solution)/shard_map/ppermute | solution.py:217
  158.9 1.1 copy-start.2
  160.0 1.1 copy-start.4

commit v2 on v1

v2 whole, which is shorter than its diff:
```python
import functools

import jax
import jax.numpy as jnp
import numpy as np
from jax import lax
from jax.experimental import pallas as pl
from jax.experimental.pallas import tpu as pltpu
from jax.sharding import PartitionSpec as P

CHANNELS = 1024
TAPS = 4
CORR = 12
VMEM_LIMIT = 32 << 20
NT = (((1,), (1,)), ((), ()))


def make_basis(bands, length):
    index = np.arange(length, dtype=np.int64)
    m = (np.arange(CHANNELS, dtype=np.int64)[:, None] * index[None, :]) % length
    phases = np.float32(2.0 * np.pi / length) * m.astype(np.float32)
    stacked = np.stack([np.cos(phases), -np.sin(phases)], axis=0)
    stacked = stacked.reshape(2, bands, CHANNELS // bands, length).transpose(1, 0, 2, 3)
    return stacked.reshape(2 * CHANNELS, length).astype(jnp.bfloat16)


def spectra_kernel(group, span, start_ref, volt_ref, before_ref, taper_ref, basis_ref, *refs):
    out_ref, filt = refs[-2:]
    sig_dev = volt_ref.shape[0]
    length = taper_ref.shape[1]
    bands = out_ref.shape[0]
    ch_band = basis_ref.shape[0] // (2 * bands)
    held = group * 2 * ch_band

    def frame(at):
        if at < 0:
            return before_ref[:, (at + TAPS - 1) * length : (at + TAPS) * length]
        return volt_ref[:, at * length : (at + 1) * length]

    totals = []
    for at in span:
        total = taper_ref[0:1, :] * frame(at - TAPS + 1).astype(jnp.float32)
        for tap in range(1, TAPS):
            total = total + taper_ref[tap : tap + 1, :] * frame(at + tap - TAPS + 1).astype(
                jnp.float32
            )
        totals.append(total)
    filt[...] = jnp.transpose(jnp.concatenate(totals, axis=0)).astype(jnp.bfloat16)

    part = 8
    shape = (2 * CORR, part * 2 * ch_band)
    row = lax.broadcasted_iota(jnp.int32, shape, 0)
    at_first = lax.broadcasted_iota(jnp.int32, shape, 1) - row
    at_first = at_first - jnp.where(row < CORR, 0, ch_band - CORR)

    def bands_from(at, carry):
        first = pl.multiple_of(at * held, held)
        products = jnp.dot(
            basis_ref[pl.ds(first, held), :], filt[...], preferred_element_type=jnp.float32
        ).astype(jnp.bfloat16)
        for begin in range(0, group, part):
            band_at = at * group + begin
            picks = [
                jnp.where(at_first == band * 2 * ch_band + start_ref[band_at + band], 1.0, 0.0)
                for band in range(part)
            ]
            spectra = jnp.dot(
                jnp.concatenate(picks, axis=0).astype(jnp.bfloat16),
                products[begin * 2 * ch_band : (begin + part) * 2 * ch_band],
                preferred_element_type=jnp.float32,
            )
            for band in range(part):
                these = spectra[band * 2 * CORR : (band + 1) * 2 * CORR].astype(jnp.bfloat16)
                if len(refs) == 3:
                    these = jnp.concatenate([these, refs[0][band_at + band]], axis=1)
                out_ref[band_at + band] = these
        return carry

    lax.fori_loop(0, bands // group, bands_from, 0)


def picked_spectra(voltages, before, taper, basis, band_start, bands, span, later=None):
    sig_dev, samples = voltages.shape
    length = taper.shape[1]
    columns = sig_dev * len(span)
    wide = columns if later is None else columns + later.shape[2]
    beside = [] if later is None else [later]
    whole = pl.BlockSpec(memory_space=pltpu.VMEM)
    return pl.pallas_call(
        functools.partial(spectra_kernel, 16, span),
        in_specs=[pl.BlockSpec(memory_space=pltpu.SMEM)] + [whole] * (4 + len(beside)),
        out_specs=whole,
        scratch_shapes=[pltpu.VMEM((length, columns), jnp.bfloat16)],
        out_shape=jax.ShapeDtypeStruct((bands, 2 * CORR, wide), jnp.bfloat16),
        compiler_params=pltpu.CompilerParams(vmem_limit_bytes=VMEM_LIMIT),
        cost_estimate=pl.CostEstimate(
            flops=2 * 2 * CHANNELS * length * columns,
            bytes_accessed=2 * 2 * CHANNELS * length + 4 * sig_dev * samples,
            transcendentals=0,
        ),
    )(band_start, voltages, before, taper, basis, *beside)


def order_kernel(turned_ref, input_ref, out_ref, lined):
    bands, values, columns = turned_ref.shape
    signals = out_ref.shape[1]
    sig_dev = signals // bands
    frames = columns // sig_dev
    per_tile = 128 // sig_dev

    def tile(at, carry):
        lane = lax.broadcasted_iota(jnp.int32, (values, 128), 1) // sig_dev
        blocks = [turned_ref[at * per_tile + k].astype(jnp.float32) for k in range(per_tile)]
        for frame in range(frames):
            half, place = frame // per_tile, frame % per_tile
            merged = None
            for k in range(per_tile):
                piece = blocks[k][:, half * 128 : (half + 1) * 128]
                shift = (k - place) * sig_dev % 128
                if shift:
                    piece = pltpu.roll(piece, shift, 1)
                merged = piece if merged is None else jnp.where(lane == k, piece, merged)
            lined[at, frame * values : (frame + 1) * values, :] = merged
        return carry

    lax.fori_loop(0, bands // per_tile, tile, 0)
    wanted = jnp.broadcast_to(input_ref[...], (16, signals)).astype(jnp.int16)
    row = lax.broadcasted_iota(jnp.int32, (16, signals), 0).astype(jnp.int16)
    one = jnp.ones((16, signals), jnp.bfloat16)
    zero = jnp.zeros((16, signals), jnp.bfloat16)
    part = 256
    total = None
    for at in range(signals // part):
        held = jnp.concatenate([lined[2 * at], lined[2 * at + 1]], axis=1).astype(jnp.bfloat16)
        chosen = jnp.concatenate(
            [
                jnp.where(row == wanted - (at * part + first), one, zero)
                for first in range(0, part, 16)
            ],
            axis=0,
        )
        product = jnp.dot(held, chosen, preferred_element_type=jnp.float32)
        total = product if total is None else total + product
    out_ref[...] = total.astype(jnp.bfloat16)


def order_signals(turned, input_of):
    bands, values, columns = turned.shape
    signals = input_of.shape[0]
    rows = values * columns * bands // signals
    return pl.pallas_call(
        order_kernel,
        in_specs=[pl.BlockSpec(memory_space=pltpu.VMEM)] * 2,
        out_specs=pl.BlockSpec(memory_space=pltpu.VMEM),
        out_shape=jax.ShapeDtypeStruct((rows, signals), jnp.bfloat16),
        scratch_shapes=[pltpu.VMEM((signals // 128, rows, 128), jnp.float32)],
        compiler_params=pltpu.CompilerParams(vmem_limit_bytes=VMEM_LIMIT),
        cost_estimate=pl.CostEstimate(
            flops=2 * rows * signals * signals,
            bytes_accessed=4 * rows * signals,
            transcendentals=0,
        ),
    )(turned, input_of.reshape(1, signals))


def correlate_kernel(scale, count, tile, position_ref, *refs):
    blocks, before, out_ref, left = refs[:count], refs[count:-2], refs[-2], refs[-1]
    row_count = left.shape[0] // 2
    values = 2 * CORR
    step = pl.program_id(0)

    @pl.when(step == 0)
    def _():
        first = pl.multiple_of(position_ref[0] * row_count, row_count)
        own = jnp.concatenate([r[:, pl.ds(first, row_count)] for r in blocks], axis=0)
        part = 192
        row = lax.broadcasted_iota(jnp.int32, (part, part), 0)
        column = lax.broadcasted_iota(jnp.int32, (part, part), 1)
        upper = row % values < CORR
        swap = jnp.where(upper & (column == row + CORR), 1.0, 0.0)
        swap = swap - jnp.where(jnp.logical_not(upper) & (column == row - CORR), 1.0, 0.0)
        swap = swap.astype(jnp.bfloat16)
        pieces = [own[at : at + part] for at in range(0, own.shape[0], part)]
        turned = [jnp.dot(swap, p, preferred_element_type=jnp.float32) for p in pieces]
        left[:row_count] = jnp.transpose(own.astype(jnp.float32)).astype(jnp.bfloat16)
        left[row_count:] = jnp.transpose(jnp.concatenate(turned, axis=0)).astype(jnp.bfloat16)

    columns = pl.ds(pl.multiple_of(step * tile, tile), tile)
    right = jnp.concatenate([r[:, columns] for r in blocks], axis=0)
    summed = jnp.dot(left[...], right, preferred_element_type=jnp.float32)
    if before:
        summed = summed + before[0][:, columns]
    if scale is None:
        out_ref[:, columns] = summed
    else:
        summed = summed * scale
        out_ref[0, 0] = summed[:row_count].astype(jnp.bfloat16)
        out_ref[0, 1] = summed[row_count:].astype(jnp.bfloat16)


def correlate(position, blocks, row_count, before=(), scale=None):
    signals = blocks[0].shape[1]
    depth = sum(b.shape[0] for b in blocks)
    tile = 512
    whole = pl.BlockSpec(memory_space=pltpu.VMEM)
    if scale is None:
        out_spec = whole
        out_shape = jax.ShapeDtypeStruct((2 * row_count, signals), jnp.float32)
    else:
        out_spec = pl.BlockSpec((1, 2, row_count, tile), lambda g, p: (0, 0, 0, g))
        out_shape = jax.ShapeDtypeStruct((1, 2, row_count, signals), jnp.bfloat16)
    return pl.pallas_call(
        functools.partial(correlate_kernel, scale, len(blocks), tile),
        grid_spec=pltpu.PrefetchScalarGridSpec(
            num_scalar_prefetch=1,
            grid=(signals // tile,),
            in_specs=[whole] * (len(blocks) + len(before)),
            out_specs=out_spec,
            scratch_shapes=[pltpu.VMEM((2 * row_count, depth), jnp.bfloat16)],
        ),
        out_shape=out_shape,
        compiler_params=pltpu.CompilerParams(vmem_limit_bytes=VMEM_LIMIT),
        cost_estimate=pl.CostEstimate(
            flops=4 * row_count * signals * depth,
            bytes_accessed=2 * signals * depth + 8 * row_count * signals,
            transcendentals=0,
        ),
    )(position, *blocks, *before)


def from_slice(value, dx, dy, slices):
    along = slices // 2
    pairs = []
    for target in range(slices):
        source = ((target // 2 + dx) % along) * 2 + (target % 2 + dy) % 2
        pairs.append((source, target))
    return lax.ppermute(value, "tslice", pairs)


def gather_and_correlate(own, position, slices, row_count, scale):
    take = functools.partial(from_slice, slices=slices)
    near = lax.optimization_barrier((take(own, 1, 0), take(own, 0, 1), take(own, -1, 0)))
    right, other, left = near
    summed = correlate(position, [own, right, other, left], row_count)
    right_other, left_other, far = take(right, 0, 1), take(other, -1, 0), take(right, 1, 0)
    left_other, summed = lax.optimization_barrier((left_other, summed))
    third = own.shape[0] // 3
    last = [
        take(right_other[:third], 1, 0),
        take(left_other[third : 2 * third], -1, 0),
        take(far[2 * third :], 0, 1),
    ]
    summed = correlate(position, [right_other, left_other, far], row_count, [summed])
    return correlate(position, last, row_count, [summed], scale)


def on_device(voltages, taper, input_of, band_start):
    length = 2 * CHANNELS
    bands = lax.axis_size("band")
    slices = lax.axis_size("tslice")
    frames = voltages.shape[1] // length
    signals = input_of.shape[0]
    position = lax.axis_index("tslice")
    tail = voltages[:, (frames - TAPS + 1) * length :]
    before = lax.ppermute(tail, "tslice", [(s, s + 1) for s in range(slices - 1)])
    basis = jnp.asarray(make_basis(bands, length))
    half = frames // 2
    transform = functools.partial(picked_spectra, voltages)
    rest = (taper, basis, band_start, bands)
    later = transform(voltages[:8, :128], *rest, tuple(range(half, frames)))
    spectra = transform(before, *rest, tuple(range(half)), later)
    turned = lax.all_to_all(spectra, "band", split_axis=0, concat_axis=0, tiled=True)
    own = order_signals(turned, input_of)
    position = position.astype(jnp.int32).reshape(1)
    scale = 1.0 / (CORR * frames * slices)
    return gather_and_correlate(own, position, slices, signals // slices, scale)


def solution(mesh):
    return jax.shard_map(
        on_device,
        mesh=mesh,
        in_specs=(P("band", "tslice"), P(), P(), P()),
        out_specs=P("band", None, "tslice", None),
        check_vma=False,
    )
```

time: 169 us -> 157 us (0.929)
  waiting for transfers between devices: 40.6 us -> 26.4 us
  Pallas kernels: 17.6 us -> 22.4 us
  starting transfers between devices: 35.8 us -> 33.4 us
    ppermute x1, waiting for transfers between devices: 8.33 us -> 0.01 us  [on_device(): lax.ppermute(tail, 'tslice', [(s, s + 1) for s in range(slices - 1)])]
    ppermute x9, waiting for transfers between devices: 32.3 us -> 26.4 us  [from_slice(): return lax.ppermute(value, 'tslice', pairs)]
    pallas_call x2 -> x5, Pallas kernels: 14.1 us -> 18.9 us  [the longest x2 9.48 us: picked_spectra(): pl.pallas_call(functools.partial(spectra_kernel, 16, span), in_specs=[pl....]
    ppermute x9, starting transfers between devices: 32.3 us -> 29.9 us  [from_slice(): return lax.ppermute(value, 'tslice', pairs)]
    unnamed x18 -> x20, local copies, waits for them, and re-layouts: 9.23 us -> 10.1 us
  transfers between devices with their start and end apart: 10 -> 10, of which waited for: 5 -> 5; matrix products, arithmetic and copies ran while one was open for 1% -> 0% of each run, Pallas kernels for 0% -> 7%
where the time goes in v2:
time: 157 us; the launch traced here: 156 us
  blocking collectives  61.7 us (39%)
  starting transfers between devices  33.4 us (21%)
  waiting for transfers between devices  26.4 us (17%)
  Pallas kernels  22.4 us (14%)
  local copies, waits for them, and re-layouts  11.8 us (8%)
    all_to_all x1, blocking collectives, on_device(): lax.all_to_all(spectra, 'band', split_axis=0, concat_axis=0, tiled=True)  61.7 us
    ppermute x9, starting transfers between devices, from_slice(): return lax.ppermute(value, 'tslice', pairs)  29.9 us
    ppermute x9, waiting for transfers between devices, from_slice(): return lax.ppermute(value, 'tslice', pairs)  26.4 us
    unnamed x20, local copies, waits for them, and re-layouts  10.1 us
    pallas_call x2, Pallas kernels, picked_spectra(): pl.pallas_call(functools.partial(spectra_kernel, 16, span), in_specs=[pl....  9.48 us
    pallas_call x3, Pallas kernels, correlate(): pl.pallas_call(functools.partial(correlate_kernel, scale, len(blocks), ti...  9.37 us
    pallas_call x1, Pallas kernels, order_signals(): pl.pallas_call(order_kernel, in_specs=[pl.BlockSpec(memory_space=pltpu.VM...  3.56 us
    ppermute x1, starting transfers between devices, on_device(): lax.ppermute(tail, 'tslice', [(s, s + 1) for s in range(slices - 1)])  3.5 us
  transfers between devices with their start and end apart: 10, of which 5 were waited for; matrix products, arithmetic and copies ran while one was open for 0% of the time, Pallas kernels for 7%

profile of v2, /device:TPU:32, one launch (start us, length us, event | category | flops | bytes accessed | tf_op | source)
XLA Modules:
  0.0 155.9 jit_solution(15870487233064327086)
XLA Ops:
  0.0 1.0 slice.15
  1.0 3.5 %collective-permute-start = (bf16[32,6144]{1,0:T(8,128)(2,1)S(1)}, bf16[32,6144]{1,0:T(8,128)(2,1)S(1)}, u32[]{:S(2)}, u32[]{:S(2)}) collective-permute-start(bf16[32,6144]{1,0:T(8,128)(2,1)S(1)} %slice.15), channel_id=1, source_target_pairs={{0,1},{1,2},{2,3},{3,4},{4,5},{5,6},{6,7},{8,9},{9,10},{10,11},{11... | collective-permute-start | bytes 1179656 | tf_op jit(solution)/shard_map/ppermute | solution.py:265
  4.5 0.7 slice.16.before_ref
  5.2 3.4 %copy-done = bf16[2048,2048]{1,0:T(8,128)(2,1)S(1)} copy-done((bf16[2048,2048]{1,0:T(8,128)(2,1)S(1)}, bf16[2048,2048]{1,0:T(8,128)(2,1)}, u32[]{:S(2)}) %copy-start) | copy-done | bytes 8388632
  8.6 1.2 copy-done.2
  9.8 0.8 copy-done.7
  10.6 0.7 copy-done.8
  11.2 4.7 %shard_map.55.refs_0_ = bf16[64,24,128]{2,1,0:T(8,128)(2,1)S(1)} custom-call(s32[64]{0:T(128)S(1)} %copy-done.8, bf16[32,16384]{1,0:T(8,128)(2,1)S(1)} %copy-done.2, bf16[8,128]{1,0:T(8,128)(2,1)S(1)} %slice.16.before_ref, f32[4,2048]{1,0:T(4,128)S(1)} %copy-done.7, bf16[2048,2048]{1,0:T(8,128)(2,1)S(1)} %copy-done), custom_call_target="tpu_custom_call" | custom-call | flops 1073741824 | bytes 10485760 | tf_op jit(solution)/shard_map/pallas_call | solution.py:89
  16.0 4.7 %shard_map.56 = bf16[64,24,256]{2,1,0:T(8,128)(2,1)S(1)} custom-call(s32[64]{0:T(128)S(1)} %copy-done.8, bf16[32,16384]{1,0:T(8,128)(2,1)S(1)} %copy-done.2, bf16[32,6144]{1,0:T(8,128)(2,1)S(1)} %collective-permute-done.before_ref, f32[4,2048]{1,0:T(4,128)S(1)} %copy-done.7, bf16[2048,2048]{1,0:T(8,128)(2,1)S(1)} %copy-done.1, ...), custom_call_target="tpu_custom_call" | custom-call | flops 1073741824 | bytes 10485760 | tf_op jit(solution)/shard_map/pallas_call | solution.py:89
  20.8 61.7 %all_to_all.5.turned_ref = bf16[64,24,256]{2,1,0:T(8,128)(2,1)S(1)} all-to-all(bf16[64,24,256]{2,1,0:T(8,128)(2,1)S(1)} %shard_map.56), channel_id=1, replica_groups=mesh['band'=64,'tslice'=8] {'band'}, dimensions={0} | all-to-all | bytes 1572864 | tf_op jit(solution)/shard_map/all_to_all | solution.py:272
  82.4 3.6 %shard_map.57.refs_0_ = bf16[192,2048]{1,0:T(8,128)(2,1)S(1)} custom-call(bf16[64,24,256]{2,1,0:T(8,128)(2,1)S(1)} %all_to_all.5.turned_ref, s32[1,2048]{1,0:T(1,128)S(1)} %bitcast.2), custom_call_target="tpu_custom_call" | custom-call | flops 1610612736 | bytes 1572864 | tf_op jit(solution)/shard_map/pallas_call | solution.py:151
  86.0 4.7 %collective-permute-start.1 = (bf16[192,2048]{1,0:T(8,128)(2,1)S(1)}, bf16[192,2048]{1,0:T(8,128)(2,1)S(1)}, u32[]{:S(2)}, u32[]{:S(2)}) collective-permute-start(bf16[192,2048]{1,0:T(8,128)(2,1)S(1)} %shard_map.57.refs_0_), channel_id=1, source_target_pairs={{2,0},{3,1},{4,2},{5,3},{6,4},{7,5},{0,6},{1,7},{10,8},{11,9},{12,... | collective-permute-start | bytes 2359304 | tf_op jit(solution)/shard_map/ppermute | solution.py:237
  90.7 1.9 %collective-permute-start.2 = (bf16[192,2048]{1,0:T(8,128)(2,1)S(1)}, bf16[192,2048]{1,0:T(8,128)(2,1)}, u32[]{:S(2)}, u32[]{:S(2)}) collective-permute-start(bf16[192,2048]{1,0:T(8,128)(2,1)S(1)} %shard_map.57.refs_0_), channel_id=1, source_target_pairs={{1,0},{0,1},{3,2},{2,3},{5,4},{4,5},{7,6},{6,7},{9,8},{8,9},{11,10... | collective-permute-start | bytes 2359304 | tf_op jit(solution)/shard_map/ppermute | solution.py:237
  92.6 2.2 %collective-permute-start.3 = (bf16[192,2048]{1,0:T(8,128)(2,1)S(1)}, bf16[192,2048]{1,0:T(8,128)(2,1)S(1)}, u32[]{:S(2)}, u32[]{:S(2)}) collective-permute-start(bf16[192,2048]{1,0:T(8,128)(2,1)S(1)} %shard_map.57.refs_0_), channel_id=1, source_target_pairs={{6,0},{7,1},{0,2},{1,3},{2,4},{3,5},{4,6},{5,7},{14,8},{15,9},{8,1... | collective-permute-start | bytes 2359304 | tf_op jit(solution)/shard_map/ppermute | solution.py:237
  94.8 0.9 copy-done.3
  95.7 12.1 %collective-permute-done.1.refs_1_ = bf16[192,2048]{1,0:T(8,128)(2,1)S(1)} collective-permute-done((bf16[192,2048]{1,0:T(8,128)(2,1)S(1)}, bf16[192,2048]{1,0:T(8,128)(2,1)S(1)}, u32[]{:S(2)}, u32[]{:S(2)}) %collective-permute-start.1) | collective-permute-done | bytes 786464 | tf_op jit(solution)/shard_map/ppermute | solution.py:237
  107.8 4.2 %collective-permute-done.2.refs_2_ = bf16[192,2048]{1,0:T(8,128)(2,1)} collective-permute-done((bf16[192,2048]{1,0:T(8,128)(2,1)S(1)}, bf16[192,2048]{1,0:T(8,128)(2,1)}, u32[]{:S(2)}, u32[]{:S(2)}) %collective-permute-start.2) | collective-permute-done | bytes 786464 | tf_op jit(solution)/shard_map/ppermute | solution.py:237
  112.0 3.0 %collective-permute-done.3.refs_3_ = bf16[192,2048]{1,0:T(8,128)(2,1)S(1)} collective-permute-done((bf16[192,2048]{1,0:T(8,128)(2,1)S(1)}, bf16[192,2048]{1,0:T(8,128)(2,1)S(1)}, u32[]{:S(2)}, u32[]{:S(2)}) %collective-permute-start.3) | collective-permute-done | bytes 786464 | tf_op jit(solution)/shard_map/ppermute | solution.py:237
  115.0 0.9 copy-done.5
  115.9 1.9 %collective-permute-start.6 = (bf16[192,2048]{1,0:T(8,128)(2,1)}, bf16[192,2048]{1,0:T(8,128)(2,1)S(1)}, u32[]{:S(2)}, u32[]{:S(2)}) collective-permute-start(bf16[192,2048]{1,0:T(8,128)(2,1)} %collective-permute-done.2.refs_2_), channel_id=1, source_target_pairs={{6,0},{7,1},{0,2},{1,3},{2,4},{3,5},{4,6},{5,7},{14,8},{15,9},{8,1... | collective-permute-start | bytes 2359304 | tf_op jit(solution)/shard_map/ppermute | solution.py:237
  117.8 3.6 %collective-permute-start.4 = (bf16[192,2048]{1,0:T(8,128)(2,1)S(1)}, bf16[192,2048]{1,0:T(8,128)(2,1)S(1)}, u32[]{:S(2)}, u32[]{:S(2)}) collective-permute-start(bf16[192,2048]{1,0:T(8,128)(2,1)S(1)} %collective-permute-done.1.refs_1_), channel_id=1, source_target_pairs={{1,0},{0,1},{3,2},{2,3},{5,4},{4,5},{7,6},{6,7},{9,8},{8,9},{11,10... | collective-permute-start | bytes 2359304 | tf_op jit(solution)/shard_map/ppermute | solution.py:237
  121.5 5.1 %collective-permute-start.8 = (bf16[192,2048]{1,0:T(8,128)(2,1)S(1)}, bf16[192,2048]{1,0:T(8,128)(2,1)S(1)}, u32[]{:S(2)}, u32[]{:S(2)}) collective-permute-start(bf16[192,2048]{1,0:T(8,128)(2,1)S(1)} %collective-permute-done.1.refs_1_), channel_id=1, source_target_pairs={{2,0},{3,1},{4,2},{5,3},{6,4},{7,5},{0,6},{1,7},{10,8},{11,9},{12,... | collective-permute-start | bytes 2359304 | tf_op jit(solution)/shard_map/ppermute | solution.py:237
  126.6 1.1 copy-done.4
  127.8 1.1 copy-done.6
  128.9 3.9 %shard_map.58.refs_3_ = f32[512,2048]{1,0:T(8,128)S(1)} custom-call(s32[1]{0:T(128)} %bitcast.position_ref, bf16[192,2048]{1,0:T(8,128)(2,1)S(1)} %copy-done.4, bf16[192,2048]{1,0:T(8,128)(2,1)S(1)} %collective-permute-done.1.refs_1_, bf16[192,2048]{1,0:T(8,128)(2,1)} %collective-permute-done.2.refs_2_, bf16[192,2048]{1,0:T(8,128)(2,1)S(1)} %copy-done.6), custom_call_target="tpu_custom_call" | custom-call | flops 1610612736 | bytes 7340032 | tf_op jit(solution)/shard_map/pallas_call | solution.py:212
  132.8 4.9 %collective-permute-done.6.refs_1_ = bf16[192,2048]{1,0:T(8,128)(2,1)S(1)} collective-permute-done((bf16[192,2048]{1,0:T(8,128)(2,1)}, bf16[192,2048]{1,0:T(8,128)(2,1)S(1)}, u32[]{:S(2)}, u32[]{:S(2)}) %collective-permute-start.6) | collective-permute-done | bytes 786464 | tf_op jit(solution)/shard_map/ppermute | solution.py:237
  137.7 1.9 %collective-permute-start.7 = (bf16[64,2048]{1,0:T(8,128)(2,1)S(1)}, bf16[64,2048]{1,0:T(8,128)(2,1)S(1)}, u32[]{:S(2)}, u32[]{:S(2)}) collective-permute-start(bf16[64,2048]{1,0:T(8,128)(2,1)S(1)} %slice.18), channel_id=1, source_target_pairs={{6,0},{7,1},{0,2},{1,3},{2,4},{3,5},{4,6},{5,7},{14,8},{15,9},{8,1... | collective-permute-start | bytes 786440 | tf_op jit(solution)/shard_map/ppermute | solution.py:237
  139.7 5.1 %collective-permute-start.5 = (bf16[64,2048]{1,0:T(8,128)(2,1)S(1)}, bf16[64,2048]{1,0:T(8,128)(2,1)S(1)}, u32[]{:S(2)}, u32[]{:S(2)}) collective-permute-start(bf16[64,2048]{1,0:T(8,128)(2,1)S(1)} %slice.20), channel_id=1, source_target_pairs={{2,0},{3,1},{4,2},{5,3},{6,4},{7,5},{0,6},{1,7},{10,8},{11,9},{12,... | collective-permute-start | bytes 786440 | tf_op jit(solution)/shard_map/ppermute | solution.py:237
  144.8 3.3 %collective-permute-start.9 = (bf16[64,2048]{1,0:T(8,128)(2,1)S(1)}, bf16[64,2048]{1,0:T(8,128)(2,1)S(1)}, u32[]{:S(2)}, u32[]{:S(2)}) collective-permute-start(bf16[64,2048]{1,0:T(8,128)(2,1)S(1)} %slice.21), channel_id=1, source_target_pairs={{1,0},{0,1},{3,2},{2,3},{5,4},{4,5},{7,6},{6,7},{9,8},{8,9},{11,10... | collective-permute-start | bytes 786440 | tf_op jit(solution)/shard_map/ppermute | solution.py:237
  148.2 2.7 %shard_map.59.refs_3_ = f32[512,2048]{1,0:T(8,128)S(1)} custom-call(s32[1]{0:T(128)} %bitcast.position_ref, bf16[192,2048]{1,0:T(8,128)(2,1)S(1)} %collective-permute-done.4.refs_0_, bf16[192,2048]{1,0:T(8,128)(2,1)S(1)} %collective-permute-done.6.refs_1_, bf16[192,2048]{1,0:T(8,128)(2,1)S(1)} %collective-permute-done.8.refs_2_, ...), custom_call_target="tpu_custom_call" | custom-call | flops 1207959552 | bytes 6553600 | tf_op jit(solution)/shard_map/pallas_call | solution.py:212
  150.9 2.2 %collective-permute-done.9.refs_2_ = bf16[64,2048]{1,0:T(8,128)(2,1)S(1)} collective-permute-done((bf16[64,2048]{1,0:T(8,128)(2,1)S(1)}, bf16[64,2048]{1,0:T(8,128)(2,1)S(1)}, u32[]{:S(2)}, u32[]{:S(2)}) %collective-permute-start.9) | collective-permute-done | bytes 262176 | tf_op jit(solution)/shard_map/ppermute | solution.py:237
  153.1 2.8 %shard_map.60 = bf16[1,2,256,2048]{3,2,1,0:T(8,128)(2,1)} custom-call(s32[1]{0:T(128)} %bitcast.position_ref, bf16[64,2048]{1,0:T(8,128)(2,1)S(1)} %collective-permute-done.5.refs_0_, bf16[64,2048]{1,0:T(8,128)(2,1)S(1)} %collective-permute-done.7.refs_1_, bf16[64,2048]{1,0:T(8,128)(2,1)S(1)} %collective-permute-done.9.refs_2_, ...), custom_call_target="tpu_custom_call" | custom-call | flops 402653184 | bytes 4980736 | tf_op jit(solution)/shard_map/pallas_call | solution.py:212
  (20 shorter events, 0.1 us)
Async XLA Ops:
  1.0 15.0 %collective-permute-start = (bf16[32,6144]{1,0:T(8,128)(2,1)S(1)}, bf16[32,6144]{1,0:T(8,128)(2,1)S(1)}, u32[]{:S(2)}, u32[]{:S(2)}) collective-permute-start(bf16[32,6144]{1,0:T(8,128)(2,1)S(1)} %slice.15), channel_id=1, source_target_pairs={{0,1},{1,2},{2,3},{3,4},{4,5},{5,6},{6,7},{8,9},{9,10},{10,11},{11... | collective-permute-start | bytes 1179656 | tf_op jit(solution)/shard_map/ppermute | solution.py:265
  5.2 3.4 %copy-start = (bf16[2048,2048]{1,0:T(8,128)(2,1)S(1)}, bf16[2048,2048]{1,0:T(8,128)(2,1)}, u32[]{:S(2)}) copy-start(bf16[2048,2048]{1,0:T(8,128)(2,1)} %constant.6.clone.basis_ref) | copy-start | bytes 25165828
  8.6 1.2 copy-start.2
  9.8 0.8 copy-start.7
  10.6 0.7 copy-start.8
  11.2 4.8 %copy-start.1 = (bf16[2048,2048]{1,0:T(8,128)(2,1)S(1)}, bf16[2048,2048]{1,0:T(8,128)(2,1)}, u32[]{:S(2)}) copy-start(bf16[2048,2048]{1,0:T(8,128)(2,1)} %constant.6.clone.basis_ref) | copy-start | bytes 25165828
  16.0 66.4 %copy-start.9 = (s32[2048]{0:T(1024)S(1)}, s32[2048]{0:T(1024)}, u32[]{:S(2)}) copy-start(s32[2048]{0:T(1024)} %param.7) | copy-start | bytes 24580
  86.0 21.8 %collective-permute-start.1 = (bf16[192,2048]{1,0:T(8,128)(2,1)S(1)}, bf16[192,2048]{1,0:T(8,128)(2,1)S(1)}, u32[]{:S(2)}, u32[]{:S(2)}) collective-permute-start(bf16[192,2048]{1,0:T(8,128)(2,1)S(1)} %shard_map.57.refs_0_), channel_id=1, source_target_pairs={{2,0},{3,1},{4,2},{5,3},{6,4},{7,5},{0,6},{1,7},{10,8},{11,9},{12,... | collective-permute-start | bytes 2359304 | tf_op jit(solution)/shard_map/ppermute | solution.py:237
  90.7 21.3 %collective-permute-start.2 = (bf16[192,2048]{1,0:T(8,128)(2,1)S(1)}, bf16[192,2048]{1,0:T(8,128)(2,1)}, u32[]{:S(2)}, u32[]{:S(2)}) collective-permute-start(bf16[192,2048]{1,0:T(8,128)(2,1)S(1)} %shard_map.57.refs_0_), channel_id=1, source_target_pairs={{1,0},{0,1},{3,2},{2,3},{5,4},{4,5},{7,6},{6,7},{9,8},{8,9},{11,10... | collective-permute-start | bytes 2359304 | tf_op jit(solution)/shard_map/ppermute | solution.py:237
  92.6 22.4 %collective-permute-start.3 = (bf16[192,2048]{1,0:T(8,128)(2,1)S(1)}, bf16[192,2048]{1,0:T(8,128)(2,1)S(1)}, u32[]{:S(2)}, u32[]{:S(2)}) collective-permute-start(bf16[192,2048]{1,0:T(8,128)(2,1)S(1)} %shard_map.57.refs_0_), channel_id=1, source_target_pairs={{6,0},{7,1},{0,2},{1,3},{2,4},{3,5},{4,6},{5,7},{14,8},{15,9},{8,1... | collective-permute-start | bytes 2359304 | tf_op jit(solution)/shard_map/ppermute | solution.py:237
  94.8 0.9 copy-start.3
  115.0 0.9 copy-start.5
  115.9 21.8 %collective-permute-start.6 = (bf16[192,2048]{1,0:T(8,128)(2,1)}, bf16[192,2048]{1,0:T(8,128)(2,1)S(1)}, u32[]{:S(2)}, u32[]{:S(2)}) collective-permute-start(bf16[192,2048]{1,0:T(8,128)(2,1)} %collective-permute-done.2.refs_2_), channel_id=1, source_target_pairs={{6,0},{7,1},{0,2},{1,3},{2,4},{3,5},{4,6},{5,7},{14,8},{15,9},{8,1... | collective-permute-start | bytes 2359304 | tf_op jit(solution)/shard_map/ppermute | solution.py:237
  117.8 21.8 %collective-permute-start.4 = (bf16[192,2048]{1,0:T(8,128)(2,1)S(1)}, bf16[192,2048]{1,0:T(8,128)(2,1)S(1)}, u32[]{:S(2)}, u32[]{:S(2)}) collective-permute-start(bf16[192,2048]{1,0:T(8,128)(2,1)S(1)} %collective-permute-done.1.refs_1_), channel_id=1, source_target_pairs={{1,0},{0,1},{3,2},{2,3},{5,4},{4,5},{7,6},{6,7},{9,8},{8,9},{11,10... | collective-permute-start | bytes 2359304 | tf_op jit(solution)/shard_map/ppermute | solution.py:237
  121.5 23.3 %collective-permute-start.8 = (bf16[192,2048]{1,0:T(8,128)(2,1)S(1)}, bf16[192,2048]{1,0:T(8,128)(2,1)S(1)}, u32[]{:S(2)}, u32[]{:S(2)}) collective-permute-start(bf16[192,2048]{1,0:T(8,128)(2,1)S(1)} %collective-permute-done.1.refs_1_), channel_id=1, source_target_pairs={{2,0},{3,1},{4,2},{5,3},{6,4},{7,5},{0,6},{1,7},{10,8},{11,9},{12,... | collective-permute-start | bytes 2359304 | tf_op jit(solution)/shard_map/ppermute | solution.py:237
  126.6 1.1 copy-start.4
  127.8 1.1 copy-start.6
  137.7 13.2 %collective-permute-start.7 = (bf16[64,2048]{1,0:T(8,128)(2,1)S(1)}, bf16[64,2048]{1,0:T(8,128)(2,1)S(1)}, u32[]{:S(2)}, u32[]{:S(2)}) collective-permute-start(bf16[64,2048]{1,0:T(8,128)(2,1)S(1)} %slice.18), channel_id=1, source_target_pairs={{6,0},{7,1},{0,2},{1,3},{2,4},{3,5},{4,6},{5,7},{14,8},{15,9},{8,1... | collective-permute-start | bytes 786440 | tf_op jit(solution)/shard_map/ppermute | solution.py:237
  139.7 11.3 %collective-permute-start.5 = (bf16[64,2048]{1,0:T(8,128)(2,1)S(1)}, bf16[64,2048]{1,0:T(8,128)(2,1)S(1)}, u32[]{:S(2)}, u32[]{:S(2)}) collective-permute-start(bf16[64,2048]{1,0:T(8,128)(2,1)S(1)} %slice.20), channel_id=1, source_target_pairs={{2,0},{3,1},{4,2},{5,3},{6,4},{7,5},{0,6},{1,7},{10,8},{11,9},{12,... | collective-permute-start | bytes 786440 | tf_op jit(solution)/shard_map/ppermute | solution.py:237
  144.8 8.3 %collective-permute-start.9 = (bf16[64,2048]{1,0:T(8,128)(2,1)S(1)}, bf16[64,2048]{1,0:T(8,128)(2,1)S(1)}, u32[]{:S(2)}, u32[]{:S(2)}) collective-permute-start(bf16[64,2048]{1,0:T(8,128)(2,1)S(1)} %slice.21), channel_id=1, source_target_pairs={{1,0},{0,1},{3,2},{2,3},{5,4},{4,5},{7,6},{6,7},{9,8},{8,9},{11,10... | collective-permute-start | bytes 786440 | tf_op jit(solution)/shard_map/ppermute | solution.py:237

commit v3 on v2

--- a/solution.py
+++ b/solution.py
@@ -11,94 +11,118 @@
 CHANNELS = 1024
 TAPS = 4
 CORR = 12
-VMEM_LIMIT = 32 << 20
-NT = (((1,), (1,)), ((), ()))
+VMEM_LIMIT = 16 << 20
 
 
 def make_basis(bands, length):
-    index = np.arange(length, dtype=np.int64)
+    half = length // 2
+    index = np.arange(half, dtype=np.int64)
     m = (np.arange(CHANNELS, dtype=np.int64)[:, None] * index[None, :]) % length
     phases = np.float32(2.0 * np.pi / length) * m.astype(np.float32)
     stacked = np.stack([np.cos(phases), -np.sin(phases)], axis=0)
-    stacked = stacked.reshape(2, bands, CHANNELS // bands, length).transpose(1, 0, 2, 3)
-    return stacked.reshape(2 * CHANNELS, length).astype(jnp.bfloat16)
-
-
-def spectra_kernel(group, span, start_ref, volt_ref, before_ref, taper_ref, basis_ref, *refs):
-    out_ref, filt = refs[-2:]
+    stacked = stacked.reshape(2, bands, CHANNELS // bands // 2, 2, half)
+    stacked = stacked.transpose(3, 1, 0, 2, 4).reshape(2, CHANNELS, half)
+    return stacked.astype(jnp.bfloat16)
+
+
+def spectra_kernel(group, span, start_ref, volt_ref, taper_ref, basis_ref, *refs):
+    out_ref, folded = refs[-2:]
+    before_ref, later_ref = refs[:2] if len(refs) == 4 else (None, None)
     sig_dev = volt_ref.shape[0]
     length = taper_ref.shape[1]
+    half = length // 2
     bands = out_ref.shape[0]
-    ch_band = basis_ref.shape[0] // (2 * bands)
-    held = group * 2 * ch_band
-
-    def frame(at):
+    columns = sig_dev * len(span)
+    ch_band = basis_ref.shape[1] // bands
+
+    def frame(at, second):
+        first = second * half
         if at < 0:
-            return before_ref[:, (at + TAPS - 1) * length : (at + TAPS) * length]
-        return volt_ref[:, at * length : (at + 1) * length]
-
-    totals = []
+            first = first + (at + TAPS - 1) * length
+            return before_ref[:, first : first + half].astype(jnp.float32)
+        first = first + at * length
+        return volt_ref[:, first : first + half].astype(jnp.float32)
+
+    parts = [[], [], [], []]
     for at in span:
-        total = taper_ref[0:1, :] * frame(at - TAPS + 1).astype(jnp.float32)
-        for tap in range(1, TAPS):
-            total = total + taper_ref[tap : tap + 1, :] * frame(at + tap - TAPS + 1).astype(
-                jnp.float32
+        halves = []
+        for second in range(2):
+            place = slice(second * half, (second + 1) * half)
+            total = taper_ref[0:1, place] * frame(at - TAPS + 1, second)
+            for tap in range(1, TAPS):
+                total = total + taper_ref[tap : tap + 1, place] * frame(at + tap - TAPS + 1, second)
+            halves.append(total.astype(jnp.bfloat16).astype(jnp.float32))
+        for odd, value in enumerate((halves[0] + halves[1], halves[0] - halves[1])):
+            main = value.astype(jnp.bfloat16).astype(jnp.float32)
+            parts[2 * odd].append(main)
+            parts[2 * odd + 1].append(value - main)
+    for odd in range(2):
+        rows = jnp.concatenate(parts[2 * odd] + parts[2 * odd + 1], axis=0)
+        folded[odd] = jnp.transpose(rows).astype(jnp.bfloat16)
+
+    part = 8
+    held = part * ch_band
+    shape = (2 * CORR, 2 * held)
+    row = lax.broadcasted_iota(jnp.int32, shape, 0)
+    column = lax.broadcasted_iota(jnp.int32, shape, 1)
+    imag = column % ch_band // (ch_band // 2)
+    channel = 2 * (column % (ch_band // 2)) + column // held
+    band_at = column % held // ch_band
+    wanted = channel - row % CORR + jnp.where(imag == row // CORR, 0, -2 * CHANNELS)
+
+    def bands_from(at, carry):
+        first = pl.multiple_of(at * group * ch_band, group * ch_band)
+        products = []
+        for odd in range(2):
+            both = jnp.dot(
+                basis_ref[odd, pl.ds(first, group * ch_band), :],
+                folded[odd],
+                preferred_element_type=jnp.float32,
             )
-        totals.append(total)
-    filt[...] = jnp.transpose(jnp.concatenate(totals, axis=0)).astype(jnp.bfloat16)
-
-    part = 8
-    shape = (2 * CORR, part * 2 * ch_band)
-    row = lax.broadcasted_iota(jnp.int32, shape, 0)
-    at_first = lax.broadcasted_iota(jnp.int32, shape, 1) - row
-    at_first = at_first - jnp.where(row < CORR, 0, ch_band - CORR)
-
-    def bands_from(at, carry):
-        first = pl.multiple_of(at * held, held)
-        products = jnp.dot(
-            basis_ref[pl.ds(first, held), :], filt[...], preferred_element_type=jnp.float32
-        ).astype(jnp.bfloat16)
+            products.append((both[:, :columns] + both[:, columns:]).astype(jnp.bfloat16))
         for begin in range(0, group, part):
-            band_at = at * group + begin
             picks = [
-                jnp.where(at_first == band * 2 * ch_band + start_ref[band_at + band], 1.0, 0.0)
+                jnp.where(
+                    (band_at == band) & (wanted == start_ref[at * group + begin + band]), 1.0, 0.0
+                )
                 for band in range(part)
             ]
-            spectra = jnp.dot(
-                jnp.concatenate(picks, axis=0).astype(jnp.bfloat16),
-                products[begin * 2 * ch_band : (begin + part) * 2 * ch_band],
-                preferred_element_type=jnp.float32,
-            )
+            picked = jnp.concatenate(picks, axis=0).astype(jnp.bfloat16)
+            place = slice(begin * ch_band, (begin + part) * ch_band)
+            source = jnp.concatenate([p[place] for p in products], axis=0)
+            spectra = jnp.dot(picked, source, preferred_element_type=jnp.float32)
             for band in range(part):
                 these = spectra[band * 2 * CORR : (band + 1) * 2 * CORR].astype(jnp.bfloat16)
-                if len(refs) == 3:
-                    these = jnp.concatenate([these, refs[0][band_at + band]], axis=1)
-                out_ref[band_at + band] = these
+                if later_ref is not None:
+                    later = later_ref[at * group + begin + band]
+                    these = jnp.concatenate([these, later], axis=1)
+                out_ref[at * group + begin + band] = these
         return carry
 
     lax.fori_loop(0, bands // group, bands_from, 0)
 
 
-def picked_spectra(voltages, before, taper, basis, band_start, bands, span, later=None):
+def picked_spectra(voltages, taper, basis, band_start, span, before=None, later=None):
+    bands = band_start.shape[0]
     sig_dev, samples = voltages.shape
     length = taper.shape[1]
     columns = sig_dev * len(span)
     wide = columns if later is None else columns + later.shape[2]
-    beside = [] if later is None else [later]
+    beside = [] if later is None else [before, later]
     whole = pl.BlockSpec(memory_space=pltpu.VMEM)
     return pl.pallas_call(
         functools.partial(spectra_kernel, 16, span),
-        in_specs=[pl.BlockSpec(memory_space=pltpu.SMEM)] + [whole] * (4 + len(beside)),
+        in_specs=[pl.BlockSpec(memory_space=pltpu.SMEM)] + [whole] * (3 + len(beside)),
         out_specs=whole,
-        scratch_shapes=[pltpu.VMEM((length, columns), jnp.bfloat16)],
+        scratch_shapes=[pltpu.VMEM((2, length // 2, 2 * columns), jnp.bfloat16)],
         out_shape=jax.ShapeDtypeStruct((bands, 2 * CORR, wide), jnp.bfloat16),
         compiler_params=pltpu.CompilerParams(vmem_limit_bytes=VMEM_LIMIT),
         cost_estimate=pl.CostEstimate(
-            flops=2 * 2 * CHANNELS * length * columns,
-            bytes_accessed=2 * 2 * CHANNELS * length + 4 * sig_dev * samples,
+            flops=2 * CHANNELS * length * 2 * columns,
+            bytes_accessed=2 * CHANNELS * length + 4 * sig_dev * samples,
             transcendentals=0,
         ),
-    )(band_start, voltages, before, taper, basis, *beside)
+    )(band_start, voltages, taper, basis, *beside)
 
 
 def order_kernel(turned_ref, input_ref, out_ref, lined):
@@ -228,28 +252,27 @@
     )(position, *blocks, *before)
 
 
-def from_slice(value, dx, dy, slices):
+def from_slice(value, dx, dy):
+    bands, slices = lax.axis_size("band"), lax.axis_size("tslice")
     along = slices // 2
     pairs = []
-    for target in range(slices):
-        source = ((target // 2 + dx) % along) * 2 + (target % 2 + dy) % 2
-        pairs.append((source, target))
-    return lax.ppermute(value, "tslice", pairs)
-
-
-def gather_and_correlate(own, position, slices, row_count, scale):
-    take = functools.partial(from_slice, slices=slices)
-    near = lax.optimization_barrier((take(own, 1, 0), take(own, 0, 1), take(own, -1, 0)))
+    for band in range(bands):
+        way = -dx if band % 2 else dx
+        for target in range(slices):
+            source = ((target // 2 + way) % along) * 2 + (target % 2 + dy) % 2
+            pairs.append((band * slices + source, band * slices + target))
+    return lax.ppermute(value, ("band", "tslice"), pairs)
+
+
+def gather_and_correlate(own, position, row_count, scale):
+    take = from_slice
+    near = (take(own, 1, 0), take(own, 0, 1), take(own, -1, 0))
     right, other, left = near
     summed = correlate(position, [own, right, other, left], row_count)
     right_other, left_other, far = take(right, 0, 1), take(other, -1, 0), take(right, 1, 0)
     left_other, summed = lax.optimization_barrier((left_other, summed))
-    third = own.shape[0] // 3
-    last = [
-        take(right_other[:third], 1, 0),
-        take(left_other[third : 2 * third], -1, 0),
-        take(far[2 * third :], 0, 1),
-    ]
+    cut = own.shape[0] * 2 // 3
+    last = [take(left_other[:cut], -1, 0), take(right_other[cut:], 1, 0)]
     summed = correlate(position, [right_other, left_other, far], row_count, [summed])
     return correlate(position, last, row_count, [summed], scale)
 
@@ -265,15 +288,14 @@
     before = lax.ppermute(tail, "tslice", [(s, s + 1) for s in range(slices - 1)])
     basis = jnp.asarray(make_basis(bands, length))
     half = frames // 2
-    transform = functools.partial(picked_spectra, voltages)
-    rest = (taper, basis, band_start, bands)
-    later = transform(voltages[:8, :128], *rest, tuple(range(half, frames)))
-    spectra = transform(before, *rest, tuple(range(half)), later)
+    transform = functools.partial(picked_spectra, voltages, taper, basis, band_start)
+    later = transform(tuple(range(half, frames)))
+    spectra = transform(tuple(range(half)), before, later)
     turned = lax.all_to_all(spectra, "band", split_axis=0, concat_axis=0, tiled=True)
     own = order_signals(turned, input_of)
     position = position.astype(jnp.int32).reshape(1)
     scale = 1.0 / (CORR * frames * slices)
-    return gather_and_correlate(own, position, slices, signals // slices, scale)
+    return gather_and_correlate(own, position, signals // slices, scale)
 
 
 def solution(mesh):

time: 157 us -> 145 us (0.924)
  the two profiles are of different devices: /device:TPU:32 before, /device:TPU:16 now
where the time goes in v3:
time: 145 us; the launch traced here: 144 us
  blocking collectives  63.2 us (44%)
  starting transfers between devices  35.7 us (25%)
  Pallas kernels  22 us (15%)
  waiting for transfers between devices  17.2 us (12%)
  local copies, waits for them, and re-layouts  5.9 us (4%)
    all_to_all x1, blocking collectives, on_device(): lax.all_to_all(spectra, 'band', split_axis=0, concat_axis=0, tiled=True)  63.2 us
    ppermute x8, starting transfers between devices, from_slice(): return lax.ppermute(value, ('band', 'tslice'), pairs)  32.5 us
    ppermute x8, waiting for transfers between devices, from_slice(): return lax.ppermute(value, ('band', 'tslice'), pairs)  17.2 us
    pallas_call x3, Pallas kernels, correlate(): pl.pallas_call(functools.partial(correlate_kernel, scale, len(blocks), ti...  10.8 us
    pallas_call x2, Pallas kernels, picked_spectra(): pl.pallas_call(functools.partial(spectra_kernel, 16, span), in_specs=[pl....  7.65 us
    unnamed x10, local copies, waits for them, and re-layouts  4.83 us
    pallas_call x1, Pallas kernels, order_signals(): pl.pallas_call(order_kernel, in_specs=[pl.BlockSpec(memory_space=pltpu.VM...  3.56 us
    ppermute x1, starting transfers between devices, on_device(): lax.ppermute(tail, 'tslice', [(s, s + 1) for s in range(slices - 1)])  3.21 us
  transfers between devices with their start and end apart: 9, of which 6 were waited for; matrix products, arithmetic and copies ran while one was open for 0% of the time, Pallas kernels for 8%

profile of v3, /device:TPU:16, one launch (start us, length us, event | category | flops | bytes accessed | tf_op | source)
XLA Modules:
  0.0 144.3 jit_solution(3088844953999652854)
XLA Ops:
  0.0 1.0 slice.9
  1.0 3.2 %collective-permute-start = (bf16[32,6144]{1,0:T(8,128)(2,1)S(1)}, bf16[32,6144]{1,0:T(8,128)(2,1)S(1)}, u32[]{:S(2)}, u32[]{:S(2)}) collective-permute-start(bf16[32,6144]{1,0:T(8,128)(2,1)S(1)} %slice.9), channel_id=1, source_target_pairs={{0,1},{1,2},{2,3},{3,4},{4,5},{5,6},{6,7},{8,9},{9,10},{10,11},{11... | collective-permute-start | bytes 1179656 | tf_op jit(solution)/shard_map/ppermute | solution.py:288
  4.2 0.0 copy-start
  4.3 2.2 %copy-done = bf16[2,1024,1024]{2,1,0:T(8,128)(2,1)S(1)} copy-done((bf16[2,1024,1024]{2,1,0:T(8,128)(2,1)S(1)}, bf16[2,1024,1024]{2,1,0:T(8,128)(2,1)}, u32[]{:S(2)}) %copy-start) | copy-done | bytes 4194328
  6.4 1.2 copy-done.1
  7.7 0.8 copy-done.2
  8.4 0.7 copy-done.3
  9.1 3.8 %shard_map.55.refs_1_ = bf16[64,24,128]{2,1,0:T(8,128)(2,1)S(1)} custom-call(s32[64]{0:T(128)S(1)} %copy-done.3, bf16[32,16384]{1,0:T(8,128)(2,1)S(1)} %copy-done.1, f32[4,2048]{1,0:T(4,128)S(1)} %copy-done.2, bf16[2,1024,1024]{2,1,0:T(8,128)(2,1)S(1)} %copy-done), custom_call_target="tpu_custom_call" | custom-call | flops 1073741824 | bytes 6291456 | tf_op jit(solution)/shard_map/pallas_call | solution.py:113
  12.9 0.0 copy-start.4
  12.9 0.0 collective-permute-done.refs_0_
  12.9 3.8 %shard_map.56 = bf16[64,24,256]{2,1,0:T(8,128)(2,1)S(1)} custom-call(s32[64]{0:T(128)S(1)} %copy-done.3, bf16[32,16384]{1,0:T(8,128)(2,1)S(1)} %copy-done.1, f32[4,2048]{1,0:T(4,128)S(1)} %copy-done.2, bf16[2,1024,1024]{2,1,0:T(8,128)(2,1)S(1)} %copy-done, bf16[32,6144]{1,0:T(8,128)(2,1)S(1)} %collective-permute-done.refs_0_, ...), custom_call_target="tpu_custom_call" | custom-call | flops 1073741824 | bytes 6291456 | tf_op jit(solution)/shard_map/pallas_call | solution.py:113
  16.8 63.2 %all_to_all.5.turned_ref = bf16[64,24,256]{2,1,0:T(8,128)(2,1)S(1)} all-to-all(bf16[64,24,256]{2,1,0:T(8,128)(2,1)S(1)} %shard_map.56), channel_id=1, replica_groups=mesh['band'=64,'tslice'=8] {'band'}, dimensions={0} | all-to-all | bytes 1572864 | tf_op jit(solution)/shard_map/all_to_all | solution.py:294
  80.0 3.6 %shard_map.57.refs_0_ = bf16[192,2048]{1,0:T(8,128)(2,1)S(1)} custom-call(bf16[64,24,256]{2,1,0:T(8,128)(2,1)S(1)} %all_to_all.5.turned_ref, s32[1,2048]{1,0:T(1,128)S(1)} %bitcast.2), custom_call_target="tpu_custom_call" | custom-call | flops 1610612736 | bytes 1572864 | tf_op jit(solution)/shard_map/pallas_call | solution.py:175
  83.6 4.0 %collective-permute-start.1 = (bf16[192,2048]{1,0:T(8,128)(2,1)S(1)}, bf16[192,2048]{1,0:T(8,128)(2,1)}, u32[]{:S(2)}, u32[]{:S(2)}) collective-permute-start(bf16[192,2048]{1,0:T(8,128)(2,1)S(1)} %shard_map.57.refs_0_), channel_id=1, source_target_pairs={{1,0},{0,1},{3,2},{2,3},{5,4},{4,5},{7,6},{6,7},{9,8},{8,9},{11,10... | collective-permute-start | bytes 2359304 | tf_op jit(solution)/shard_map/ppermute | solution.py:264
  87.6 4.7 %collective-permute-start.3 = (bf16[192,2048]{1,0:T(8,128)(2,1)S(1)}, bf16[192,2048]{1,0:T(8,128)(2,1)S(1)}, u32[]{:S(2)}, u32[]{:S(2)}) collective-permute-start(bf16[192,2048]{1,0:T(8,128)(2,1)S(1)} %shard_map.57.refs_0_), channel_id=1, source_target_pairs={{2,0},{3,1},{4,2},{5,3},{6,4},{7,5},{0,6},{1,7},{14,8},{15,9},{8,1... | collective-permute-start | bytes 2359304 | tf_op jit(solution)/shard_map/ppermute | solution.py:264
  92.3 1.9 %collective-permute-start.4 = (bf16[192,2048]{1,0:T(8,128)(2,1)S(1)}, bf16[192,2048]{1,0:T(8,128)(2,1)}, u32[]{:S(2)}, u32[]{:S(2)}) collective-permute-start(bf16[192,2048]{1,0:T(8,128)(2,1)S(1)} %shard_map.57.refs_0_), channel_id=1, source_target_pairs={{6,0},{7,1},{0,2},{1,3},{2,4},{3,5},{4,6},{5,7},{10,8},{11,9},{12,... | collective-permute-start | bytes 2359304 | tf_op jit(solution)/shard_map/ppermute | solution.py:264
  94.2 10.3 %collective-permute-done.1.refs_2_ = bf16[192,2048]{1,0:T(8,128)(2,1)} collective-permute-done((bf16[192,2048]{1,0:T(8,128)(2,1)S(1)}, bf16[192,2048]{1,0:T(8,128)(2,1)}, u32[]{:S(2)}, u32[]{:S(2)}) %collective-permute-start.1) | collective-permute-done | bytes 786464 | tf_op jit(solution)/shard_map/ppermute | solution.py:264
  104.6 4.7 %collective-permute-start.2 = (bf16[192,2048]{1,0:T(8,128)(2,1)}, bf16[192,2048]{1,0:T(8,128)(2,1)S(1)}, u32[]{:S(2)}, u32[]{:S(2)}) collective-permute-start(bf16[192,2048]{1,0:T(8,128)(2,1)} %collective-permute-done.1.refs_2_), channel_id=1, source_target_pairs={{6,0},{7,1},{0,2},{1,3},{2,4},{3,5},{4,6},{5,7},{10,8},{11,9},{12,... | collective-permute-start | bytes 2359304 | tf_op jit(solution)/shard_map/ppermute | solution.py:264
  109.3 0.9 collective-permute-done.3.refs_1_
  110.2 3.5 %collective-permute-start.6 = (bf16[192,2048]{1,0:T(8,128)(2,1)S(1)}, bf16[192,2048]{1,0:T(8,128)(2,1)S(1)}, u32[]{:S(2)}, u32[]{:S(2)}) collective-permute-start(bf16[192,2048]{1,0:T(8,128)(2,1)S(1)} %collective-permute-done.3.refs_1_), channel_id=1, source_target_pairs={{1,0},{0,1},{3,2},{2,3},{5,4},{4,5},{7,6},{6,7},{9,8},{8,9},{11,10... | collective-permute-start | bytes 2359304 | tf_op jit(solution)/shard_map/ppermute | solution.py:264
  113.7 5.6 %collective-permute-start.8 = (bf16[192,2048]{1,0:T(8,128)(2,1)S(1)}, bf16[192,2048]{1,0:T(8,128)(2,1)}, u32[]{:S(2)}, u32[]{:S(2)}) collective-permute-start(bf16[192,2048]{1,0:T(8,128)(2,1)S(1)} %collective-permute-done.3.refs_1_), channel_id=1, source_target_pairs={{2,0},{3,1},{4,2},{5,3},{6,4},{7,5},{0,6},{1,7},{14,8},{15,9},{8,1... | collective-permute-start | bytes 2359304 | tf_op jit(solution)/shard_map/ppermute | solution.py:264
  119.4 0.0 collective-permute-done.4.refs_3_
  119.4 4.1 %shard_map.58.refs_3_ = f32[512,2048]{1,0:T(8,128)S(1)} custom-call(s32[1]{0:T(128)} %bitcast.position_ref, bf16[192,2048]{1,0:T(8,128)(2,1)S(1)} %shard_map.57.refs_0_, bf16[192,2048]{1,0:T(8,128)(2,1)S(1)} %collective-permute-done.3.refs_1_, bf16[192,2048]{1,0:T(8,128)(2,1)} %collective-permute-done.1.refs_2_, bf16[192,2048]{1,0:T(8,128)(2,1)} %collective-permute-done.4.refs_3_), custom_call_target="tpu_custom_call" | custom-call | flops 1610612736 | bytes 7340032 | tf_op jit(solution)/shard_map/pallas_call | solution.py:236
  123.5 1.7 %collective-permute-done.2.refs_1_ = bf16[192,2048]{1,0:T(8,128)(2,1)S(1)} collective-permute-done((bf16[192,2048]{1,0:T(8,128)(2,1)}, bf16[192,2048]{1,0:T(8,128)(2,1)S(1)}, u32[]{:S(2)}, u32[]{:S(2)}) %collective-permute-start.2) | collective-permute-done | bytes 786464 | tf_op jit(solution)/shard_map/ppermute | solution.py:264
  125.2 4.5 %collective-permute-start.5 = (bf16[128,2048]{1,0:T(8,128)(2,1)S(1)}, bf16[128,2048]{1,0:T(8,128)(2,1)S(1)}, u32[]{:S(2)}, u32[]{:S(2)}) collective-permute-start(bf16[128,2048]{1,0:T(8,128)(2,1)S(1)} %slice.10), channel_id=1, source_target_pairs={{6,0},{7,1},{0,2},{1,3},{2,4},{3,5},{4,6},{5,7},{10,8},{11,9},{12,... | collective-permute-start | bytes 1572872 | tf_op jit(solution)/shard_map/ppermute | solution.py:264
  129.7 0.2 collective-permute-done.6.refs_0_
  129.9 3.6 %collective-permute-start.7 = (bf16[64,2048]{1,0:T(8,128)(2,1)S(1)}, bf16[64,2048]{1,0:T(8,128)(2,1)S(1)}, u32[]{:S(2)}, u32[]{:S(2)}) collective-permute-start(bf16[64,2048]{1,0:T(8,128)(2,1)S(1)} %slice.12), channel_id=1, source_target_pairs={{2,0},{3,1},{4,2},{5,3},{6,4},{7,5},{0,6},{1,7},{14,8},{15,9},{8,1... | collective-permute-start | bytes 786440 | tf_op jit(solution)/shard_map/ppermute | solution.py:264
  133.5 0.0 collective-permute-done.8.refs_2_
  133.5 3.9 %shard_map.59.refs_2_ = f32[512,2048]{1,0:T(8,128)S(1)} custom-call(s32[1]{0:T(128)} %bitcast.position_ref, bf16[192,2048]{1,0:T(8,128)(2,1)S(1)} %collective-permute-done.6.refs_0_, bf16[192,2048]{1,0:T(8,128)(2,1)S(1)} %collective-permute-done.2.refs_1_, bf16[192,2048]{1,0:T(8,128)(2,1)} %collective-permute-done.8.refs_2_, f32[512,2048]{1,0:T(8,128)S(1)} %shard_map.58.refs_3_), custom_call_target="tpu_custom_call" | custom-call | flops 1207959552 | bytes 6553600 | tf_op jit(solution)/shard_map/pallas_call | solution.py:236
  137.4 1.0 collective-permute-done.7.refs_1_
  138.4 3.1 %collective-permute-done.5.refs_0_ = bf16[128,2048]{1,0:T(8,128)(2,1)S(1)} collective-permute-done((bf16[128,2048]{1,0:T(8,128)(2,1)S(1)}, bf16[128,2048]{1,0:T(8,128)(2,1)S(1)}, u32[]{:S(2)}, u32[]{:S(2)}) %collective-permute-start.5) | collective-permute-done | bytes 524320 | tf_op jit(solution)/shard_map/ppermute | solution.py:264
  141.5 2.8 %shard_map.60 = bf16[1,2,256,2048]{3,2,1,0:T(8,128)(2,1)} custom-call(s32[1]{0:T(128)} %bitcast.position_ref, bf16[128,2048]{1,0:T(8,128)(2,1)S(1)} %collective-permute-done.5.refs_0_, bf16[64,2048]{1,0:T(8,128)(2,1)S(1)} %collective-permute-done.7.refs_1_, f32[512,2048]{1,0:T(8,128)S(1)} %shard_map.59.refs_2_), custom_call_target="tpu_custom_call" | custom-call | flops 402653184 | bytes 4980736 | tf_op jit(solution)/shard_map/pallas_call | solution.py:236
  (6 shorter events, 0.1 us)
Async XLA Ops:
  1.0 11.9 %collective-permute-start = (bf16[32,6144]{1,0:T(8,128)(2,1)S(1)}, bf16[32,6144]{1,0:T(8,128)(2,1)S(1)}, u32[]{:S(2)}, u32[]{:S(2)}) collective-permute-start(bf16[32,6144]{1,0:T(8,128)(2,1)S(1)} %slice.9), channel_id=1, source_target_pairs={{0,1},{1,2},{2,3},{3,4},{4,5},{5,6},{6,7},{8,9},{9,10},{10,11},{11... | collective-permute-start | bytes 1179656 | tf_op jit(solution)/shard_map/ppermute | solution.py:288
  4.2 2.2 %copy-start = (bf16[2,1024,1024]{2,1,0:T(8,128)(2,1)S(1)}, bf16[2,1024,1024]{2,1,0:T(8,128)(2,1)}, u32[]{:S(2)}) copy-start(bf16[2,1024,1024]{2,1,0:T(8,128)(2,1)} %constant.6.clone.basis_ref) | copy-start | bytes 12582916
  6.4 1.2 copy-start.1
  7.7 0.8 copy-start.2
  8.4 0.7 copy-start.3
  12.9 67.1 %copy-start.4 = (s32[2048]{0:T(1024)S(1)}, s32[2048]{0:T(1024)}, u32[]{:S(2)}) copy-start(s32[2048]{0:T(1024)} %param.7) | copy-start | bytes 24580
  83.6 21.0 %collective-permute-start.1 = (bf16[192,2048]{1,0:T(8,128)(2,1)S(1)}, bf16[192,2048]{1,0:T(8,128)(2,1)}, u32[]{:S(2)}, u32[]{:S(2)}) collective-permute-start(bf16[192,2048]{1,0:T(8,128)(2,1)S(1)} %shard_map.57.refs_0_), channel_id=1, source_target_pairs={{1,0},{0,1},{3,2},{2,3},{5,4},{4,5},{7,6},{6,7},{9,8},{8,9},{11,10... | collective-permute-start | bytes 2359304 | tf_op jit(solution)/shard_map/ppermute | solution.py:264
  87.6 22.6 %collective-permute-start.3 = (bf16[192,2048]{1,0:T(8,128)(2,1)S(1)}, bf16[192,2048]{1,0:T(8,128)(2,1)S(1)}, u32[]{:S(2)}, u32[]{:S(2)}) collective-permute-start(bf16[192,2048]{1,0:T(8,128)(2,1)S(1)} %shard_map.57.refs_0_), channel_id=1, source_target_pairs={{2,0},{3,1},{4,2},{5,3},{6,4},{7,5},{0,6},{1,7},{14,8},{15,9},{8,1... | collective-permute-start | bytes 2359304 | tf_op jit(solution)/shard_map/ppermute | solution.py:264
  92.3 27.1 %collective-permute-start.4 = (bf16[192,2048]{1,0:T(8,128)(2,1)S(1)}, bf16[192,2048]{1,0:T(8,128)(2,1)}, u32[]{:S(2)}, u32[]{:S(2)}) collective-permute-start(bf16[192,2048]{1,0:T(8,128)(2,1)S(1)} %shard_map.57.refs_0_), channel_id=1, source_target_pairs={{6,0},{7,1},{0,2},{1,3},{2,4},{3,5},{4,6},{5,7},{10,8},{11,9},{12,... | collective-permute-start | bytes 2359304 | tf_op jit(solution)/shard_map/ppermute | solution.py:264
  104.6 20.6 %collective-permute-start.2 = (bf16[192,2048]{1,0:T(8,128)(2,1)}, bf16[192,2048]{1,0:T(8,128)(2,1)S(1)}, u32[]{:S(2)}, u32[]{:S(2)}) collective-permute-start(bf16[192,2048]{1,0:T(8,128)(2,1)} %collective-permute-done.1.refs_2_), channel_id=1, source_target_pairs={{6,0},{7,1},{0,2},{1,3},{2,4},{3,5},{4,6},{5,7},{10,8},{11,9},{12,... | collective-permute-start | bytes 2359304 | tf_op jit(solution)/shard_map/ppermute | solution.py:264
  110.2 19.7 %collective-permute-start.6 = (bf16[192,2048]{1,0:T(8,128)(2,1)S(1)}, bf16[192,2048]{1,0:T(8,128)(2,1)S(1)}, u32[]{:S(2)}, u32[]{:S(2)}) collective-permute-start(bf16[192,2048]{1,0:T(8,128)(2,1)S(1)} %collective-permute-done.3.refs_1_), channel_id=1, source_target_pairs={{1,0},{0,1},{3,2},{2,3},{5,4},{4,5},{7,6},{6,7},{9,8},{8,9},{11,10... | collective-permute-start | bytes 2359304 | tf_op jit(solution)/shard_map/ppermute | solution.py:264
  113.7 19.7 %collective-permute-start.8 = (bf16[192,2048]{1,0:T(8,128)(2,1)S(1)}, bf16[192,2048]{1,0:T(8,128)(2,1)}, u32[]{:S(2)}, u32[]{:S(2)}) collective-permute-start(bf16[192,2048]{1,0:T(8,128)(2,1)S(1)} %collective-permute-done.3.refs_1_), channel_id=1, source_target_pairs={{2,0},{3,1},{4,2},{5,3},{6,4},{7,5},{0,6},{1,7},{14,8},{15,9},{8,1... | collective-permute-start | bytes 2359304 | tf_op jit(solution)/shard_map/ppermute | solution.py:264
  125.2 16.2 %collective-permute-start.5 = (bf16[128,2048]{1,0:T(8,128)(2,1)S(1)}, bf16[128,2048]{1,0:T(8,128)(2,1)S(1)}, u32[]{:S(2)}, u32[]{:S(2)}) collective-permute-start(bf16[128,2048]{1,0:T(8,128)(2,1)S(1)} %slice.10), channel_id=1, source_target_pairs={{6,0},{7,1},{0,2},{1,3},{2,4},{3,5},{4,6},{5,7},{10,8},{11,9},{12,... | collective-permute-start | bytes 1572872 | tf_op jit(solution)/shard_map/ppermute | solution.py:264
  129.9 8.5 %collective-permute-start.7 = (bf16[64,2048]{1,0:T(8,128)(2,1)S(1)}, bf16[64,2048]{1,0:T(8,128)(2,1)S(1)}, u32[]{:S(2)}, u32[]{:S(2)}) collective-permute-start(bf16[64,2048]{1,0:T(8,128)(2,1)S(1)} %slice.12), channel_id=1, source_target_pairs={{2,0},{3,1},{4,2},{5,3},{6,4},{7,5},{0,6},{1,7},{14,8},{15,9},{8,1... | collective-permute-start | bytes 786440 | tf_op jit(solution)/shard_map/ppermute | solution.py:264

commit v4 on v3

--- a/solution.py
+++ b/solution.py
@@ -53,12 +53,12 @@
                 total = total + taper_ref[tap : tap + 1, place] * frame(at + tap - TAPS + 1, second)
             halves.append(total.astype(jnp.bfloat16).astype(jnp.float32))
         for odd, value in enumerate((halves[0] + halves[1], halves[0] - halves[1])):
-            main = value.astype(jnp.bfloat16).astype(jnp.float32)
+            main = value.astype(jnp.bfloat16)
             parts[2 * odd].append(main)
-            parts[2 * odd + 1].append(value - main)
+            parts[2 * odd + 1].append((value - main.astype(jnp.float32)).astype(jnp.bfloat16))
     for odd in range(2):
         rows = jnp.concatenate(parts[2 * odd] + parts[2 * odd + 1], axis=0)
-        folded[odd] = jnp.transpose(rows).astype(jnp.bfloat16)
+        folded[odd] = jnp.transpose(rows)
 
     part = 8
     held = part * ch_band
@@ -148,24 +148,19 @@
         return carry
 
     lax.fori_loop(0, bands // per_tile, tile, 0)
-    wanted = jnp.broadcast_to(input_ref[...], (16, signals)).astype(jnp.int16)
-    row = lax.broadcasted_iota(jnp.int32, (16, signals), 0).astype(jnp.int16)
-    one = jnp.ones((16, signals), jnp.bfloat16)
-    zero = jnp.zeros((16, signals), jnp.bfloat16)
-    part = 256
-    total = None
-    for at in range(signals // part):
-        held = jnp.concatenate([lined[2 * at], lined[2 * at + 1]], axis=1).astype(jnp.bfloat16)
+    held = jnp.concatenate([lined[at].astype(jnp.bfloat16) for at in range(signals // 128)], axis=1)
+    part = 512
+    row = lax.broadcasted_iota(jnp.int32, (16, part), 0).astype(jnp.int16)
+    one = jnp.ones((16, part), jnp.bfloat16)
+    zero = jnp.zeros((16, part), jnp.bfloat16)
+    for at in range(0, signals, part):
+        wanted = jnp.broadcast_to(input_ref[:, at : at + part], (16, part)).astype(jnp.int16)
         chosen = jnp.concatenate(
-            [
-                jnp.where(row == wanted - (at * part + first), one, zero)
-                for first in range(0, part, 16)
-            ],
-            axis=0,
+            [jnp.where(row == wanted - first, one, zero) for first in range(0, signals, 16)], axis=0
         )
-        product = jnp.dot(held, chosen, preferred_element_type=jnp.float32)
-        total = product if total is None else total + product
-    out_ref[...] = total.astype(jnp.bfloat16)
+        out_ref[:, at : at + part] = jnp.dot(
+            held, chosen, preferred_element_type=jnp.float32
+        ).astype(jnp.bfloat16)
 
 
 def order_signals(turned, input_of):
@@ -225,7 +220,7 @@
 def correlate(position, blocks, row_count, before=(), scale=None):
     signals = blocks[0].shape[1]
     depth = sum(b.shape[0] for b in blocks)
-    tile = 512
+    tile = 512 if scale is None else 1024
     whole = pl.BlockSpec(memory_space=pltpu.VMEM)
     if scale is None:
         out_spec = whole
@@ -270,9 +265,9 @@
     right, other, left = near
     summed = correlate(position, [own, right, other, left], row_count)
     right_other, left_other, far = take(right, 0, 1), take(other, -1, 0), take(right, 1, 0)
-    left_other, summed = lax.optimization_barrier((left_other, summed))
+    right_other, summed = lax.optimization_barrier((right_other, summed))
     cut = own.shape[0] * 2 // 3
-    last = [take(left_other[:cut], -1, 0), take(right_other[cut:], 1, 0)]
+    last = [take(right_other[:cut], 1, 0), take(far[cut:], 0, 1)]
     summed = correlate(position, [right_other, left_other, far], row_count, [summed])
     return correlate(position, last, row_count, [summed], scale)
 

time: 145 us -> 142 us (0.979)
  starting transfers between devices: 35.7 us -> 28.9 us
  waiting for transfers between devices: 17.2 us -> 21.4 us
    ppermute x8, starting transfers between devices: 32.5 us -> 25.7 us  [from_slice(): return lax.ppermute(value, ('band', 'tslice'), pairs)]
    ppermute x8, waiting for transfers between devices: 17.2 us -> 21.4 us  [from_slice(): return lax.ppermute(value, ('band', 'tslice'), pairs)]
  transfers between devices with their start and end apart: 9 -> 9, of which waited for: 6 -> 4; matrix products, arithmetic and copies ran while one was open for 0% -> 0% of each run, Pallas kernels for 8% -> 8%
where the time goes in v4:
time: 142 us
  blocking collectives  63.2 us (45%)
  starting transfers between devices  28.9 us (20%)
  Pallas kernels  22 us (15%)
  waiting for transfers between devices  21.4 us (15%)
  local copies, waits for them, and re-layouts  5.9 us (4%)
    all_to_all x1, blocking collectives, on_device(): lax.all_to_all(spectra, 'band', split_axis=0, concat_axis=0, tiled=True)  63.2 us
    ppermute x8, starting transfers between devices, from_slice(): return lax.ppermute(value, ('band', 'tslice'), pairs)  25.7 us
    ppermute x8, waiting for transfers between devices, from_slice(): return lax.ppermute(value, ('band', 'tslice'), pairs)  21.4 us
    pallas_call x3, Pallas kernels, correlate(): pl.pallas_call(functools.partial(correlate_kernel, scale, len(blocks), ti...  10.1 us
    pallas_call x2, Pallas kernels, picked_spectra(): pl.pallas_call(functools.partial(spectra_kernel, 16, span), in_specs=[pl....  7.45 us
    unnamed x10, local copies, waits for them, and re-layouts  4.83 us
    pallas_call x1, Pallas kernels, order_signals(): pl.pallas_call(order_kernel, in_specs=[pl.BlockSpec(memory_space=pltpu.VM...  4.45 us
    ppermute x1, starting transfers between devices, on_device(): lax.ppermute(tail, 'tslice', [(s, s + 1) for s in range(slices - 1)])  3.21 us
  transfers between devices with their start and end apart: 9, of which 4 were waited for; matrix products, arithmetic and copies ran while one was open for 0% of the time, Pallas kernels for 8%

profile of v4, /device:TPU:16, one launch (start us, length us, event | category | flops | bytes accessed | tf_op | source)
XLA Modules:
  0.0 141.6 jit_solution(10243894269273029017)
XLA Ops:
  0.0 1.0 slice.9
  1.0 3.2 %collective-permute-start = (bf16[32,6144]{1,0:T(8,128)(2,1)S(1)}, bf16[32,6144]{1,0:T(8,128)(2,1)S(1)}, u32[]{:S(2)}, u32[]{:S(2)}) collective-permute-start(bf16[32,6144]{1,0:T(8,128)(2,1)S(1)} %slice.9), channel_id=1, source_target_pairs={{0,1},{1,2},{2,3},{3,4},{4,5},{5,6},{6,7},{8,9},{9,10},{10,11},{11... | collective-permute-start | bytes 1179656 | tf_op jit(solution)/shard_map/ppermute | solution.py:283
  4.2 0.0 copy-start
  4.3 2.2 %copy-done = bf16[2,1024,1024]{2,1,0:T(8,128)(2,1)S(1)} copy-done((bf16[2,1024,1024]{2,1,0:T(8,128)(2,1)S(1)}, bf16[2,1024,1024]{2,1,0:T(8,128)(2,1)}, u32[]{:S(2)}) %copy-start) | copy-done | bytes 4194328
  6.4 1.2 copy-done.1
  7.7 0.8 copy-done.2
  8.4 0.7 copy-done.3
  9.1 3.7 %shard_map.55.refs_1_ = bf16[64,24,128]{2,1,0:T(8,128)(2,1)S(1)} custom-call(s32[64]{0:T(128)S(1)} %copy-done.3, bf16[32,16384]{1,0:T(8,128)(2,1)S(1)} %copy-done.1, f32[4,2048]{1,0:T(4,128)S(1)} %copy-done.2, bf16[2,1024,1024]{2,1,0:T(8,128)(2,1)S(1)} %copy-done), custom_call_target="tpu_custom_call" | custom-call | flops 1073741824 | bytes 6291456 | tf_op jit(solution)/shard_map/pallas_call | solution.py:113
  12.8 0.0 copy-start.4
  12.8 0.0 collective-permute-done.refs_0_
  12.8 3.7 %shard_map.56 = bf16[64,24,256]{2,1,0:T(8,128)(2,1)S(1)} custom-call(s32[64]{0:T(128)S(1)} %copy-done.3, bf16[32,16384]{1,0:T(8,128)(2,1)S(1)} %copy-done.1, f32[4,2048]{1,0:T(4,128)S(1)} %copy-done.2, bf16[2,1024,1024]{2,1,0:T(8,128)(2,1)S(1)} %copy-done, bf16[32,6144]{1,0:T(8,128)(2,1)S(1)} %collective-permute-done.refs_0_, ...), custom_call_target="tpu_custom_call" | custom-call | flops 1073741824 | bytes 6291456 | tf_op jit(solution)/shard_map/pallas_call | solution.py:113
  16.6 63.2 %all_to_all.5.turned_ref = bf16[64,24,256]{2,1,0:T(8,128)(2,1)S(1)} all-to-all(bf16[64,24,256]{2,1,0:T(8,128)(2,1)S(1)} %shard_map.56), channel_id=1, replica_groups=mesh['band'=64,'tslice'=8] {'band'}, dimensions={0} | all-to-all | bytes 1572864 | tf_op jit(solution)/shard_map/all_to_all | solution.py:289
  79.8 4.4 %shard_map.57.refs_0_ = bf16[192,2048]{1,0:T(8,128)(2,1)} custom-call(bf16[64,24,256]{2,1,0:T(8,128)(2,1)S(1)} %all_to_all.5.turned_ref, s32[1,2048]{1,0:T(1,128)S(1)} %bitcast.2), custom_call_target="tpu_custom_call" | custom-call | flops 1610612736 | bytes 1572864 | tf_op jit(solution)/shard_map/pallas_call | solution.py:170
  84.3 6.5 %collective-permute-start.1 = (bf16[192,2048]{1,0:T(8,128)(2,1)}, bf16[192,2048]{1,0:T(8,128)(2,1)S(1)}, u32[]{:S(2)}, u32[]{:S(2)}) collective-permute-start(bf16[192,2048]{1,0:T(8,128)(2,1)} %shard_map.57.refs_0_), channel_id=1, source_target_pairs={{2,0},{3,1},{4,2},{5,3},{6,4},{7,5},{0,6},{1,7},{14,8},{15,9},{8,1... | collective-permute-start | bytes 2359304 | tf_op jit(solution)/shard_map/ppermute | solution.py:259
  90.8 2.3 %collective-permute-start.3 = (bf16[192,2048]{1,0:T(8,128)(2,1)}, bf16[192,2048]{1,0:T(8,128)(2,1)S(1)}, u32[]{:S(2)}, u32[]{:S(2)}) collective-permute-start(bf16[192,2048]{1,0:T(8,128)(2,1)} %shard_map.57.refs_0_), channel_id=1, source_target_pairs={{1,0},{0,1},{3,2},{2,3},{5,4},{4,5},{7,6},{6,7},{9,8},{8,9},{11,10... | collective-permute-start | bytes 2359304 | tf_op jit(solution)/shard_map/ppermute | solution.py:259
  93.1 1.9 %collective-permute-start.4 = (bf16[192,2048]{1,0:T(8,128)(2,1)}, bf16[192,2048]{1,0:T(8,128)(2,1)}, u32[]{:S(2)}, u32[]{:S(2)}) collective-permute-start(bf16[192,2048]{1,0:T(8,128)(2,1)} %shard_map.57.refs_0_), channel_id=1, source_target_pairs={{6,0},{7,1},{0,2},{1,3},{2,4},{3,5},{4,6},{5,7},{10,8},{11,9},{12,... | collective-permute-start | bytes 2359304 | tf_op jit(solution)/shard_map/ppermute | solution.py:259
  95.0 11.6 %collective-permute-done.1.refs_1_ = bf16[192,2048]{1,0:T(8,128)(2,1)S(1)} collective-permute-done((bf16[192,2048]{1,0:T(8,128)(2,1)}, bf16[192,2048]{1,0:T(8,128)(2,1)S(1)}, u32[]{:S(2)}, u32[]{:S(2)}) %collective-permute-start.1) | collective-permute-done | bytes 786464 | tf_op jit(solution)/shard_map/ppermute | solution.py:259
  106.6 1.9 %collective-permute-start.2 = (bf16[192,2048]{1,0:T(8,128)(2,1)S(1)}, bf16[192,2048]{1,0:T(8,128)(2,1)S(1)}, u32[]{:S(2)}, u32[]{:S(2)}) collective-permute-start(bf16[192,2048]{1,0:T(8,128)(2,1)S(1)} %collective-permute-done.1.refs_1_), channel_id=1, source_target_pairs={{1,0},{0,1},{3,2},{2,3},{5,4},{4,5},{7,6},{6,7},{9,8},{8,9},{11,10... | collective-permute-start | bytes 2359304 | tf_op jit(solution)/shard_map/ppermute | solution.py:259
  108.5 5.5 %collective-permute-start.6 = (bf16[192,2048]{1,0:T(8,128)(2,1)S(1)}, bf16[192,2048]{1,0:T(8,128)(2,1)S(1)}, u32[]{:S(2)}, u32[]{:S(2)}) collective-permute-start(bf16[192,2048]{1,0:T(8,128)(2,1)S(1)} %collective-permute-done.1.refs_1_), channel_id=1, source_target_pairs={{2,0},{3,1},{4,2},{5,3},{6,4},{7,5},{0,6},{1,7},{14,8},{15,9},{8,1... | collective-permute-start | bytes 2359304 | tf_op jit(solution)/shard_map/ppermute | solution.py:259
  114.0 0.0 collective-permute-done.3.refs_2_
  114.0 1.9 %collective-permute-start.8 = (bf16[192,2048]{1,0:T(8,128)(2,1)S(1)}, bf16[192,2048]{1,0:T(8,128)(2,1)}, u32[]{:S(2)}, u32[]{:S(2)}) collective-permute-start(bf16[192,2048]{1,0:T(8,128)(2,1)S(1)} %collective-permute-done.3.refs_2_), channel_id=1, source_target_pairs={{6,0},{7,1},{0,2},{1,3},{2,4},{3,5},{4,6},{5,7},{10,8},{11,9},{12,... | collective-permute-start | bytes 2359304 | tf_op jit(solution)/shard_map/ppermute | solution.py:259
  116.0 0.0 collective-permute-done.4.refs_3_
  116.0 4.1 %shard_map.58.refs_3_ = f32[512,2048]{1,0:T(8,128)S(1)} custom-call(s32[1]{0:T(128)} %bitcast.position_ref, bf16[192,2048]{1,0:T(8,128)(2,1)} %shard_map.57.refs_0_, bf16[192,2048]{1,0:T(8,128)(2,1)S(1)} %collective-permute-done.1.refs_1_, bf16[192,2048]{1,0:T(8,128)(2,1)S(1)} %collective-permute-done.3.refs_2_, bf16[192,2048]{1,0:T(8,128)(2,1)} %collective-permute-done.4.refs_3_), custom_call_target="tpu_custom_call" | custom-call | flops 1610612736 | bytes 7340032 | tf_op jit(solution)/shard_map/pallas_call | solution.py:231
  120.1 6.7 %collective-permute-done.2.refs_0_ = bf16[192,2048]{1,0:T(8,128)(2,1)S(1)} collective-permute-done((bf16[192,2048]{1,0:T(8,128)(2,1)S(1)}, bf16[192,2048]{1,0:T(8,128)(2,1)S(1)}, u32[]{:S(2)}, u32[]{:S(2)}) %collective-permute-start.2) | collective-permute-done | bytes 786464 | tf_op jit(solution)/shard_map/ppermute | solution.py:259
  126.8 3.5 %collective-permute-start.5 = (bf16[128,2048]{1,0:T(8,128)(2,1)S(1)}, bf16[128,2048]{1,0:T(8,128)(2,1)S(1)}, u32[]{:S(2)}, u32[]{:S(2)}) collective-permute-start(bf16[128,2048]{1,0:T(8,128)(2,1)S(1)} %slice.10), channel_id=1, source_target_pairs={{2,0},{3,1},{4,2},{5,3},{6,4},{7,5},{0,6},{1,7},{14,8},{15,9},{8,1... | collective-permute-start | bytes 1572872 | tf_op jit(solution)/shard_map/ppermute | solution.py:259
  130.3 0.3 collective-permute-done.6.refs_2_
  130.6 2.2 %collective-permute-start.7 = (bf16[64,2048]{1,0:T(8,128)(2,1)S(1)}, bf16[64,2048]{1,0:T(8,128)(2,1)S(1)}, u32[]{:S(2)}, u32[]{:S(2)}) collective-permute-start(bf16[64,2048]{1,0:T(8,128)(2,1)S(1)} %slice.12), channel_id=1, source_target_pairs={{1,0},{0,1},{3,2},{2,3},{5,4},{4,5},{7,6},{6,7},{9,8},{8,9},{11,10... | collective-permute-start | bytes 786440 | tf_op jit(solution)/shard_map/ppermute | solution.py:259
  132.8 0.0 collective-permute-done.8.refs_1_
  132.8 3.9 %shard_map.59.refs_2_ = f32[512,2048]{1,0:T(8,128)S(1)} custom-call(s32[1]{0:T(128)} %bitcast.position_ref, bf16[192,2048]{1,0:T(8,128)(2,1)S(1)} %collective-permute-done.2.refs_0_, bf16[192,2048]{1,0:T(8,128)(2,1)} %collective-permute-done.8.refs_1_, bf16[192,2048]{1,0:T(8,128)(2,1)S(1)} %collective-permute-done.6.refs_2_, f32[512,2048]{1,0:T(8,128)S(1)} %shard_map.58.refs_3_), custom_call_target="tpu_custom_call" | custom-call | flops 1207959552 | bytes 6553600 | tf_op jit(solution)/shard_map/pallas_call | solution.py:231
  136.7 2.8 %collective-permute-done.7.refs_1_ = bf16[64,2048]{1,0:T(8,128)(2,1)S(1)} collective-permute-done((bf16[64,2048]{1,0:T(8,128)(2,1)S(1)}, bf16[64,2048]{1,0:T(8,128)(2,1)S(1)}, u32[]{:S(2)}, u32[]{:S(2)}) %collective-permute-start.7) | collective-permute-done | bytes 262176 | tf_op jit(solution)/shard_map/ppermute | solution.py:259
  139.5 0.0 collective-permute-done.5.refs_0_
  139.5 2.1 %shard_map.60 = bf16[1,2,256,2048]{3,2,1,0:T(8,128)(2,1)} custom-call(s32[1]{0:T(128)} %bitcast.position_ref, bf16[128,2048]{1,0:T(8,128)(2,1)S(1)} %collective-permute-done.5.refs_0_, bf16[64,2048]{1,0:T(8,128)(2,1)S(1)} %collective-permute-done.7.refs_1_, f32[512,2048]{1,0:T(8,128)S(1)} %shard_map.59.refs_2_), custom_call_target="tpu_custom_call" | custom-call | flops 402653184 | bytes 4980736 | tf_op jit(solution)/shard_map/pallas_call | solution.py:231
  (6 shorter events, 0.1 us)
Async XLA Ops:
  1.0 11.8 %collective-permute-start = (bf16[32,6144]{1,0:T(8,128)(2,1)S(1)}, bf16[32,6144]{1,0:T(8,128)(2,1)S(1)}, u32[]{:S(2)}, u32[]{:S(2)}) collective-permute-start(bf16[32,6144]{1,0:T(8,128)(2,1)S(1)} %slice.9), channel_id=1, source_target_pairs={{0,1},{1,2},{2,3},{3,4},{4,5},{5,6},{6,7},{8,9},{9,10},{10,11},{11... | collective-permute-start | bytes 1179656 | tf_op jit(solution)/shard_map/ppermute | solution.py:283
  4.2 2.2 %copy-start = (bf16[2,1024,1024]{2,1,0:T(8,128)(2,1)S(1)}, bf16[2,1024,1024]{2,1,0:T(8,128)(2,1)}, u32[]{:S(2)}) copy-start(bf16[2,1024,1024]{2,1,0:T(8,128)(2,1)} %constant.6.clone.basis_ref) | copy-start | bytes 12582916
  6.4 1.2 copy-start.1
  7.7 0.8 copy-start.2
  8.4 0.7 copy-start.3
  12.8 67.0 %copy-start.4 = (s32[2048]{0:T(1024)S(1)}, s32[2048]{0:T(1024)}, u32[]{:S(2)}) copy-start(s32[2048]{0:T(1024)} %param.7) | copy-start | bytes 24580
  84.3 22.3 %collective-permute-start.1 = (bf16[192,2048]{1,0:T(8,128)(2,1)}, bf16[192,2048]{1,0:T(8,128)(2,1)S(1)}, u32[]{:S(2)}, u32[]{:S(2)}) collective-permute-start(bf16[192,2048]{1,0:T(8,128)(2,1)} %shard_map.57.refs_0_), channel_id=1, source_target_pairs={{2,0},{3,1},{4,2},{5,3},{6,4},{7,5},{0,6},{1,7},{14,8},{15,9},{8,1... | collective-permute-start | bytes 2359304 | tf_op jit(solution)/shard_map/ppermute | solution.py:259
  90.8 23.3 %collective-permute-start.3 = (bf16[192,2048]{1,0:T(8,128)(2,1)}, bf16[192,2048]{1,0:T(8,128)(2,1)S(1)}, u32[]{:S(2)}, u32[]{:S(2)}) collective-permute-start(bf16[192,2048]{1,0:T(8,128)(2,1)} %shard_map.57.refs_0_), channel_id=1, source_target_pairs={{1,0},{0,1},{3,2},{2,3},{5,4},{4,5},{7,6},{6,7},{9,8},{8,9},{11,10... | collective-permute-start | bytes 2359304 | tf_op jit(solution)/shard_map/ppermute | solution.py:259
  93.1 22.9 %collective-permute-start.4 = (bf16[192,2048]{1,0:T(8,128)(2,1)}, bf16[192,2048]{1,0:T(8,128)(2,1)}, u32[]{:S(2)}, u32[]{:S(2)}) collective-permute-start(bf16[192,2048]{1,0:T(8,128)(2,1)} %shard_map.57.refs_0_), channel_id=1, source_target_pairs={{6,0},{7,1},{0,2},{1,3},{2,4},{3,5},{4,6},{5,7},{10,8},{11,9},{12,... | collective-permute-start | bytes 2359304 | tf_op jit(solution)/shard_map/ppermute | solution.py:259
  106.6 20.2 %collective-permute-start.2 = (bf16[192,2048]{1,0:T(8,128)(2,1)S(1)}, bf16[192,2048]{1,0:T(8,128)(2,1)S(1)}, u32[]{:S(2)}, u32[]{:S(2)}) collective-permute-start(bf16[192,2048]{1,0:T(8,128)(2,1)S(1)} %collective-permute-done.1.refs_1_), channel_id=1, source_target_pairs={{1,0},{0,1},{3,2},{2,3},{5,4},{4,5},{7,6},{6,7},{9,8},{8,9},{11,10... | collective-permute-start | bytes 2359304 | tf_op jit(solution)/shard_map/ppermute | solution.py:259
  108.5 22.0 %collective-permute-start.6 = (bf16[192,2048]{1,0:T(8,128)(2,1)S(1)}, bf16[192,2048]{1,0:T(8,128)(2,1)S(1)}, u32[]{:S(2)}, u32[]{:S(2)}) collective-permute-start(bf16[192,2048]{1,0:T(8,128)(2,1)S(1)} %collective-permute-done.1.refs_1_), channel_id=1, source_target_pairs={{2,0},{3,1},{4,2},{5,3},{6,4},{7,5},{0,6},{1,7},{14,8},{15,9},{8,1... | collective-permute-start | bytes 2359304 | tf_op jit(solution)/shard_map/ppermute | solution.py:259
  114.0 18.8 %collective-permute-start.8 = (bf16[192,2048]{1,0:T(8,128)(2,1)S(1)}, bf16[192,2048]{1,0:T(8,128)(2,1)}, u32[]{:S(2)}, u32[]{:S(2)}) collective-permute-start(bf16[192,2048]{1,0:T(8,128)(2,1)S(1)} %collective-permute-done.3.refs_2_), channel_id=1, source_target_pairs={{6,0},{7,1},{0,2},{1,3},{2,4},{3,5},{4,6},{5,7},{10,8},{11,9},{12,... | collective-permute-start | bytes 2359304 | tf_op jit(solution)/shard_map/ppermute | solution.py:259
  126.8 12.7 %collective-permute-start.5 = (bf16[128,2048]{1,0:T(8,128)(2,1)S(1)}, bf16[128,2048]{1,0:T(8,128)(2,1)S(1)}, u32[]{:S(2)}, u32[]{:S(2)}) collective-permute-start(bf16[128,2048]{1,0:T(8,128)(2,1)S(1)} %slice.10), channel_id=1, source_target_pairs={{2,0},{3,1},{4,2},{5,3},{6,4},{7,5},{0,6},{1,7},{14,8},{15,9},{8,1... | collective-permute-start | bytes 1572872 | tf_op jit(solution)/shard_map/ppermute | solution.py:259
  130.6 8.9 %collective-permute-start.7 = (bf16[64,2048]{1,0:T(8,128)(2,1)S(1)}, bf16[64,2048]{1,0:T(8,128)(2,1)S(1)}, u32[]{:S(2)}, u32[]{:S(2)}) collective-permute-start(bf16[64,2048]{1,0:T(8,128)(2,1)S(1)} %slice.12), channel_id=1, source_target_pairs={{1,0},{0,1},{3,2},{2,3},{5,4},{4,5},{7,6},{6,7},{9,8},{8,9},{11,10... | collective-permute-start | bytes 786440 | tf_op jit(solution)/shard_map/ppermute | solution.py:259

commit v5 on v4

--- a/solution.py
+++ b/solution.py
@@ -99,7 +99,7 @@
                 out_ref[at * group + begin + band] = these
         return carry
 
-    lax.fori_loop(0, bands // group, bands_from, 0)
+    lax.fori_loop(0, bands // group, bands_from, 0, unroll=True)
 
 
 def picked_spectra(voltages, taper, basis, band_start, span, before=None, later=None):
@@ -147,7 +147,7 @@
             lined[at, frame * values : (frame + 1) * values, :] = merged
         return carry
 
-    lax.fori_loop(0, bands // per_tile, tile, 0)
+    lax.fori_loop(0, bands // per_tile, tile, 0, unroll=True)
     held = jnp.concatenate([lined[at].astype(jnp.bfloat16) for at in range(signals // 128)], axis=1)
     part = 512
     row = lax.broadcasted_iota(jnp.int32, (16, part), 0).astype(jnp.int16)
@@ -220,7 +220,7 @@
 def correlate(position, blocks, row_count, before=(), scale=None):
     signals = blocks[0].shape[1]
     depth = sum(b.shape[0] for b in blocks)
-    tile = 512 if scale is None else 1024
+    tile = 1024
     whole = pl.BlockSpec(memory_space=pltpu.VMEM)
     if scale is None:
         out_spec = whole
@@ -263,10 +263,11 @@
     take = from_slice
     near = (take(own, 1, 0), take(own, 0, 1), take(own, -1, 0))
     right, other, left = near
-    summed = correlate(position, [own, right, other, left], row_count)
+    summed = correlate(position, [own], row_count)
+    summed = correlate(position, [right, other, left], row_count, [summed])
     right_other, left_other, far = take(right, 0, 1), take(other, -1, 0), take(right, 1, 0)
     right_other, summed = lax.optimization_barrier((right_other, summed))
-    cut = own.shape[0] * 2 // 3
+    cut = own.shape[0] * 3 // 4
     last = [take(right_other[:cut], 1, 0), take(far[cut:], 0, 1)]
     summed = correlate(position, [right_other, left_other, far], row_count, [summed])
     return correlate(position, last, row_count, [summed], scale)

time: 142 us -> 138 us (0.972)
  the two profiles are of different devices: /device:TPU:16 before, /device:TPU:22 now
where the time goes in v5:
time: 138 us; the launch traced here: 137 us
  blocking collectives  63.3 us (46%)
  starting transfers between devices  27.4 us (20%)
  waiting for transfers between devices  22 us (16%)
  Pallas kernels  18.7 us (14%)
  local copies, waits for them, and re-layouts  5.9 us (4%)
    all_to_all x1, blocking collectives, on_device(): lax.all_to_all(spectra, 'band', split_axis=0, concat_axis=0, tiled=True)  63.3 us
    ppermute x8, starting transfers between devices, from_slice(): return lax.ppermute(value, ('band', 'tslice'), pairs)  24.2 us
    ppermute x8, waiting for transfers between devices, from_slice(): return lax.ppermute(value, ('band', 'tslice'), pairs)  19.4 us
    pallas_call x4, Pallas kernels, correlate(): pl.pallas_call(functools.partial(correlate_kernel, scale, len(blocks), ti...  10.6 us
    pallas_call x2, Pallas kernels, picked_spectra(): pl.pallas_call(functools.partial(spectra_kernel, 16, span), in_specs=[pl....  5.95 us
    unnamed x10, local copies, waits for them, and re-layouts  4.83 us
    ppermute x1, starting transfers between devices, on_device(): lax.ppermute(tail, 'tslice', [(s, s + 1) for s in range(slices - 1)])  3.19 us
  transfers between devices with their start and end apart: 9, of which 5 were waited for; matrix products, arithmetic and copies ran while one was open for 0% of the time, Pallas kernels for 8%

profile of v5, /device:TPU:22, one launch (start us, length us, event | category | flops | bytes accessed | tf_op | source)
XLA Modules:
  0.0 137.5 jit_solution(2424096559897223636)
XLA Ops:
  0.0 1.0 slice.9
  1.0 3.2 %collective-permute-start = (bf16[32,6144]{1,0:T(8,128)(2,1)S(1)}, bf16[32,6144]{1,0:T(8,128)(2,1)S(1)}, u32[]{:S(2)}, u32[]{:S(2)}) collective-permute-start(bf16[32,6144]{1,0:T(8,128)(2,1)S(1)} %slice.9), channel_id=1, source_target_pairs={{0,1},{1,2},{2,3},{3,4},{4,5},{5,6},{6,7},{8,9},{9,10},{10,11},{11... | collective-permute-start | bytes 1179656 | tf_op jit(solution)/shard_map/ppermute | solution.py:284
  4.2 0.0 copy-start
  4.2 2.2 %copy-done = bf16[2,1024,1024]{2,1,0:T(8,128)(2,1)S(1)} copy-done((bf16[2,1024,1024]{2,1,0:T(8,128)(2,1)S(1)}, bf16[2,1024,1024]{2,1,0:T(8,128)(2,1)}, u32[]{:S(2)}) %copy-start) | copy-done | bytes 4194328
  6.4 1.2 copy-done.1
  7.6 0.8 copy-done.2
  8.4 0.7 copy-done.3
  9.1 3.0 %shard_map.55.refs_1_ = bf16[64,24,128]{2,1,0:T(8,128)(2,1)S(1)} custom-call(s32[64]{0:T(128)S(1)} %copy-done.3, bf16[32,16384]{1,0:T(8,128)(2,1)S(1)} %copy-done.1, f32[4,2048]{1,0:T(4,128)S(1)} %copy-done.2, bf16[2,1024,1024]{2,1,0:T(8,128)(2,1)S(1)} %copy-done), custom_call_target="tpu_custom_call" | custom-call | flops 1073741824 | bytes 6291456 | tf_op jit(solution)/shard_map/pallas_call | solution.py:113
  12.0 0.0 copy-start.4
  12.0 2.6 %collective-permute-done.refs_0_ = bf16[32,6144]{1,0:T(8,128)(2,1)S(1)} collective-permute-done((bf16[32,6144]{1,0:T(8,128)(2,1)S(1)}, bf16[32,6144]{1,0:T(8,128)(2,1)S(1)}, u32[]{:S(2)}, u32[]{:S(2)}) %collective-permute-start) | collective-permute-done | bytes 393248 | tf_op jit(solution)/shard_map/ppermute | solution.py:284
  14.7 3.0 %shard_map.56 = bf16[64,24,256]{2,1,0:T(8,128)(2,1)S(1)} custom-call(s32[64]{0:T(128)S(1)} %copy-done.3, bf16[32,16384]{1,0:T(8,128)(2,1)S(1)} %copy-done.1, f32[4,2048]{1,0:T(4,128)S(1)} %copy-done.2, bf16[2,1024,1024]{2,1,0:T(8,128)(2,1)S(1)} %copy-done, bf16[32,6144]{1,0:T(8,128)(2,1)S(1)} %collective-permute-done.refs_0_, ...), custom_call_target="tpu_custom_call" | custom-call | flops 1073741824 | bytes 6291456 | tf_op jit(solution)/shard_map/pallas_call | solution.py:113
  17.7 63.3 %all_to_all.5.turned_ref = bf16[64,24,256]{2,1,0:T(8,128)(2,1)S(1)} all-to-all(bf16[64,24,256]{2,1,0:T(8,128)(2,1)S(1)} %shard_map.56), channel_id=1, replica_groups=mesh['band'=64,'tslice'=8] {'band'}, dimensions={0} | all-to-all | bytes 1572864 | tf_op jit(solution)/shard_map/all_to_all | solution.py:290
  80.9 2.1 %shard_map.57.refs_0_ = bf16[192,2048]{1,0:T(8,128)(2,1)S(1)} custom-call(bf16[64,24,256]{2,1,0:T(8,128)(2,1)S(1)} %all_to_all.5.turned_ref, s32[1,2048]{1,0:T(1,128)S(1)} %bitcast.2), custom_call_target="tpu_custom_call" | custom-call | flops 1610612736 | bytes 1572864 | tf_op jit(solution)/shard_map/pallas_call | solution.py:170
  83.0 2.7 %collective-permute-start.1 = (bf16[192,2048]{1,0:T(8,128)(2,1)S(1)}, bf16[192,2048]{1,0:T(8,128)(2,1)}, u32[]{:S(2)}, u32[]{:S(2)}) collective-permute-start(bf16[192,2048]{1,0:T(8,128)(2,1)S(1)} %shard_map.57.refs_0_), channel_id=1, source_target_pairs={{2,0},{3,1},{4,2},{5,3},{6,4},{7,5},{0,6},{1,7},{14,8},{15,9},{8,1... | collective-permute-start | bytes 2359304 | tf_op jit(solution)/shard_map/ppermute | solution.py:259
  85.8 2.3 %collective-permute-start.3 = (bf16[192,2048]{1,0:T(8,128)(2,1)S(1)}, bf16[192,2048]{1,0:T(8,128)(2,1)S(1)}, u32[]{:S(2)}, u32[]{:S(2)}) collective-permute-start(bf16[192,2048]{1,0:T(8,128)(2,1)S(1)} %shard_map.57.refs_0_), channel_id=1, source_target_pairs={{1,0},{0,1},{3,2},{2,3},{5,4},{4,5},{7,6},{6,7},{9,8},{8,9},{11,10... | collective-permute-start | bytes 2359304 | tf_op jit(solution)/shard_map/ppermute | solution.py:259
  88.0 4.3 %collective-permute-start.4 = (bf16[192,2048]{1,0:T(8,128)(2,1)S(1)}, bf16[192,2048]{1,0:T(8,128)(2,1)}, u32[]{:S(2)}, u32[]{:S(2)}) collective-permute-start(bf16[192,2048]{1,0:T(8,128)(2,1)S(1)} %shard_map.57.refs_0_), channel_id=1, source_target_pairs={{6,0},{7,1},{0,2},{1,3},{2,4},{3,5},{4,6},{5,7},{10,8},{11,9},{12,... | collective-permute-start | bytes 2359304 | tf_op jit(solution)/shard_map/ppermute | solution.py:259
  92.4 11.9 %collective-permute-done.1.refs_0_ = bf16[192,2048]{1,0:T(8,128)(2,1)} collective-permute-done((bf16[192,2048]{1,0:T(8,128)(2,1)S(1)}, bf16[192,2048]{1,0:T(8,128)(2,1)}, u32[]{:S(2)}, u32[]{:S(2)}) %collective-permute-start.1) | collective-permute-done | bytes 786464 | tf_op jit(solution)/shard_map/ppermute | solution.py:259
  104.3 1.9 %collective-permute-start.2 = (bf16[192,2048]{1,0:T(8,128)(2,1)}, bf16[192,2048]{1,0:T(8,128)(2,1)S(1)}, u32[]{:S(2)}, u32[]{:S(2)}) collective-permute-start(bf16[192,2048]{1,0:T(8,128)(2,1)} %collective-permute-done.1.refs_0_), channel_id=1, source_target_pairs={{1,0},{0,1},{3,2},{2,3},{5,4},{4,5},{7,6},{6,7},{9,8},{8,9},{11,10... | collective-permute-start | bytes 2359304 | tf_op jit(solution)/shard_map/ppermute | solution.py:259
  106.2 1.9 %collective-permute-start.6 = (bf16[192,2048]{1,0:T(8,128)(2,1)}, bf16[192,2048]{1,0:T(8,128)(2,1)S(1)}, u32[]{:S(2)}, u32[]{:S(2)}) collective-permute-start(bf16[192,2048]{1,0:T(8,128)(2,1)} %collective-permute-done.1.refs_0_), channel_id=1, source_target_pairs={{2,0},{3,1},{4,2},{5,3},{6,4},{7,5},{0,6},{1,7},{14,8},{15,9},{8,1... | collective-permute-start | bytes 2359304 | tf_op jit(solution)/shard_map/ppermute | solution.py:259
  108.1 0.0 collective-permute-done.3.refs_1_
  108.1 5.1 %collective-permute-start.8 = (bf16[192,2048]{1,0:T(8,128)(2,1)S(1)}, bf16[192,2048]{1,0:T(8,128)(2,1)}, u32[]{:S(2)}, u32[]{:S(2)}) collective-permute-start(bf16[192,2048]{1,0:T(8,128)(2,1)S(1)} %collective-permute-done.3.refs_1_), channel_id=1, source_target_pairs={{6,0},{7,1},{0,2},{1,3},{2,4},{3,5},{4,6},{5,7},{10,8},{11,9},{12,... | collective-permute-start | bytes 2359304 | tf_op jit(solution)/shard_map/ppermute | solution.py:259
  113.3 1.2 shard_map.58.refs_3_
  114.5 0.0 collective-permute-done.4.refs_2_
  114.5 3.8 %shard_map.59.refs_3_ = f32[512,2048]{1,0:T(8,128)S(1)} custom-call(s32[1]{0:T(128)} %bitcast.position_ref, bf16[192,2048]{1,0:T(8,128)(2,1)} %collective-permute-done.1.refs_0_, bf16[192,2048]{1,0:T(8,128)(2,1)S(1)} %collective-permute-done.3.refs_1_, bf16[192,2048]{1,0:T(8,128)(2,1)} %collective-permute-done.4.refs_2_, f32[512,2048]{1,0:T(8,128)S(1)} %shard_map.58.refs_3_), custom_call_target="tpu_custom_call" | custom-call | flops 1207959552 | bytes 6553600 | tf_op jit(solution)/shard_map/pallas_call | solution.py:231
  118.3 4.0 %collective-permute-done.2.refs_0_ = bf16[192,2048]{1,0:T(8,128)(2,1)S(1)} collective-permute-done((bf16[192,2048]{1,0:T(8,128)(2,1)}, bf16[192,2048]{1,0:T(8,128)(2,1)S(1)}, u32[]{:S(2)}, u32[]{:S(2)}) %collective-permute-start.2) | collective-permute-done | bytes 786464 | tf_op jit(solution)/shard_map/ppermute | solution.py:259
  122.3 3.6 %collective-permute-start.5 = (bf16[144,2048]{1,0:T(8,128)(2,1)S(1)}, bf16[144,2048]{1,0:T(8,128)(2,1)S(1)}, u32[]{:S(2)}, u32[]{:S(2)}) collective-permute-start(bf16[144,2048]{1,0:T(8,128)(2,1)S(1)} %slice.10), channel_id=1, source_target_pairs={{2,0},{3,1},{4,2},{5,3},{6,4},{7,5},{0,6},{1,7},{14,8},{15,9},{8,1... | collective-permute-start | bytes 1769480 | tf_op jit(solution)/shard_map/ppermute | solution.py:259
  126.0 0.0 collective-permute-done.6.refs_2_
  126.0 2.3 %collective-permute-start.7 = (bf16[48,2048]{1,0:T(8,128)(2,1)S(1)}, bf16[48,2048]{1,0:T(8,128)(2,1)S(1)}, u32[]{:S(2)}, u32[]{:S(2)}) collective-permute-start(bf16[48,2048]{1,0:T(8,128)(2,1)S(1)} %slice.12), channel_id=1, source_target_pairs={{1,0},{0,1},{3,2},{2,3},{5,4},{4,5},{7,6},{6,7},{9,8},{8,9},{11,10... | collective-permute-start | bytes 589832 | tf_op jit(solution)/shard_map/ppermute | solution.py:259
  128.3 3.5 %shard_map.60.refs_2_ = f32[512,2048]{1,0:T(8,128)S(1)} custom-call(s32[1]{0:T(128)} %bitcast.position_ref, bf16[192,2048]{1,0:T(8,128)(2,1)S(1)} %collective-permute-done.2.refs_0_, bf16[192,2048]{1,0:T(8,128)(2,1)} %collective-permute-done.8.refs_1_, bf16[192,2048]{1,0:T(8,128)(2,1)S(1)} %collective-permute-done.6.refs_2_, f32[512,2048]{1,0:T(8,128)S(1)} %shard_map.59.refs_3_), custom_call_target="tpu_custom_call" | custom-call | flops 1207959552 | bytes 6553600 | tf_op jit(solution)/shard_map/pallas_call | solution.py:231
  131.9 1.7 %collective-permute-done.7.refs_1_ = bf16[48,2048]{1,0:T(8,128)(2,1)S(1)} collective-permute-done((bf16[48,2048]{1,0:T(8,128)(2,1)S(1)}, bf16[48,2048]{1,0:T(8,128)(2,1)S(1)}, u32[]{:S(2)}, u32[]{:S(2)}) %collective-permute-start.7) | collective-permute-done | bytes 196640 | tf_op jit(solution)/shard_map/ppermute | solution.py:259
  133.6 1.7 %collective-permute-done.5.refs_0_ = bf16[144,2048]{1,0:T(8,128)(2,1)S(1)} collective-permute-done((bf16[144,2048]{1,0:T(8,128)(2,1)S(1)}, bf16[144,2048]{1,0:T(8,128)(2,1)S(1)}, u32[]{:S(2)}, u32[]{:S(2)}) %collective-permute-start.5) | collective-permute-done | bytes 589856 | tf_op jit(solution)/shard_map/ppermute | solution.py:259
  135.3 2.1 %shard_map.61 = bf16[1,2,256,2048]{3,2,1,0:T(8,128)(2,1)} custom-call(s32[1]{0:T(128)} %bitcast.position_ref, bf16[144,2048]{1,0:T(8,128)(2,1)S(1)} %collective-permute-done.5.refs_0_, bf16[48,2048]{1,0:T(8,128)(2,1)S(1)} %collective-permute-done.7.refs_1_, f32[512,2048]{1,0:T(8,128)S(1)} %shard_map.60.refs_2_), custom_call_target="tpu_custom_call" | custom-call | flops 402653184 | bytes 4980736 | tf_op jit(solution)/shard_map/pallas_call | solution.py:231
  (7 shorter events, 0.1 us)
Async XLA Ops:
  1.0 13.6 %collective-permute-start = (bf16[32,6144]{1,0:T(8,128)(2,1)S(1)}, bf16[32,6144]{1,0:T(8,128)(2,1)S(1)}, u32[]{:S(2)}, u32[]{:S(2)}) collective-permute-start(bf16[32,6144]{1,0:T(8,128)(2,1)S(1)} %slice.9), channel_id=1, source_target_pairs={{0,1},{1,2},{2,3},{3,4},{4,5},{5,6},{6,7},{8,9},{9,10},{10,11},{11... | collective-permute-start | bytes 1179656 | tf_op jit(solution)/shard_map/ppermute | solution.py:284
  4.2 2.2 %copy-start = (bf16[2,1024,1024]{2,1,0:T(8,128)(2,1)S(1)}, bf16[2,1024,1024]{2,1,0:T(8,128)(2,1)}, u32[]{:S(2)}) copy-start(bf16[2,1024,1024]{2,1,0:T(8,128)(2,1)} %constant.6.clone.basis_ref) | copy-start | bytes 12582916
  6.4 1.2 copy-start.1
  7.6 0.8 copy-start.2
  8.4 0.7 copy-start.3
  12.0 68.9 %copy-start.4 = (s32[2048]{0:T(1024)S(1)}, s32[2048]{0:T(1024)}, u32[]{:S(2)}) copy-start(s32[2048]{0:T(1024)} %param.7) | copy-start | bytes 24580
  83.0 21.3 %collective-permute-start.1 = (bf16[192,2048]{1,0:T(8,128)(2,1)S(1)}, bf16[192,2048]{1,0:T(8,128)(2,1)}, u32[]{:S(2)}, u32[]{:S(2)}) collective-permute-start(bf16[192,2048]{1,0:T(8,128)(2,1)S(1)} %shard_map.57.refs_0_), channel_id=1, source_target_pairs={{2,0},{3,1},{4,2},{5,3},{6,4},{7,5},{0,6},{1,7},{14,8},{15,9},{8,1... | collective-permute-start | bytes 2359304 | tf_op jit(solution)/shard_map/ppermute | solution.py:259
  85.8 22.4 %collective-permute-start.3 = (bf16[192,2048]{1,0:T(8,128)(2,1)S(1)}, bf16[192,2048]{1,0:T(8,128)(2,1)S(1)}, u32[]{:S(2)}, u32[]{:S(2)}) collective-permute-start(bf16[192,2048]{1,0:T(8,128)(2,1)S(1)} %shard_map.57.refs_0_), channel_id=1, source_target_pairs={{1,0},{0,1},{3,2},{2,3},{5,4},{4,5},{7,6},{6,7},{9,8},{8,9},{11,10... | collective-permute-start | bytes 2359304 | tf_op jit(solution)/shard_map/ppermute | solution.py:259
  88.0 26.4 %collective-permute-start.4 = (bf16[192,2048]{1,0:T(8,128)(2,1)S(1)}, bf16[192,2048]{1,0:T(8,128)(2,1)}, u32[]{:S(2)}, u32[]{:S(2)}) collective-permute-start(bf16[192,2048]{1,0:T(8,128)(2,1)S(1)} %shard_map.57.refs_0_), channel_id=1, source_target_pairs={{6,0},{7,1},{0,2},{1,3},{2,4},{3,5},{4,6},{5,7},{10,8},{11,9},{12,... | collective-permute-start | bytes 2359304 | tf_op jit(solution)/shard_map/ppermute | solution.py:259
  104.3 18.0 %collective-permute-start.2 = (bf16[192,2048]{1,0:T(8,128)(2,1)}, bf16[192,2048]{1,0:T(8,128)(2,1)S(1)}, u32[]{:S(2)}, u32[]{:S(2)}) collective-permute-start(bf16[192,2048]{1,0:T(8,128)(2,1)} %collective-permute-done.1.refs_0_), channel_id=1, source_target_pairs={{1,0},{0,1},{3,2},{2,3},{5,4},{4,5},{7,6},{6,7},{9,8},{8,9},{11,10... | collective-permute-start | bytes 2359304 | tf_op jit(solution)/shard_map/ppermute | solution.py:259
  106.2 19.8 %collective-permute-start.6 = (bf16[192,2048]{1,0:T(8,128)(2,1)}, bf16[192,2048]{1,0:T(8,128)(2,1)S(1)}, u32[]{:S(2)}, u32[]{:S(2)}) collective-permute-start(bf16[192,2048]{1,0:T(8,128)(2,1)} %collective-permute-done.1.refs_0_), channel_id=1, source_target_pairs={{2,0},{3,1},{4,2},{5,3},{6,4},{7,5},{0,6},{1,7},{14,8},{15,9},{8,1... | collective-permute-start | bytes 2359304 | tf_op jit(solution)/shard_map/ppermute | solution.py:259
  108.1 20.2 %collective-permute-start.8 = (bf16[192,2048]{1,0:T(8,128)(2,1)S(1)}, bf16[192,2048]{1,0:T(8,128)(2,1)}, u32[]{:S(2)}, u32[]{:S(2)}) collective-permute-start(bf16[192,2048]{1,0:T(8,128)(2,1)S(1)} %collective-permute-done.3.refs_1_), channel_id=1, source_target_pairs={{6,0},{7,1},{0,2},{1,3},{2,4},{3,5},{4,6},{5,7},{10,8},{11,9},{12,... | collective-permute-start | bytes 2359304 | tf_op jit(solution)/shard_map/ppermute | solution.py:259
  122.3 13.0 %collective-permute-start.5 = (bf16[144,2048]{1,0:T(8,128)(2,1)S(1)}, bf16[144,2048]{1,0:T(8,128)(2,1)S(1)}, u32[]{:S(2)}, u32[]{:S(2)}) collective-permute-start(bf16[144,2048]{1,0:T(8,128)(2,1)S(1)} %slice.10), channel_id=1, source_target_pairs={{2,0},{3,1},{4,2},{5,3},{6,4},{7,5},{0,6},{1,7},{14,8},{15,9},{8,1... | collective-permute-start | bytes 1769480 | tf_op jit(solution)/shard_map/ppermute | solution.py:259
  126.0 7.6 %collective-permute-start.7 = (bf16[48,2048]{1,0:T(8,128)(2,1)S(1)}, bf16[48,2048]{1,0:T(8,128)(2,1)S(1)}, u32[]{:S(2)}, u32[]{:S(2)}) collective-permute-start(bf16[48,2048]{1,0:T(8,128)(2,1)S(1)} %slice.12), channel_id=1, source_target_pairs={{1,0},{0,1},{3,2},{2,3},{5,4},{4,5},{7,6},{6,7},{9,8},{8,9},{11,10... | collective-permute-start | bytes 589832 | tf_op jit(solution)/shard_map/ppermute | solution.py:259

commit v6 on v5

--- a/solution.py
+++ b/solution.py
@@ -261,9 +261,9 @@
 
 def gather_and_correlate(own, position, row_count, scale):
     take = from_slice
-    near = (take(own, 1, 0), take(own, 0, 1), take(own, -1, 0))
-    right, other, left = near
-    summed = correlate(position, [own], row_count)
+    right, other = take(own, 1, 0), take(own, 0, 1)
+    own, summed = lax.optimization_barrier((own, correlate(position, [own], row_count)))
+    left = take(own, -1, 0)
     summed = correlate(position, [right, other, left], row_count, [summed])
     right_other, left_other, far = take(right, 0, 1), take(other, -1, 0), take(right, 1, 0)
     right_other, summed = lax.optimization_barrier((right_other, summed))

time: 138 us -> 138 us (level)
  waiting for transfers between devices: 22 us -> 25.3 us
  Pallas kernels: 18.7 us -> 16.2 us
    ppermute x8, waiting for transfers between devices: 19.4 us -> 22.7 us  [from_slice(): return lax.ppermute(value, ('band', 'tslice'), pairs)]
    pallas_call x4, Pallas kernels: 10.6 us -> 8.16 us  [correlate(): pl.pallas_call(functools.partial(correlate_kernel, scale, len(blocks), ti...]
  transfers between devices with their start and end apart: 9 -> 9, of which waited for: 5 -> 6; matrix products, arithmetic and copies ran while one was open for 0% -> 0% of each run, Pallas kernels for 8% -> 7%
where the time goes in v6:
time: 138 us; the launch traced here: 137 us
  blocking collectives  63.3 us (46%)
  starting transfers between devices  26.6 us (19%)
  waiting for transfers between devices  25.3 us (18%)
  Pallas kernels  16.2 us (12%)
  local copies, waits for them, and re-layouts  5.91 us (4%)
    all_to_all x1, blocking collectives, on_device(): lax.all_to_all(spectra, 'band', split_axis=0, concat_axis=0, tiled=True)  63.3 us
    ppermute x8, starting transfers between devices, from_slice(): return lax.ppermute(value, ('band', 'tslice'), pairs)  23.4 us
    ppermute x8, waiting for transfers between devices, from_slice(): return lax.ppermute(value, ('band', 'tslice'), pairs)  22.7 us
    pallas_call x4, Pallas kernels, correlate(): pl.pallas_call(functools.partial(correlate_kernel, scale, len(blocks), ti...  8.16 us
    pallas_call x2, Pallas kernels, picked_spectra(): pl.pallas_call(functools.partial(spectra_kernel, 16, span), in_specs=[pl....  5.95 us
    unnamed x10, local copies, waits for them, and re-layouts  4.83 us
    ppermute x1, starting transfers between devices, on_device(): lax.ppermute(tail, 'tslice', [(s, s + 1) for s in range(slices - 1)])  3.19 us
  transfers between devices with their start and end apart: 9, of which 6 were waited for; matrix products, arithmetic and copies ran while one was open for 0% of the time, Pallas kernels for 7%

profile of v6, /device:TPU:22, one launch (start us, length us, event | category | flops | bytes accessed | tf_op | source)
XLA Modules:
  0.0 137.5 jit_solution(100834955394107122)
XLA Ops:
  0.0 1.0 slice.9
  1.0 3.2 %collective-permute-start = (bf16[32,6144]{1,0:T(8,128)(2,1)S(1)}, bf16[32,6144]{1,0:T(8,128)(2,1)S(1)}, u32[]{:S(2)}, u32[]{:S(2)}) collective-permute-start(bf16[32,6144]{1,0:T(8,128)(2,1)S(1)} %slice.9), channel_id=1, source_target_pairs={{0,1},{1,2},{2,3},{3,4},{4,5},{5,6},{6,7},{8,9},{9,10},{10,11},{11... | collective-permute-start | bytes 1179656 | tf_op jit(solution)/shard_map/ppermute | solution.py:284
  4.2 0.0 copy-start
  4.2 2.2 %copy-done = bf16[2,1024,1024]{2,1,0:T(8,128)(2,1)S(1)} copy-done((bf16[2,1024,1024]{2,1,0:T(8,128)(2,1)S(1)}, bf16[2,1024,1024]{2,1,0:T(8,128)(2,1)}, u32[]{:S(2)}) %copy-start) | copy-done | bytes 4194328
  6.4 1.2 copy-done.1
  7.6 0.8 copy-done.2
  8.4 0.7 copy-done.3
  9.1 3.0 %shard_map.55.refs_1_ = bf16[64,24,128]{2,1,0:T(8,128)(2,1)S(1)} custom-call(s32[64]{0:T(128)S(1)} %copy-done.3, bf16[32,16384]{1,0:T(8,128)(2,1)S(1)} %copy-done.1, f32[4,2048]{1,0:T(4,128)S(1)} %copy-done.2, bf16[2,1024,1024]{2,1,0:T(8,128)(2,1)S(1)} %copy-done), custom_call_target="tpu_custom_call" | custom-call | flops 1073741824 | bytes 6291456 | tf_op jit(solution)/shard_map/pallas_call | solution.py:113
  12.0 0.0 copy-start.4
  12.0 2.6 %collective-permute-done.refs_0_ = bf16[32,6144]{1,0:T(8,128)(2,1)S(1)} collective-permute-done((bf16[32,6144]{1,0:T(8,128)(2,1)S(1)}, bf16[32,6144]{1,0:T(8,128)(2,1)S(1)}, u32[]{:S(2)}, u32[]{:S(2)}) %collective-permute-start) | collective-permute-done | bytes 393248 | tf_op jit(solution)/shard_map/ppermute | solution.py:284
  14.7 3.0 %shard_map.56 = bf16[64,24,256]{2,1,0:T(8,128)(2,1)S(1)} custom-call(s32[64]{0:T(128)S(1)} %copy-done.3, bf16[32,16384]{1,0:T(8,128)(2,1)S(1)} %copy-done.1, f32[4,2048]{1,0:T(4,128)S(1)} %copy-done.2, bf16[2,1024,1024]{2,1,0:T(8,128)(2,1)S(1)} %copy-done, bf16[32,6144]{1,0:T(8,128)(2,1)S(1)} %collective-permute-done.refs_0_, ...), custom_call_target="tpu_custom_call" | custom-call | flops 1073741824 | bytes 6291456 | tf_op jit(solution)/shard_map/pallas_call | solution.py:113
  17.7 63.3 %all_to_all.5.turned_ref = bf16[64,24,256]{2,1,0:T(8,128)(2,1)S(1)} all-to-all(bf16[64,24,256]{2,1,0:T(8,128)(2,1)S(1)} %shard_map.56), channel_id=1, replica_groups=mesh['band'=64,'tslice'=8] {'band'}, dimensions={0} | all-to-all | bytes 1572864 | tf_op jit(solution)/shard_map/all_to_all | solution.py:290
  80.9 2.1 %shard_map.57.refs_0_ = bf16[192,2048]{1,0:T(8,128)(2,1)S(1)} custom-call(bf16[64,24,256]{2,1,0:T(8,128)(2,1)S(1)} %all_to_all.5.turned_ref, s32[1,2048]{1,0:T(1,128)S(1)} %bitcast.2), custom_call_target="tpu_custom_call" | custom-call | flops 1610612736 | bytes 1572864 | tf_op jit(solution)/shard_map/pallas_call | solution.py:170
  83.0 2.7 %collective-permute-start.1 = (bf16[192,2048]{1,0:T(8,128)(2,1)S(1)}, bf16[192,2048]{1,0:T(8,128)(2,1)S(1)}, u32[]{:S(2)}, u32[]{:S(2)}) collective-permute-start(bf16[192,2048]{1,0:T(8,128)(2,1)S(1)} %shard_map.57.refs_0_), channel_id=1, source_target_pairs={{2,0},{3,1},{4,2},{5,3},{6,4},{7,5},{0,6},{1,7},{14,8},{15,9},{8,1... | collective-permute-start | bytes 2359304 | tf_op jit(solution)/shard_map/ppermute | solution.py:259
  85.8 2.3 %collective-permute-start.3 = (bf16[192,2048]{1,0:T(8,128)(2,1)S(1)}, bf16[192,2048]{1,0:T(8,128)(2,1)S(1)}, u32[]{:S(2)}, u32[]{:S(2)}) collective-permute-start(bf16[192,2048]{1,0:T(8,128)(2,1)S(1)} %shard_map.57.refs_0_), channel_id=1, source_target_pairs={{1,0},{0,1},{3,2},{2,3},{5,4},{4,5},{7,6},{6,7},{9,8},{8,9},{11,10... | collective-permute-start | bytes 2359304 | tf_op jit(solution)/shard_map/ppermute | solution.py:259
  88.0 1.2 shard_map.58.refs_3_
  89.2 4.3 %collective-permute-start.4 = (bf16[192,2048]{1,0:T(8,128)(2,1)S(1)}, bf16[192,2048]{1,0:T(8,128)(2,1)S(1)}, u32[]{:S(2)}, u32[]{:S(2)}) collective-permute-start(bf16[192,2048]{1,0:T(8,128)(2,1)S(1)} %shard_map.57.refs_0_), channel_id=1, source_target_pairs={{6,0},{7,1},{0,2},{1,3},{2,4},{3,5},{4,6},{5,7},{10,8},{11,9},{12,... | collective-permute-start | bytes 2359304 | tf_op jit(solution)/shard_map/ppermute | solution.py:259
  93.6 9.4 %collective-permute-done.1.refs_0_ = bf16[192,2048]{1,0:T(8,128)(2,1)S(1)} collective-permute-done((bf16[192,2048]{1,0:T(8,128)(2,1)S(1)}, bf16[192,2048]{1,0:T(8,128)(2,1)S(1)}, u32[]{:S(2)}, u32[]{:S(2)}) %collective-permute-start.1) | collective-permute-done | bytes 786464 | tf_op jit(solution)/shard_map/ppermute | solution.py:259
  103.0 1.9 %collective-permute-start.2 = (bf16[192,2048]{1,0:T(8,128)(2,1)S(1)}, bf16[192,2048]{1,0:T(8,128)(2,1)S(1)}, u32[]{:S(2)}, u32[]{:S(2)}) collective-permute-start(bf16[192,2048]{1,0:T(8,128)(2,1)S(1)} %collective-permute-done.1.refs_0_), channel_id=1, source_target_pairs={{1,0},{0,1},{3,2},{2,3},{5,4},{4,5},{7,6},{6,7},{9,8},{8,9},{11,10... | collective-permute-start | bytes 2359304 | tf_op jit(solution)/shard_map/ppermute | solution.py:259
  104.9 1.9 %collective-permute-start.6 = (bf16[192,2048]{1,0:T(8,128)(2,1)S(1)}, bf16[192,2048]{1,0:T(8,128)(2,1)S(1)}, u32[]{:S(2)}, u32[]{:S(2)}) collective-permute-start(bf16[192,2048]{1,0:T(8,128)(2,1)S(1)} %collective-permute-done.1.refs_0_), channel_id=1, source_target_pairs={{2,0},{3,1},{4,2},{5,3},{6,4},{7,5},{0,6},{1,7},{14,8},{15,9},{8,1... | collective-permute-start | bytes 2359304 | tf_op jit(solution)/shard_map/ppermute | solution.py:259
  106.8 1.3 collective-permute-done.3.refs_1_
  108.1 4.3 %collective-permute-start.8 = (bf16[192,2048]{1,0:T(8,128)(2,1)S(1)}, bf16[192,2048]{1,0:T(8,128)(2,1)S(1)}, u32[]{:S(2)}, u32[]{:S(2)}) collective-permute-start(bf16[192,2048]{1,0:T(8,128)(2,1)S(1)} %collective-permute-done.3.refs_1_), channel_id=1, source_target_pairs={{6,0},{7,1},{0,2},{1,3},{2,4},{3,5},{4,6},{5,7},{10,8},{11,9},{12,... | collective-permute-start | bytes 2359304 | tf_op jit(solution)/shard_map/ppermute | solution.py:259
  112.4 0.0 collective-permute-done.4.refs_2_
  112.5 2.4 %shard_map.59.refs_3_ = f32[512,2048]{1,0:T(8,128)S(1)} custom-call(s32[1]{0:T(128)} %bitcast.position_ref, bf16[192,2048]{1,0:T(8,128)(2,1)S(1)} %collective-permute-done.1.refs_0_, bf16[192,2048]{1,0:T(8,128)(2,1)S(1)} %collective-permute-done.3.refs_1_, bf16[192,2048]{1,0:T(8,128)(2,1)S(1)} %collective-permute-done.4.refs_2_, ...), custom_call_target="tpu_custom_call" | custom-call | flops 1207959552 | bytes 6553600 | tf_op jit(solution)/shard_map/pallas_call | solution.py:231
  114.9 7.4 %collective-permute-done.2.refs_0_ = bf16[192,2048]{1,0:T(8,128)(2,1)S(1)} collective-permute-done((bf16[192,2048]{1,0:T(8,128)(2,1)S(1)}, bf16[192,2048]{1,0:T(8,128)(2,1)S(1)}, u32[]{:S(2)}, u32[]{:S(2)}) %collective-permute-start.2) | collective-permute-done | bytes 786464 | tf_op jit(solution)/shard_map/ppermute | solution.py:259
  122.3 3.6 %collective-permute-start.5 = (bf16[144,2048]{1,0:T(8,128)(2,1)S(1)}, bf16[144,2048]{1,0:T(8,128)(2,1)S(1)}, u32[]{:S(2)}, u32[]{:S(2)}) collective-permute-start(bf16[144,2048]{1,0:T(8,128)(2,1)S(1)} %slice.10), channel_id=1, source_target_pairs={{2,0},{3,1},{4,2},{5,3},{6,4},{7,5},{0,6},{1,7},{14,8},{15,9},{8,1... | collective-permute-start | bytes 1769480 | tf_op jit(solution)/shard_map/ppermute | solution.py:259
  126.0 0.0 collective-permute-done.6.refs_2_
  126.0 2.3 %collective-permute-start.7 = (bf16[48,2048]{1,0:T(8,128)(2,1)S(1)}, bf16[48,2048]{1,0:T(8,128)(2,1)S(1)}, u32[]{:S(2)}, u32[]{:S(2)}) collective-permute-start(bf16[48,2048]{1,0:T(8,128)(2,1)S(1)} %slice.12), channel_id=1, source_target_pairs={{1,0},{0,1},{3,2},{2,3},{5,4},{4,5},{7,6},{6,7},{9,8},{8,9},{11,10... | collective-permute-start | bytes 589832 | tf_op jit(solution)/shard_map/ppermute | solution.py:259
  128.3 2.4 %shard_map.60.refs_2_ = f32[512,2048]{1,0:T(8,128)S(1)} custom-call(s32[1]{0:T(128)} %bitcast.position_ref, bf16[192,2048]{1,0:T(8,128)(2,1)S(1)} %collective-permute-done.2.refs_0_, bf16[192,2048]{1,0:T(8,128)(2,1)S(1)} %collective-permute-done.8.refs_1_, bf16[192,2048]{1,0:T(8,128)(2,1)S(1)} %collective-permute-done.6.refs_2_, ...), custom_call_target="tpu_custom_call" | custom-call | flops 1207959552 | bytes 6553600 | tf_op jit(solution)/shard_map/pallas_call | solution.py:231
  130.8 2.8 %collective-permute-done.7.refs_1_ = bf16[48,2048]{1,0:T(8,128)(2,1)S(1)} collective-permute-done((bf16[48,2048]{1,0:T(8,128)(2,1)S(1)}, bf16[48,2048]{1,0:T(8,128)(2,1)S(1)}, u32[]{:S(2)}, u32[]{:S(2)}) %collective-permute-start.7) | collective-permute-done | bytes 196640 | tf_op jit(solution)/shard_map/ppermute | solution.py:259
  133.6 1.7 %collective-permute-done.5.refs_0_ = bf16[144,2048]{1,0:T(8,128)(2,1)S(1)} collective-permute-done((bf16[144,2048]{1,0:T(8,128)(2,1)S(1)}, bf16[144,2048]{1,0:T(8,128)(2,1)S(1)}, u32[]{:S(2)}, u32[]{:S(2)}) %collective-permute-start.5) | collective-permute-done | bytes 589856 | tf_op jit(solution)/shard_map/ppermute | solution.py:259
  135.3 2.1 %shard_map.61 = bf16[1,2,256,2048]{3,2,1,0:T(8,128)(2,1)} custom-call(s32[1]{0:T(128)} %bitcast.position_ref, bf16[144,2048]{1,0:T(8,128)(2,1)S(1)} %collective-permute-done.5.refs_0_, bf16[48,2048]{1,0:T(8,128)(2,1)S(1)} %collective-permute-done.7.refs_1_, f32[512,2048]{1,0:T(8,128)S(1)} %shard_map.60.refs_2_), custom_call_target="tpu_custom_call" | custom-call | flops 402653184 | bytes 4980736 | tf_op jit(solution)/shard_map/pallas_call | solution.py:231
  (7 shorter events, 0.1 us)
Async XLA Ops:
  1.0 13.6 %collective-permute-start = (bf16[32,6144]{1,0:T(8,128)(2,1)S(1)}, bf16[32,6144]{1,0:T(8,128)(2,1)S(1)}, u32[]{:S(2)}, u32[]{:S(2)}) collective-permute-start(bf16[32,6144]{1,0:T(8,128)(2,1)S(1)} %slice.9), channel_id=1, source_target_pairs={{0,1},{1,2},{2,3},{3,4},{4,5},{5,6},{6,7},{8,9},{9,10},{10,11},{11... | collective-permute-start | bytes 1179656 | tf_op jit(solution)/shard_map/ppermute | solution.py:284
  4.2 2.2 %copy-start = (bf16[2,1024,1024]{2,1,0:T(8,128)(2,1)S(1)}, bf16[2,1024,1024]{2,1,0:T(8,128)(2,1)}, u32[]{:S(2)}) copy-start(bf16[2,1024,1024]{2,1,0:T(8,128)(2,1)} %constant.6.clone.basis_ref) | copy-start | bytes 12582916
  6.4 1.2 copy-start.1
  7.6 0.8 copy-start.2
  8.4 0.7 copy-start.3
  12.0 68.9 %copy-start.4 = (s32[2048]{0:T(1024)S(1)}, s32[2048]{0:T(1024)}, u32[]{:S(2)}) copy-start(s32[2048]{0:T(1024)} %param.7) | copy-start | bytes 24580
  83.0 20.0 %collective-permute-start.1 = (bf16[192,2048]{1,0:T(8,128)(2,1)S(1)}, bf16[192,2048]{1,0:T(8,128)(2,1)S(1)}, u32[]{:S(2)}, u32[]{:S(2)}) collective-permute-start(bf16[192,2048]{1,0:T(8,128)(2,1)S(1)} %shard_map.57.refs_0_), channel_id=1, source_target_pairs={{2,0},{3,1},{4,2},{5,3},{6,4},{7,5},{0,6},{1,7},{14,8},{15,9},{8,1... | collective-permute-start | bytes 2359304 | tf_op jit(solution)/shard_map/ppermute | solution.py:259
  85.8 22.4 %collective-permute-start.3 = (bf16[192,2048]{1,0:T(8,128)(2,1)S(1)}, bf16[192,2048]{1,0:T(8,128)(2,1)S(1)}, u32[]{:S(2)}, u32[]{:S(2)}) collective-permute-start(bf16[192,2048]{1,0:T(8,128)(2,1)S(1)} %shard_map.57.refs_0_), channel_id=1, source_target_pairs={{1,0},{0,1},{3,2},{2,3},{5,4},{4,5},{7,6},{6,7},{9,8},{8,9},{11,10... | collective-permute-start | bytes 2359304 | tf_op jit(solution)/shard_map/ppermute | solution.py:259
  89.2 23.2 %collective-permute-start.4 = (bf16[192,2048]{1,0:T(8,128)(2,1)S(1)}, bf16[192,2048]{1,0:T(8,128)(2,1)S(1)}, u32[]{:S(2)}, u32[]{:S(2)}) collective-permute-start(bf16[192,2048]{1,0:T(8,128)(2,1)S(1)} %shard_map.57.refs_0_), channel_id=1, source_target_pairs={{6,0},{7,1},{0,2},{1,3},{2,4},{3,5},{4,6},{5,7},{10,8},{11,9},{12,... | collective-permute-start | bytes 2359304 | tf_op jit(solution)/shard_map/ppermute | solution.py:259
  103.0 19.3 %collective-permute-start.2 = (bf16[192,2048]{1,0:T(8,128)(2,1)S(1)}, bf16[192,2048]{1,0:T(8,128)(2,1)S(1)}, u32[]{:S(2)}, u32[]{:S(2)}) collective-permute-start(bf16[192,2048]{1,0:T(8,128)(2,1)S(1)} %collective-permute-done.1.refs_0_), channel_id=1, source_target_pairs={{1,0},{0,1},{3,2},{2,3},{5,4},{4,5},{7,6},{6,7},{9,8},{8,9},{11,10... | collective-permute-start | bytes 2359304 | tf_op jit(solution)/shard_map/ppermute | solution.py:259
  104.9 21.1 %collective-permute-start.6 = (bf16[192,2048]{1,0:T(8,128)(2,1)S(1)}, bf16[192,2048]{1,0:T(8,128)(2,1)S(1)}, u32[]{:S(2)}, u32[]{:S(2)}) collective-permute-start(bf16[192,2048]{1,0:T(8,128)(2,1)S(1)} %collective-permute-done.1.refs_0_), channel_id=1, source_target_pairs={{2,0},{3,1},{4,2},{5,3},{6,4},{7,5},{0,6},{1,7},{14,8},{15,9},{8,1... | collective-permute-start | bytes 2359304 | tf_op jit(solution)/shard_map/ppermute | solution.py:259
  108.1 20.2 %collective-permute-start.8 = (bf16[192,2048]{1,0:T(8,128)(2,1)S(1)}, bf16[192,2048]{1,0:T(8,128)(2,1)S(1)}, u32[]{:S(2)}, u32[]{:S(2)}) collective-permute-start(bf16[192,2048]{1,0:T(8,128)(2,1)S(1)} %collective-permute-done.3.refs_1_), channel_id=1, source_target_pairs={{6,0},{7,1},{0,2},{1,3},{2,4},{3,5},{4,6},{5,7},{10,8},{11,9},{12,... | collective-permute-start | bytes 2359304 | tf_op jit(solution)/shard_map/ppermute | solution.py:259
  122.3 13.0 %collective-permute-start.5 = (bf16[144,2048]{1,0:T(8,128)(2,1)S(1)}, bf16[144,2048]{1,0:T(8,128)(2,1)S(1)}, u32[]{:S(2)}, u32[]{:S(2)}) collective-permute-start(bf16[144,2048]{1,0:T(8,128)(2,1)S(1)} %slice.10), channel_id=1, source_target_pairs={{2,0},{3,1},{4,2},{5,3},{6,4},{7,5},{0,6},{1,7},{14,8},{15,9},{8,1... | collective-permute-start | bytes 1769480 | tf_op jit(solution)/shard_map/ppermute | solution.py:259
  126.0 7.6 %collective-permute-start.7 = (bf16[48,2048]{1,0:T(8,128)(2,1)S(1)}, bf16[48,2048]{1,0:T(8,128)(2,1)S(1)}, u32[]{:S(2)}, u32[]{:S(2)}) collective-permute-start(bf16[48,2048]{1,0:T(8,128)(2,1)S(1)} %slice.12), channel_id=1, source_target_pairs={{1,0},{0,1},{3,2},{2,3},{5,4},{4,5},{7,6},{6,7},{9,8},{8,9},{11,10... | collective-permute-start | bytes 589832 | tf_op jit(solution)/shard_map/ppermute | solution.py:259

commit v7 on v6

--- a/solution.py
+++ b/solution.py
@@ -111,7 +111,7 @@
     beside = [] if later is None else [before, later]
     whole = pl.BlockSpec(memory_space=pltpu.VMEM)
     return pl.pallas_call(
-        functools.partial(spectra_kernel, 16, span),
+        functools.partial(spectra_kernel, 32, span),
         in_specs=[pl.BlockSpec(memory_space=pltpu.SMEM)] + [whole] * (3 + len(beside)),
         out_specs=whole,
         scratch_shapes=[pltpu.VMEM((2, length // 2, 2 * columns), jnp.bfloat16)],

time: 138 us -> 138 us (level)
  the two profiles are of different devices: /device:TPU:22 before, /device:TPU:16 now
where the time goes in v7:
time: 138 us; the launch traced here: 137 us
  blocking collectives  63.2 us (46%)
  starting transfers between devices  29.6 us (21%)
  waiting for transfers between devices  22.8 us (17%)
  Pallas kernels  15.3 us (11%)
  local copies, waits for them, and re-layouts  5.91 us (4%)
    all_to_all x1, blocking collectives, on_device(): lax.all_to_all(spectra, 'band', split_axis=0, concat_axis=0, tiled=True)  63.2 us
    ppermute x8, starting transfers between devices, from_slice(): return lax.ppermute(value, ('band', 'tslice'), pairs)  26.4 us
    ppermute x8, waiting for transfers between devices, from_slice(): return lax.ppermute(value, ('band', 'tslice'), pairs)  21.8 us
    pallas_call x4, Pallas kernels, correlate(): pl.pallas_call(functools.partial(correlate_kernel, scale, len(blocks), ti...  8.16 us
    pallas_call x2, Pallas kernels, picked_spectra(): pl.pallas_call(functools.partial(spectra_kernel, 32, span), in_specs=[pl....  5.05 us
    unnamed x10, local copies, waits for them, and re-layouts  4.83 us
    ppermute x1, starting transfers between devices, on_device(): lax.ppermute(tail, 'tslice', [(s, s + 1) for s in range(slices - 1)])  3.21 us
  transfers between devices with their start and end apart: 9, of which 6 were waited for; matrix products, arithmetic and copies ran while one was open for 0% of the time, Pallas kernels for 6%

profile of v7, /device:TPU:16, one launch (start us, length us, event | category | flops | bytes accessed | tf_op | source)
XLA Modules:
  0.0 137.0 jit_solution(7121877324466461944)
XLA Ops:
  0.0 1.0 slice.9
  1.0 3.2 %collective-permute-start = (bf16[32,6144]{1,0:T(8,128)(2,1)S(1)}, bf16[32,6144]{1,0:T(8,128)(2,1)S(1)}, u32[]{:S(2)}, u32[]{:S(2)}) collective-permute-start(bf16[32,6144]{1,0:T(8,128)(2,1)S(1)} %slice.9), channel_id=1, source_target_pairs={{0,1},{1,2},{2,3},{3,4},{4,5},{5,6},{6,7},{8,9},{9,10},{10,11},{11... | collective-permute-start | bytes 1179656 | tf_op jit(solution)/shard_map/ppermute | solution.py:284
  4.2 0.0 copy-start
  4.3 2.2 %copy-done = bf16[2,1024,1024]{2,1,0:T(8,128)(2,1)S(1)} copy-done((bf16[2,1024,1024]{2,1,0:T(8,128)(2,1)S(1)}, bf16[2,1024,1024]{2,1,0:T(8,128)(2,1)}, u32[]{:S(2)}) %copy-start) | copy-done | bytes 4194328
  6.4 1.2 copy-done.1
  7.7 0.8 copy-done.2
  8.4 0.7 copy-done.3
  9.1 2.5 %shard_map.55.refs_1_ = bf16[64,24,128]{2,1,0:T(8,128)(2,1)S(1)} custom-call(s32[64]{0:T(128)S(1)} %copy-done.3, bf16[32,16384]{1,0:T(8,128)(2,1)S(1)} %copy-done.1, f32[4,2048]{1,0:T(4,128)S(1)} %copy-done.2, bf16[2,1024,1024]{2,1,0:T(8,128)(2,1)S(1)} %copy-done), custom_call_target="tpu_custom_call" | custom-call | flops 1073741824 | bytes 6291456 | tf_op jit(solution)/shard_map/pallas_call | solution.py:113
  11.6 0.0 copy-start.4
  11.6 1.0 collective-permute-done.refs_0_
  12.6 2.5 %shard_map.56 = bf16[64,24,256]{2,1,0:T(8,128)(2,1)S(1)} custom-call(s32[64]{0:T(128)S(1)} %copy-done.3, bf16[32,16384]{1,0:T(8,128)(2,1)S(1)} %copy-done.1, f32[4,2048]{1,0:T(4,128)S(1)} %copy-done.2, bf16[2,1024,1024]{2,1,0:T(8,128)(2,1)S(1)} %copy-done, bf16[32,6144]{1,0:T(8,128)(2,1)S(1)} %collective-permute-done.refs_0_, ...), custom_call_target="tpu_custom_call" | custom-call | flops 1073741824 | bytes 6291456 | tf_op jit(solution)/shard_map/pallas_call | solution.py:113
  15.1 63.2 %all_to_all.5.turned_ref = bf16[64,24,256]{2,1,0:T(8,128)(2,1)S(1)} all-to-all(bf16[64,24,256]{2,1,0:T(8,128)(2,1)S(1)} %shard_map.56), channel_id=1, replica_groups=mesh['band'=64,'tslice'=8] {'band'}, dimensions={0} | all-to-all | bytes 1572864 | tf_op jit(solution)/shard_map/all_to_all | solution.py:290
  78.4 2.1 %shard_map.57.refs_0_ = bf16[192,2048]{1,0:T(8,128)(2,1)S(1)} custom-call(bf16[64,24,256]{2,1,0:T(8,128)(2,1)S(1)} %all_to_all.5.turned_ref, s32[1,2048]{1,0:T(1,128)S(1)} %bitcast.2), custom_call_target="tpu_custom_call" | custom-call | flops 1610612736 | bytes 1572864 | tf_op jit(solution)/shard_map/pallas_call | solution.py:170
  80.4 6.8 %collective-permute-start.1 = (bf16[192,2048]{1,0:T(8,128)(2,1)S(1)}, bf16[192,2048]{1,0:T(8,128)(2,1)S(1)}, u32[]{:S(2)}, u32[]{:S(2)}) collective-permute-start(bf16[192,2048]{1,0:T(8,128)(2,1)S(1)} %shard_map.57.refs_0_), channel_id=1, source_target_pairs={{2,0},{3,1},{4,2},{5,3},{6,4},{7,5},{0,6},{1,7},{14,8},{15,9},{8,1... | collective-permute-start | bytes 2359304 | tf_op jit(solution)/shard_map/ppermute | solution.py:259
  87.2 2.3 %collective-permute-start.3 = (bf16[192,2048]{1,0:T(8,128)(2,1)S(1)}, bf16[192,2048]{1,0:T(8,128)(2,1)S(1)}, u32[]{:S(2)}, u32[]{:S(2)}) collective-permute-start(bf16[192,2048]{1,0:T(8,128)(2,1)S(1)} %shard_map.57.refs_0_), channel_id=1, source_target_pairs={{1,0},{0,1},{3,2},{2,3},{5,4},{4,5},{7,6},{6,7},{9,8},{8,9},{11,10... | collective-permute-start | bytes 2359304 | tf_op jit(solution)/shard_map/ppermute | solution.py:259
  89.5 1.2 shard_map.58.refs_3_
  90.7 1.9 %collective-permute-start.4 = (bf16[192,2048]{1,0:T(8,128)(2,1)S(1)}, bf16[192,2048]{1,0:T(8,128)(2,1)S(1)}, u32[]{:S(2)}, u32[]{:S(2)}) collective-permute-start(bf16[192,2048]{1,0:T(8,128)(2,1)S(1)} %shard_map.57.refs_0_), channel_id=1, source_target_pairs={{6,0},{7,1},{0,2},{1,3},{2,4},{3,5},{4,6},{5,7},{10,8},{11,9},{12,... | collective-permute-start | bytes 2359304 | tf_op jit(solution)/shard_map/ppermute | solution.py:259
  92.6 8.9 %collective-permute-done.1.refs_0_ = bf16[192,2048]{1,0:T(8,128)(2,1)S(1)} collective-permute-done((bf16[192,2048]{1,0:T(8,128)(2,1)S(1)}, bf16[192,2048]{1,0:T(8,128)(2,1)S(1)}, u32[]{:S(2)}, u32[]{:S(2)}) %collective-permute-start.1) | collective-permute-done | bytes 786464 | tf_op jit(solution)/shard_map/ppermute | solution.py:259
  101.5 1.9 %collective-permute-start.2 = (bf16[192,2048]{1,0:T(8,128)(2,1)S(1)}, bf16[192,2048]{1,0:T(8,128)(2,1)S(1)}, u32[]{:S(2)}, u32[]{:S(2)}) collective-permute-start(bf16[192,2048]{1,0:T(8,128)(2,1)S(1)} %collective-permute-done.1.refs_0_), channel_id=1, source_target_pairs={{1,0},{0,1},{3,2},{2,3},{5,4},{4,5},{7,6},{6,7},{9,8},{8,9},{11,10... | collective-permute-start | bytes 2359304 | tf_op jit(solution)/shard_map/ppermute | solution.py:259
  103.5 5.6 %collective-permute-start.6 = (bf16[192,2048]{1,0:T(8,128)(2,1)S(1)}, bf16[192,2048]{1,0:T(8,128)(2,1)S(1)}, u32[]{:S(2)}, u32[]{:S(2)}) collective-permute-start(bf16[192,2048]{1,0:T(8,128)(2,1)S(1)} %collective-permute-done.1.refs_0_), channel_id=1, source_target_pairs={{2,0},{3,1},{4,2},{5,3},{6,4},{7,5},{0,6},{1,7},{14,8},{15,9},{8,1... | collective-permute-start | bytes 2359304 | tf_op jit(solution)/shard_map/ppermute | solution.py:259
  109.1 0.5 collective-permute-done.3.refs_1_
  109.6 1.9 %collective-permute-start.8 = (bf16[192,2048]{1,0:T(8,128)(2,1)S(1)}, bf16[192,2048]{1,0:T(8,128)(2,1)S(1)}, u32[]{:S(2)}, u32[]{:S(2)}) collective-permute-start(bf16[192,2048]{1,0:T(8,128)(2,1)S(1)} %collective-permute-done.3.refs_1_), channel_id=1, source_target_pairs={{6,0},{7,1},{0,2},{1,3},{2,4},{3,5},{4,6},{5,7},{10,8},{11,9},{12,... | collective-permute-start | bytes 2359304 | tf_op jit(solution)/shard_map/ppermute | solution.py:259
  111.5 0.0 collective-permute-done.4.refs_2_
  111.5 2.4 %shard_map.59.refs_3_ = f32[512,2048]{1,0:T(8,128)S(1)} custom-call(s32[1]{0:T(128)} %bitcast.position_ref, bf16[192,2048]{1,0:T(8,128)(2,1)S(1)} %collective-permute-done.1.refs_0_, bf16[192,2048]{1,0:T(8,128)(2,1)S(1)} %collective-permute-done.3.refs_1_, bf16[192,2048]{1,0:T(8,128)(2,1)S(1)} %collective-permute-done.4.refs_2_, ...), custom_call_target="tpu_custom_call" | custom-call | flops 1207959552 | bytes 6553600 | tf_op jit(solution)/shard_map/pallas_call | solution.py:231
  113.9 9.1 %collective-permute-done.2.refs_0_ = bf16[192,2048]{1,0:T(8,128)(2,1)S(1)} collective-permute-done((bf16[192,2048]{1,0:T(8,128)(2,1)S(1)}, bf16[192,2048]{1,0:T(8,128)(2,1)S(1)}, u32[]{:S(2)}, u32[]{:S(2)}) %collective-permute-start.2) | collective-permute-done | bytes 786464 | tf_op jit(solution)/shard_map/ppermute | solution.py:259
  123.1 3.5 %collective-permute-start.5 = (bf16[144,2048]{1,0:T(8,128)(2,1)S(1)}, bf16[144,2048]{1,0:T(8,128)(2,1)S(1)}, u32[]{:S(2)}, u32[]{:S(2)}) collective-permute-start(bf16[144,2048]{1,0:T(8,128)(2,1)S(1)} %slice.10), channel_id=1, source_target_pairs={{2,0},{3,1},{4,2},{5,3},{6,4},{7,5},{0,6},{1,7},{14,8},{15,9},{8,1... | collective-permute-start | bytes 1769480 | tf_op jit(solution)/shard_map/ppermute | solution.py:259
  126.6 2.5 %collective-permute-start.7 = (bf16[48,2048]{1,0:T(8,128)(2,1)S(1)}, bf16[48,2048]{1,0:T(8,128)(2,1)S(1)}, u32[]{:S(2)}, u32[]{:S(2)}) collective-permute-start(bf16[48,2048]{1,0:T(8,128)(2,1)S(1)} %slice.12), channel_id=1, source_target_pairs={{1,0},{0,1},{3,2},{2,3},{5,4},{4,5},{7,6},{6,7},{9,8},{8,9},{11,10... | collective-permute-start | bytes 589832 | tf_op jit(solution)/shard_map/ppermute | solution.py:259
  129.1 0.0 collective-permute-done.8.refs_1_
  129.1 2.4 %shard_map.60.refs_2_ = f32[512,2048]{1,0:T(8,128)S(1)} custom-call(s32[1]{0:T(128)} %bitcast.position_ref, bf16[192,2048]{1,0:T(8,128)(2,1)S(1)} %collective-permute-done.2.refs_0_, bf16[192,2048]{1,0:T(8,128)(2,1)S(1)} %collective-permute-done.8.refs_1_, bf16[192,2048]{1,0:T(8,128)(2,1)S(1)} %collective-permute-done.6.refs_2_, ...), custom_call_target="tpu_custom_call" | custom-call | flops 1207959552 | bytes 6553600 | tf_op jit(solution)/shard_map/pallas_call | solution.py:231
  131.5 3.0 %collective-permute-done.7.refs_1_ = bf16[48,2048]{1,0:T(8,128)(2,1)S(1)} collective-permute-done((bf16[48,2048]{1,0:T(8,128)(2,1)S(1)}, bf16[48,2048]{1,0:T(8,128)(2,1)S(1)}, u32[]{:S(2)}, u32[]{:S(2)}) %collective-permute-start.7) | collective-permute-done | bytes 196640 | tf_op jit(solution)/shard_map/ppermute | solution.py:259
  134.5 0.4 collective-permute-done.5.refs_0_
  134.9 2.1 %shard_map.61 = bf16[1,2,256,2048]{3,2,1,0:T(8,128)(2,1)} custom-call(s32[1]{0:T(128)} %bitcast.position_ref, bf16[144,2048]{1,0:T(8,128)(2,1)S(1)} %collective-permute-done.5.refs_0_, bf16[48,2048]{1,0:T(8,128)(2,1)S(1)} %collective-permute-done.7.refs_1_, f32[512,2048]{1,0:T(8,128)S(1)} %shard_map.60.refs_2_), custom_call_target="tpu_custom_call" | custom-call | flops 402653184 | bytes 4980736 | tf_op jit(solution)/shard_map/pallas_call | solution.py:231
  (7 shorter events, 0.1 us)
Async XLA Ops:
  1.0 11.6 %collective-permute-start = (bf16[32,6144]{1,0:T(8,128)(2,1)S(1)}, bf16[32,6144]{1,0:T(8,128)(2,1)S(1)}, u32[]{:S(2)}, u32[]{:S(2)}) collective-permute-start(bf16[32,6144]{1,0:T(8,128)(2,1)S(1)} %slice.9), channel_id=1, source_target_pairs={{0,1},{1,2},{2,3},{3,4},{4,5},{5,6},{6,7},{8,9},{9,10},{10,11},{11... | collective-permute-start | bytes 1179656 | tf_op jit(solution)/shard_map/ppermute | solution.py:284
  4.2 2.2 %copy-start = (bf16[2,1024,1024]{2,1,0:T(8,128)(2,1)S(1)}, bf16[2,1024,1024]{2,1,0:T(8,128)(2,1)}, u32[]{:S(2)}) copy-start(bf16[2,1024,1024]{2,1,0:T(8,128)(2,1)} %constant.6.clone.basis_ref) | copy-start | bytes 12582916
  6.4 1.2 copy-start.1
  7.7 0.8 copy-start.2
  8.4 0.7 copy-start.3
  11.6 66.8 %copy-start.4 = (s32[2048]{0:T(1024)S(1)}, s32[2048]{0:T(1024)}, u32[]{:S(2)}) copy-start(s32[2048]{0:T(1024)} %param.7) | copy-start | bytes 24580
  80.4 21.1 %collective-permute-start.1 = (bf16[192,2048]{1,0:T(8,128)(2,1)S(1)}, bf16[192,2048]{1,0:T(8,128)(2,1)S(1)}, u32[]{:S(2)}, u32[]{:S(2)}) collective-permute-start(bf16[192,2048]{1,0:T(8,128)(2,1)S(1)} %shard_map.57.refs_0_), channel_id=1, source_target_pairs={{2,0},{3,1},{4,2},{5,3},{6,4},{7,5},{0,6},{1,7},{14,8},{15,9},{8,1... | collective-permute-start | bytes 2359304 | tf_op jit(solution)/shard_map/ppermute | solution.py:259
  87.2 22.4 %collective-permute-start.3 = (bf16[192,2048]{1,0:T(8,128)(2,1)S(1)}, bf16[192,2048]{1,0:T(8,128)(2,1)S(1)}, u32[]{:S(2)}, u32[]{:S(2)}) collective-permute-start(bf16[192,2048]{1,0:T(8,128)(2,1)S(1)} %shard_map.57.refs_0_), channel_id=1, source_target_pairs={{1,0},{0,1},{3,2},{2,3},{5,4},{4,5},{7,6},{6,7},{9,8},{8,9},{11,10... | collective-permute-start | bytes 2359304 | tf_op jit(solution)/shard_map/ppermute | solution.py:259
  90.7 20.8 %collective-permute-start.4 = (bf16[192,2048]{1,0:T(8,128)(2,1)S(1)}, bf16[192,2048]{1,0:T(8,128)(2,1)S(1)}, u32[]{:S(2)}, u32[]{:S(2)}) collective-permute-start(bf16[192,2048]{1,0:T(8,128)(2,1)S(1)} %shard_map.57.refs_0_), channel_id=1, source_target_pairs={{6,0},{7,1},{0,2},{1,3},{2,4},{3,5},{4,6},{5,7},{10,8},{11,9},{12,... | collective-permute-start | bytes 2359304 | tf_op jit(solution)/shard_map/ppermute | solution.py:259
  101.5 21.5 %collective-permute-start.2 = (bf16[192,2048]{1,0:T(8,128)(2,1)S(1)}, bf16[192,2048]{1,0:T(8,128)(2,1)S(1)}, u32[]{:S(2)}, u32[]{:S(2)}) collective-permute-start(bf16[192,2048]{1,0:T(8,128)(2,1)S(1)} %collective-permute-done.1.refs_0_), channel_id=1, source_target_pairs={{1,0},{0,1},{3,2},{2,3},{5,4},{4,5},{7,6},{6,7},{9,8},{8,9},{11,10... | collective-permute-start | bytes 2359304 | tf_op jit(solution)/shard_map/ppermute | solution.py:259
  103.5 23.1 %collective-permute-start.6 = (bf16[192,2048]{1,0:T(8,128)(2,1)S(1)}, bf16[192,2048]{1,0:T(8,128)(2,1)S(1)}, u32[]{:S(2)}, u32[]{:S(2)}) collective-permute-start(bf16[192,2048]{1,0:T(8,128)(2,1)S(1)} %collective-permute-done.1.refs_0_), channel_id=1, source_target_pairs={{2,0},{3,1},{4,2},{5,3},{6,4},{7,5},{0,6},{1,7},{14,8},{15,9},{8,1... | collective-permute-start | bytes 2359304 | tf_op jit(solution)/shard_map/ppermute | solution.py:259
  109.6 19.5 %collective-permute-start.8 = (bf16[192,2048]{1,0:T(8,128)(2,1)S(1)}, bf16[192,2048]{1,0:T(8,128)(2,1)S(1)}, u32[]{:S(2)}, u32[]{:S(2)}) collective-permute-start(bf16[192,2048]{1,0:T(8,128)(2,1)S(1)} %collective-permute-done.3.refs_1_), channel_id=1, source_target_pairs={{6,0},{7,1},{0,2},{1,3},{2,4},{3,5},{4,6},{5,7},{10,8},{11,9},{12,... | collective-permute-start | bytes 2359304 | tf_op jit(solution)/shard_map/ppermute | solution.py:259
  123.1 11.8 %collective-permute-start.5 = (bf16[144,2048]{1,0:T(8,128)(2,1)S(1)}, bf16[144,2048]{1,0:T(8,128)(2,1)S(1)}, u32[]{:S(2)}, u32[]{:S(2)}) collective-permute-start(bf16[144,2048]{1,0:T(8,128)(2,1)S(1)} %slice.10), channel_id=1, source_target_pairs={{2,0},{3,1},{4,2},{5,3},{6,4},{7,5},{0,6},{1,7},{14,8},{15,9},{8,1... | collective-permute-start | bytes 1769480 | tf_op jit(solution)/shard_map/ppermute | solution.py:259
  126.6 7.9 %collective-permute-start.7 = (bf16[48,2048]{1,0:T(8,128)(2,1)S(1)}, bf16[48,2048]{1,0:T(8,128)(2,1)S(1)}, u32[]{:S(2)}, u32[]{:S(2)}) collective-permute-start(bf16[48,2048]{1,0:T(8,128)(2,1)S(1)} %slice.12), channel_id=1, source_target_pairs={{1,0},{0,1},{3,2},{2,3},{5,4},{4,5},{7,6},{6,7},{9,8},{8,9},{11,10... | collective-permute-start | bytes 589832 | tf_op jit(solution)/shard_map/ppermute | solution.py:259
